TPU v7x, 128 devices: a whole 4x4x4 slice. The times are simulated.
128 devices in a mesh: row: 8 (over y, x_hi), col: 16 (over x_lo, z, core).
Axes of the slice: x: 4 (x_hi: 2, x_lo: 2; x = x_hi * 2 + x_lo), y: 4, z: 4, core: 2. Of those that a mesh axis runs over, the one named last changes fastest.
Arguments:
- start_block: float32 [32, 49152], P(None, ('row', 'col')), may hold values from -6 to 6
- center: float32 [1], replicated, may hold values from 1.05 to 1.15
- half_width: float32 [1], replicated, may hold values from 0.85 to 0.95
- matrix_tiles: bfloat16 [8, 768, 192, 192], P('row', 'col')
- tile_row: int32 [8, 768], P('row', 'col'), may hold values from 0 to 31, as said below
- tile_col: int32 [8, 768], P('row', 'col'), may hold values from 0 to 15, as said below
- tile_live: int32 [8, 768], P('row', 'col'), may hold values from 0 to 1
Outputs:
- filtered: float32 [32, 49152], P(None, ('row', 'col'))
- previous: float32 [32, 49152], P(None, ('row', 'col'))
Inputs may be any that keep to these rules, and one draw needn't show every extreme that they name: tile_row lies within the device's row clusters; on a live slot the block row's atom order is at most the block column's. tile_col lies within the device's column clusters.
All inputs are finite; a program needn't handle non-finite values.
Results may differ from a plain program's by a relative error of at most 0.03.
Values may be sent and summed in bfloat16 or wider, within the bound.
No kernel may reach another device: no remote copies, remote signals or barrier semaphores. Data moves between devices by JAX's collectives and lax.ppermute only.
A program may use at most 64 MiB of HBM per device.

v0:
```python
import jax
import jax.numpy as jnp
from jax import lax
from jax.sharding import PartitionSpec as P

DEG = 8


def spread(block, axis, source):
    block = jnp.where(lax.axis_index(axis) == source, block, jnp.zeros_like(block))
    return lax.psum(block, axis)


def advance(degree, product, current, earlier, center_value, half_value):
    if degree == 0:
        return (product - center_value * current) / half_value
    return 2.0 * (product - center_value * current) / half_value - earlier


def body(start_block, center, half_width, matrix_tiles, tile_row, tile_col, tile_live):
    tile_size = matrix_tiles.shape[-1]
    vector_count = start_block.shape[0]
    own_clusters = start_block.shape[1] // tile_size
    row_count = lax.axis_size("row")
    col_count = lax.axis_size("col")
    panel_rows = own_clusters * col_count
    panel_cols = own_clusters * row_count
    row_index = lax.axis_index("row")
    col_index = lax.axis_index("col")
    root_row = col_index * row_count // col_count
    offset = col_index * row_count % col_count * own_clusters
    owner_flag = (row_index == root_row).astype(jnp.float32)
    center_value = center[0]
    half_value = half_width[0]
    stored = matrix_tiles[0]
    row_ids = tile_row[0]
    col_ids = tile_col[0]
    weights = tile_live[0].astype(jnp.float32)
    row_onehot = (row_ids[:, None] == jnp.arange(panel_rows, dtype=jnp.int32)[None, :]).astype(
        jnp.float32
    ) * weights[:, None]
    col_onehot = (col_ids[:, None] == jnp.arange(panel_cols, dtype=jnp.int32)[None, :]).astype(
        jnp.float32
    ) * weights[:, None]
    highest = lax.Precision.HIGHEST
    own_vectors = start_block.reshape(vector_count, own_clusters, tile_size)
    current = own_vectors
    earlier = current
    for degree in range(DEG):
        row_panel = lax.all_gather(current.astype(jnp.bfloat16), "col", axis=1, tiled=True)
        col_source = lax.dynamic_slice_in_dim(row_panel, offset, panel_cols, 1)
        col_panel = spread(col_source, "row", root_row)
        x_col = jnp.take(col_panel, col_ids, axis=1)
        direct = jnp.einsum("ksb,sab->ksa", x_col, stored, preferred_element_type=jnp.float32)
        row_part = jnp.einsum("ksa,sr->kra", direct, row_onehot, precision=highest)
        x_row = jnp.take(row_panel, row_ids, axis=1)
        mirrored = jnp.einsum("ksa,sab->ksb", x_row, stored, preferred_element_type=jnp.float32)
        mirror_part = jnp.einsum("ksb,sc->kcb", mirrored, col_onehot, precision=highest)
        mirror_total = lax.psum(mirror_part, "row")
        placed = lax.dynamic_update_slice_in_dim(
            jnp.zeros_like(row_part), mirror_total * owner_flag, offset, 1
        )
        partial_sum = row_part + placed
        product = lax.psum_scatter(partial_sum, "col", scatter_dimension=1, tiled=True)
        following = advance(degree, product, current, earlier, center_value, half_value)
        earlier, current = (current, following)
    flat_shape = (vector_count, own_clusters * tile_size)
    return (current.reshape(flat_shape), earlier.reshape(flat_shape))


def solution(mesh):
    in_specs = (
        P(None, ("row", "col")),
        P(),
        P(),
        P("row", "col", None, None),
        P("row", "col"),
        P("row", "col"),
        P("row", "col"),
    )
    out_specs = (P(None, ("row", "col")), P(None, ("row", "col")))
    return jax.shard_map(body, mesh=mesh, in_specs=in_specs, out_specs=out_specs, check_vma=False)
```

profile of v0, /device:TPU:7, one launch (start us, length us, event | category | flops | bytes accessed | tf_op | source)
XLA Modules:
  0.0 2046.7 jit_solution(2276359844783974786)
XLA Ops:
  8.2 22.2 %all_gather.24 = bf16[32,32,192]{2,0,1:T(8,128)(2,1)S(1)} all-gather(bf16[32,2,192]{2,0,1:T(8,128)(2,1)S(1)} %copy.89), channel_id=1, replica_groups=mesh['row'=8,'col'=16] {'col'}, dimensions={1}, use_global_device_ids=true | all-gather | bytes 417792 | tf_op jit(solution)/shard_map/all_gather | solution.py:50
  31.9 3.4 fusion.67
  35.3 2.5 fusion.112
  37.9 69.2 %all-reduce.17.cloned.1.call-done = bf16[32,16,192]{2,0,1:T(8,128)(2,1)} async-done(((bf16[32,16,192]{2,0,1:T(8,128)(2,1)}), bf16[32,16,192]{2,0,1:T(8,128)(2,1)}) %all-reduce.17.cloned.1.call-update) | async-done | bytes 196624 | tf_op jit(solution)/shard_map/psum | solution.py:11
  108.7 3.9 fusion.64
  112.5 1.9 fusion.62
  114.5 78.8 %all-reduce.19.cloned.1.call-done = f32[32,16,192]{2,1,0:T(8,128)} async-done(((f32[32,16,192]{2,1,0:T(8,128)}), f32[32,16,192]{2,1,0:T(8,128)}) %all-reduce.19.cloned.1.call-update) | async-done | bytes 393232 | tf_op jit(solution)/shard_map/psum | solution.py:59
  198.6 62.1 %reduce-scatter.9.cloned.1.call-done = f32[32,2,192]{2,0,1:T(8,128)} async-done(((f32[32,32,192]{2,0,1:T(8,128)}), f32[32,2,192]{2,0,1:T(8,128)}) %reduce-scatter.9.cloned.1.call-update) | async-done | bytes 49168 | tf_op jit(solution)/shard_map/reduce_scatter | solution.py:64
  261.5 21.2 %all_gather.25 = bf16[32,32,192]{2,0,1:T(8,128)(2,1)S(1)} all-gather(bf16[32,2,192]{2,0,1:T(8,128)(2,1)S(1)} %fusion.312), channel_id=1, replica_groups=mesh['row'=8,'col'=16] {'col'}, dimensions={1}, use_global_device_ids=true | all-gather | bytes 417792 | tf_op jit(solution)/shard_map/all_gather | solution.py:50
  284.1 3.3 fusion.73
  287.5 2.5 fusion.115
  290.6 70.5 %all-reduce.21.cloned.1.call-done = bf16[32,16,192]{2,0,1:T(8,128)(2,1)} async-done(((bf16[32,16,192]{2,0,1:T(8,128)(2,1)}), bf16[32,16,192]{2,0,1:T(8,128)(2,1)}) %all-reduce.21.cloned.1.call-update) | async-done | bytes 196624 | tf_op jit(solution)/shard_map/psum | solution.py:11
  362.7 3.9 fusion.70
  366.6 1.9 fusion.58
  368.5 78.5 %all-reduce.23.cloned.1.call-done = f32[32,16,192]{2,1,0:T(8,128)} async-done(((f32[32,16,192]{2,1,0:T(8,128)}), f32[32,16,192]{2,1,0:T(8,128)}) %all-reduce.23.cloned.1.call-update) | async-done | bytes 393232 | tf_op jit(solution)/shard_map/psum | solution.py:59
  451.0 63.4 %reduce-scatter.11.cloned.1.call-done = f32[32,2,192]{2,0,1:T(8,128)} async-done(((f32[32,32,192]{2,0,1:T(8,128)}), f32[32,2,192]{2,0,1:T(8,128)}) %reduce-scatter.11.cloned.1.call-update) | async-done | bytes 49168 | tf_op jit(solution)/shard_map/reduce_scatter | solution.py:64
  515.3 21.2 %all_gather.26 = bf16[32,32,192]{2,0,1:T(8,128)(2,1)S(1)} all-gather(bf16[32,2,192]{2,0,1:T(8,128)(2,1)S(1)} %get-tuple-element.14), channel_id=1, replica_groups=mesh['row'=8,'col'=16] {'col'}, dimensions={1}, use_global_device_ids=true | all-gather | bytes 417792 | tf_op jit(solution)/shard_map/all_gather | solution.py:50
  537.9 3.3 fusion.79
  541.2 2.5 fusion.118
  543.8 71.1 %all-reduce.25.cloned.1.call-done = bf16[32,16,192]{2,0,1:T(8,128)(2,1)} async-done(((bf16[32,16,192]{2,0,1:T(8,128)(2,1)}), bf16[32,16,192]{2,0,1:T(8,128)(2,1)}) %all-reduce.25.cloned.1.call-update) | async-done | bytes 196624 | tf_op jit(solution)/shard_map/psum | solution.py:11
  616.4 3.9 fusion.76
  620.3 1.9 fusion.54
  622.3 78.8 %all-reduce.27.cloned.1.call-done = f32[32,16,192]{2,1,0:T(8,128)} async-done(((f32[32,16,192]{2,1,0:T(8,128)}), f32[32,16,192]{2,1,0:T(8,128)}) %all-reduce.27.cloned.1.call-update) | async-done | bytes 393232 | tf_op jit(solution)/shard_map/psum | solution.py:59
  705.1 63.4 %reduce-scatter.13.cloned.1.call-done = f32[32,2,192]{2,0,1:T(8,128)} async-done(((f32[32,32,192]{2,0,1:T(8,128)}), f32[32,2,192]{2,0,1:T(8,128)}) %reduce-scatter.13.cloned.1.call-update) | async-done | bytes 49168 | tf_op jit(solution)/shard_map/reduce_scatter | solution.py:64
  769.3 21.2 %all_gather.27 = bf16[32,32,192]{2,0,1:T(8,128)(2,1)S(1)} all-gather(bf16[32,2,192]{2,0,1:T(8,128)(2,1)S(1)} %get-tuple-element.12), channel_id=1, replica_groups=mesh['row'=8,'col'=16] {'col'}, dimensions={1}, use_global_device_ids=true | all-gather | bytes 417792 | tf_op jit(solution)/shard_map/all_gather | solution.py:50
  792.1 3.3 fusion.85
  795.5 2.5 fusion.121
  798.0 70.9 %all-reduce.29.cloned.1.call-done = bf16[32,16,192]{2,0,1:T(8,128)(2,1)} async-done(((bf16[32,16,192]{2,0,1:T(8,128)(2,1)}), bf16[32,16,192]{2,0,1:T(8,128)(2,1)}) %all-reduce.29.cloned.1.call-update) | async-done | bytes 196624 | tf_op jit(solution)/shard_map/psum | solution.py:11
  870.5 3.9 fusion.82
  874.4 1.9 fusion.50
  876.3 78.7 %all-reduce.31.cloned.1.call-done = f32[32,16,192]{2,1,0:T(8,128)} async-done(((f32[32,16,192]{2,1,0:T(8,128)}), f32[32,16,192]{2,1,0:T(8,128)}) %all-reduce.31.cloned.1.call-update) | async-done | bytes 393232 | tf_op jit(solution)/shard_map/psum | solution.py:59
  959.0 63.4 %reduce-scatter.15.cloned.1.call-done = f32[32,2,192]{2,0,1:T(8,128)} async-done(((f32[32,32,192]{2,0,1:T(8,128)}), f32[32,2,192]{2,0,1:T(8,128)}) %reduce-scatter.15.cloned.1.call-update) | async-done | bytes 49168 | tf_op jit(solution)/shard_map/reduce_scatter | solution.py:64
  1023.2 21.2 %all_gather.28 = bf16[32,32,192]{2,0,1:T(8,128)(2,1)S(1)} all-gather(bf16[32,2,192]{2,0,1:T(8,128)(2,1)S(1)} %get-tuple-element.10), channel_id=1, replica_groups=mesh['row'=8,'col'=16] {'col'}, dimensions={1}, use_global_device_ids=true | all-gather | bytes 417792 | tf_op jit(solution)/shard_map/all_gather | solution.py:50
  1045.8 3.3 fusion.91
  1049.2 2.5 fusion.124
  1051.9 70.9 %all-reduce.33.cloned.1.call-done = bf16[32,16,192]{2,0,1:T(8,128)(2,1)} async-done(((bf16[32,16,192]{2,0,1:T(8,128)(2,1)}), bf16[32,16,192]{2,0,1:T(8,128)(2,1)}) %all-reduce.33.cloned.1.call-update) | async-done | bytes 196624 | tf_op jit(solution)/shard_map/psum | solution.py:11
  1124.4 3.9 fusion.88
  1128.3 1.9 fusion.46
  1130.2 78.7 %all-reduce.35.cloned.1.call-done = f32[32,16,192]{2,1,0:T(8,128)} async-done(((f32[32,16,192]{2,1,0:T(8,128)}), f32[32,16,192]{2,1,0:T(8,128)}) %all-reduce.35.cloned.1.call-update) | async-done | bytes 393232 | tf_op jit(solution)/shard_map/psum | solution.py:59
  1212.9 63.4 %reduce-scatter.17.cloned.1.call-done = f32[32,2,192]{2,0,1:T(8,128)} async-done(((f32[32,32,192]{2,0,1:T(8,128)}), f32[32,2,192]{2,0,1:T(8,128)}) %reduce-scatter.17.cloned.1.call-update) | async-done | bytes 49168 | tf_op jit(solution)/shard_map/reduce_scatter | solution.py:64
  1277.1 21.2 %all_gather.29 = bf16[32,32,192]{2,0,1:T(8,128)(2,1)S(1)} all-gather(bf16[32,2,192]{2,0,1:T(8,128)(2,1)S(1)} %get-tuple-element.8), channel_id=1, replica_groups=mesh['row'=8,'col'=16] {'col'}, dimensions={1}, use_global_device_ids=true | all-gather | bytes 417792 | tf_op jit(solution)/shard_map/all_gather | solution.py:50
  1299.7 3.3 fusion.97
  1303.1 2.5 fusion.127
  1305.6 71.1 %all-reduce.37.cloned.1.call-done = bf16[32,16,192]{2,0,1:T(8,128)(2,1)} async-done(((bf16[32,16,192]{2,0,1:T(8,128)(2,1)}), bf16[32,16,192]{2,0,1:T(8,128)(2,1)}) %all-reduce.37.cloned.1.call-update) | async-done | bytes 196624 | tf_op jit(solution)/shard_map/psum | solution.py:11
  1378.3 3.9 fusion.94
  1382.1 1.9 fusion.42
  1384.1 78.5 %all-reduce.39.cloned.1.call-done = f32[32,16,192]{2,1,0:T(8,128)} async-done(((f32[32,16,192]{2,1,0:T(8,128)}), f32[32,16,192]{2,1,0:T(8,128)}) %all-reduce.39.cloned.1.call-update) | async-done | bytes 393232 | tf_op jit(solution)/shard_map/psum | solution.py:59
  1466.6 63.4 %reduce-scatter.19.cloned.1.call-done = f32[32,2,192]{2,0,1:T(8,128)} async-done(((f32[32,32,192]{2,0,1:T(8,128)}), f32[32,2,192]{2,0,1:T(8,128)}) %reduce-scatter.19.cloned.1.call-update) | async-done | bytes 49168 | tf_op jit(solution)/shard_map/reduce_scatter | solution.py:64
  1530.8 21.2 %all_gather.30 = bf16[32,32,192]{2,0,1:T(8,128)(2,1)S(1)} all-gather(bf16[32,2,192]{2,0,1:T(8,128)(2,1)S(1)} %get-tuple-element.6), channel_id=1, replica_groups=mesh['row'=8,'col'=16] {'col'}, dimensions={1}, use_global_device_ids=true | all-gather | bytes 417792 | tf_op jit(solution)/shard_map/all_gather | solution.py:50
  1553.7 3.3 fusion.103
  1557.0 2.5 fusion.130
  1559.6 70.8 %all-reduce.41.cloned.1.call-done = bf16[32,16,192]{2,0,1:T(8,128)(2,1)} async-done(((bf16[32,16,192]{2,0,1:T(8,128)(2,1)}), bf16[32,16,192]{2,0,1:T(8,128)(2,1)}) %all-reduce.41.cloned.1.call-update) | async-done | bytes 196624 | tf_op jit(solution)/shard_map/psum | solution.py:11
  1632.0 3.9 fusion.100
  1635.9 1.9 fusion.38
  1637.8 78.7 %all-reduce.43.cloned.1.call-done = f32[32,16,192]{2,1,0:T(8,128)} async-done(((f32[32,16,192]{2,1,0:T(8,128)}), f32[32,16,192]{2,1,0:T(8,128)}) %all-reduce.43.cloned.1.call-update) | async-done | bytes 393232 | tf_op jit(solution)/shard_map/psum | solution.py:59
  1720.5 63.4 %reduce-scatter.21.cloned.1.call-done = f32[32,2,192]{2,0,1:T(8,128)} async-done(((f32[32,32,192]{2,0,1:T(8,128)}), f32[32,2,192]{2,0,1:T(8,128)}) %reduce-scatter.21.cloned.1.call-update) | async-done | bytes 49168 | tf_op jit(solution)/shard_map/reduce_scatter | solution.py:64
  1784.7 21.2 %all_gather.31 = bf16[32,32,192]{2,0,1:T(8,128)(2,1)S(1)} all-gather(bf16[32,2,192]{2,0,1:T(8,128)(2,1)S(1)} %get-tuple-element.4), channel_id=1, replica_groups=mesh['row'=8,'col'=16] {'col'}, dimensions={1}, use_global_device_ids=true | all-gather | bytes 417792 | tf_op jit(solution)/shard_map/all_gather | solution.py:50
  1807.3 3.3 fusion.109
  1810.7 2.5 fusion.133
  1813.5 70.8 %all-reduce.45.cloned.1.call-done = bf16[32,16,192]{2,0,1:T(8,128)(2,1)} async-done(((bf16[32,16,192]{2,0,1:T(8,128)(2,1)}), bf16[32,16,192]{2,0,1:T(8,128)(2,1)}) %all-reduce.45.cloned.1.call-update) | async-done | bytes 196624 | tf_op jit(solution)/shard_map/psum | solution.py:11
  1885.9 3.9 fusion.106
  1889.8 1.9 fusion.34
  1891.7 78.7 %all-reduce.47.cloned.1.call-done = f32[32,16,192]{2,1,0:T(8,128)} async-done(((f32[32,16,192]{2,1,0:T(8,128)}), f32[32,16,192]{2,1,0:T(8,128)}) %all-reduce.47.cloned.1.call-update) | async-done | bytes 393232 | tf_op jit(solution)/shard_map/psum | solution.py:59
  1975.1 62.6 %reduce-scatter.23.cloned.1.call-done = f32[32,2,192]{2,0,1:T(8,128)} async-done(((f32[32,32,192]{2,0,1:T(8,128)}), f32[32,2,192]{2,0,1:T(8,128)}) %reduce-scatter.23.cloned.1.call-update) | async-done | bytes 49168 | tf_op jit(solution)/shard_map/reduce_scatter | solution.py:64
  (126 shorter events, 66.7 us)
Async XLA Ops:
  7.2 24.0 %copy-start.1 = (s32[1,48]{1,0:T(1,128)S(1)}, s32[1,48]{1,0:T(1,128)}, u32[]{:S(2)}) copy-start(s32[1,48]{1,0:T(1,128)} %param.15) | copy-start | bytes 580
  7.2 24.0 %copy-start.3 = (s32[1,48]{1,0:T(1,128)S(1)}, s32[1,48]{1,0:T(1,128)}, u32[]{:S(2)}) copy-start(s32[1,48]{1,0:T(1,128)} %param.17) | copy-start | bytes 580
  7.2 99.9 %all-reduce.17.cloned.1.call-start = ((), (), s32[]{:S(2)}) async-start(), calls=%async_computation.8 | async-start | bytes 524288 | tf_op jit(solution)/shard_map/psum | solution.py:11
  31.1 162.2 %all-reduce.19.cloned.1.call-start = ((), (), s32[]{:S(2)}) async-start(), calls=%async_computation.9 | async-start | bytes 1048576 | tf_op jit(solution)/shard_map/psum | solution.py:59
  31.9 3.4 copy-start.2
  37.8 222.9 %reduce-scatter.9.cloned.1.call-start = ((), (), s32[]{:S(2)}) async-start(), calls=%async_computation.10 | async-start | bytes 1114112 | tf_op jit(solution)/shard_map/reduce_scatter | solution.py:64
  197.2 163.9 %all-reduce.21.cloned.1.call-start = ((), (), s32[]{:S(2)}) async-start(), calls=%async_computation.11 | async-start | bytes 524288 | tf_op jit(solution)/shard_map/psum | solution.py:11
  284.1 163.0 %all-reduce.23.cloned.1.call-start = ((), (), s32[]{:S(2)}) async-start(), calls=%async_computation.12 | async-start | bytes 1048576 | tf_op jit(solution)/shard_map/psum | solution.py:59
  290.0 224.4 %reduce-scatter.11.cloned.1.call-start = ((), (), s32[]{:S(2)}) async-start(), calls=%async_computation.13 | async-start | bytes 1114112 | tf_op jit(solution)/shard_map/reduce_scatter | solution.py:64
  449.3 65.0 %copy-start = (f32[32,2,192]{2,0,1:T(8,128)S(1)}, f32[32,2,192]{2,0,1:T(8,128)}, u32[]{:S(2)}) copy-start(f32[32,2,192]{2,0,1:T(8,128)} %reduce-scatter.9.cloned.1.call-done) | copy-start | bytes 147460
  451.0 163.9 %all-reduce.25.cloned.1.call-start = ((), (), s32[]{:S(2)}) async-start(), calls=%async_computation.14 | async-start | bytes 524288 | tf_op jit(solution)/shard_map/psum | solution.py:11
  537.8 163.3 %all-reduce.27.cloned.1.call-start = ((), (), s32[]{:S(2)}) async-start(), calls=%async_computation.15 | async-start | bytes 1048576 | tf_op jit(solution)/shard_map/psum | solution.py:59
  543.7 224.7 %reduce-scatter.13.cloned.1.call-start = ((), (), s32[]{:S(2)}) async-start(), calls=%async_computation.16 | async-start | bytes 1114112 | tf_op jit(solution)/shard_map/reduce_scatter | solution.py:64
  705.0 163.9 %all-reduce.29.cloned.1.call-start = ((), (), s32[]{:S(2)}) async-start(), calls=%async_computation.17 | async-start | bytes 524288 | tf_op jit(solution)/shard_map/psum | solution.py:11
  791.9 163.1 %all-reduce.31.cloned.1.call-start = ((), (), s32[]{:S(2)}) async-start(), calls=%async_computation.18 | async-start | bytes 1048576 | tf_op jit(solution)/shard_map/psum | solution.py:59
  798.0 224.4 %reduce-scatter.15.cloned.1.call-start = ((), (), s32[]{:S(2)}) async-start(), calls=%async_computation.19 | async-start | bytes 1114112 | tf_op jit(solution)/shard_map/reduce_scatter | solution.py:64
  958.9 163.9 %all-reduce.33.cloned.1.call-start = ((), (), s32[]{:S(2)}) async-start(), calls=%async_computation.20 | async-start | bytes 524288 | tf_op jit(solution)/shard_map/psum | solution.py:11
  1045.8 163.1 %all-reduce.35.cloned.1.call-start = ((), (), s32[]{:S(2)}) async-start(), calls=%async_computation.21 | async-start | bytes 1048576 | tf_op jit(solution)/shard_map/psum | solution.py:59
  1051.7 224.6 %reduce-scatter.17.cloned.1.call-start = ((), (), s32[]{:S(2)}) async-start(), calls=%async_computation.22 | async-start | bytes 1114112 | tf_op jit(solution)/shard_map/reduce_scatter | solution.py:64
  1212.8 163.9 %all-reduce.37.cloned.1.call-start = ((), (), s32[]{:S(2)}) async-start(), calls=%async_computation.23 | async-start | bytes 524288 | tf_op jit(solution)/shard_map/psum | solution.py:11
  1299.7 163.0 %all-reduce.39.cloned.1.call-start = ((), (), s32[]{:S(2)}) async-start(), calls=%async_computation.24 | async-start | bytes 1048576 | tf_op jit(solution)/shard_map/psum | solution.py:59
  1305.6 224.4 %reduce-scatter.19.cloned.1.call-start = ((), (), s32[]{:S(2)}) async-start(), calls=%async_computation.25 | async-start | bytes 1114112 | tf_op jit(solution)/shard_map/reduce_scatter | solution.py:64
  1466.5 163.9 %all-reduce.41.cloned.1.call-start = ((), (), s32[]{:S(2)}) async-start(), calls=%async_computation.26 | async-start | bytes 524288 | tf_op jit(solution)/shard_map/psum | solution.py:11
  1553.4 163.1 %all-reduce.43.cloned.1.call-start = ((), (), s32[]{:S(2)}) async-start(), calls=%async_computation.27 | async-start | bytes 1048576 | tf_op jit(solution)/shard_map/psum | solution.py:59
  1559.6 224.3 %reduce-scatter.21.cloned.1.call-start = ((), (), s32[]{:S(2)}) async-start(), calls=%async_computation.28 | async-start | bytes 1114112 | tf_op jit(solution)/shard_map/reduce_scatter | solution.py:64
  1720.4 163.9 %all-reduce.45.cloned.1.call-start = ((), (), s32[]{:S(2)}) async-start(), calls=%async_computation.29 | async-start | bytes 524288 | tf_op jit(solution)/shard_map/psum | solution.py:11
  1807.3 163.1 %all-reduce.47.cloned.1.call-start = ((), (), s32[]{:S(2)}) async-start(), calls=%async_computation.30 | async-start | bytes 1048576 | tf_op jit(solution)/shard_map/psum | solution.py:59
  1813.2 224.5 %reduce-scatter.23.cloned.1.call-start = ((), (), s32[]{:S(2)}) async-start(), calls=%async_computation.31 | async-start | bytes 1114112 | tf_op jit(solution)/shard_map/reduce_scatter | solution.py:64
Sparse Core Ops, SparseCore 0:
  31.3 75.7 all-reduce.16
  109.7 83.5 all-reduce.18
  197.3 63.2 reduce-scatter.8
  284.2 76.8 all-reduce.20
  363.4 83.5 all-reduce.22
  451.1 63.2 reduce-scatter.10
  538.0 76.8 all-reduce.24
  617.5 83.5 all-reduce.26
  705.1 63.2 reduce-scatter.12
  792.0 76.8 all-reduce.28
  871.4 83.5 all-reduce.30
  959.0 63.2 reduce-scatter.14
  1045.9 76.8 all-reduce.32
  1125.3 83.5 all-reduce.34
  1212.9 63.2 reduce-scatter.16
  1299.8 76.8 all-reduce.36
  1379.0 83.5 all-reduce.38
  1466.7 63.2 reduce-scatter.18
  1553.5 76.8 all-reduce.40
  1632.9 83.5 all-reduce.42
  1720.5 63.2 reduce-scatter.20
  1807.4 76.8 all-reduce.44
  1886.8 83.5 all-reduce.46
  1974.4 63.2 reduce-scatter.22
where the time goes:
time: 2060 us; the launch traced here: 2050 us
  waiting for transfers between devices  1700 us (83%)
  blocking collectives  170 us (8%)
  matrix products  93.3 us (5%)
  local copies, waits for them, and re-layouts  41.9 us (2%)
  other arithmetic  21.9 us (1%)
    psum x8, waiting for transfers between devices, body(): mirror_total = lax.psum(mirror_part, 'row')  629 us
    psum x8, waiting for transfers between devices, spread(): return lax.psum(block, axis)  565 us
    reduce_scatter x8, waiting for transfers between devices, body(): lax.psum_scatter(partial_sum, 'col', scatter_dimension=1, tiled=True)  505 us
    all_gather x8, blocking collectives, body(): lax.all_gather(current.astype(jnp.bfloat16), 'col', axis=1, tiled=True)  170 us
  transfers between devices with their start and end apart: 24, of which 24 were waited for; matrix products, arithmetic and copies ran while one was open for 5% of the time, Pallas kernels for 0%

commit v1 on v0

v1 whole, which is shorter than its diff:
```python
import jax
import jax.numpy as jnp
from jax import lax
from jax.experimental import pallas as pl
from jax.experimental.pallas import tpu as pltpu
from jax.sharding import PartitionSpec as P

DEG = 8
GROUP = 8


def products_kernel(table, x_ref, own_ref, other_ref, out_ref, x_wide, total):
    clusters, vectors, _ = x_wide.shape
    size = own_ref.shape[-1]
    pairs = clusters // 2
    low = lax.broadcasted_iota(jnp.int32, (vectors, 128), 1) < 64

    for pair in range(pairs):
        first, middle, last = (x_ref[pair, :, 128 * i : 128 * (i + 1)].astype(jnp.float32) for i in range(3))
        middle_rolled, last_rolled = pltpu.roll(middle, 64, 1), pltpu.roll(last, 64, 1)
        x_wide[2 * pair, :, :128] = first.astype(jnp.bfloat16)
        x_wide[2 * pair, :, 128:] = middle.astype(jnp.bfloat16)
        x_wide[2 * pair + 1, :, :128] = jnp.where(low, middle_rolled, last_rolled).astype(jnp.bfloat16)
        x_wide[2 * pair + 1, :, 128:] = last_rolled.astype(jnp.bfloat16)

    total[...] = jnp.zeros_like(total)

    def run(contract):
        for part, tiles in enumerate((own_ref, other_ref)):

            @pl.loop(0, table[0, 1 + part])
            def _(group):
                sums = [
                    lax.dot_general(
                        x_wide[table[3 + part, group * GROUP + member], :, :size],
                        tiles[table[1 + part, group * GROUP + member]],
                        (((1,), (contract,)), ((), ())),
                        preferred_element_type=jnp.float32,
                    )
                    for member in range(GROUP)
                ]
                for member in range(GROUP):
                    where = table[5 + part, group * GROUP + member]
                    total[where, :, :size] += sums[member]

    @pl.when(table[0, 0] == 0)
    def _():
        run(0)

    @pl.when(table[0, 0] == 1)
    def _():
        run(1)

    for pair in range(pairs):
        even_a, even_b = total[2 * pair, :, :128], total[2 * pair, :, 128:]
        odd_a = pltpu.roll(total[2 * pair + 1, :, :128], 64, 1)
        odd_b = pltpu.roll(total[2 * pair + 1, :, 128:], 64, 1)
        out_ref[pair, :, :128] = even_a.astype(jnp.bfloat16)
        out_ref[pair, :, 128:256] = jnp.where(low, even_b, odd_a).astype(jnp.bfloat16)
        out_ref[pair, :, 256:] = jnp.where(low, odd_a, odd_b).astype(jnp.bfloat16)


def products(table, x, own, other):
    pairs, vectors, width = x.shape
    count, size, _ = own.shape
    smem = pl.BlockSpec(memory_space=pltpu.SMEM)
    vmem = pl.BlockSpec(memory_space=pltpu.VMEM)
    flops = 2 * 2 * count * size * size * vectors
    return pl.pallas_call(
        products_kernel,
        out_shape=jax.ShapeDtypeStruct(x.shape, jnp.bfloat16),
        in_specs=[smem, vmem, vmem, vmem],
        out_specs=vmem,
        scratch_shapes=[
            pltpu.VMEM((2 * pairs, vectors, 256), jnp.bfloat16),
            pltpu.VMEM((2 * pairs + 1, vectors, 256), jnp.float32),
        ],
        compiler_params=pltpu.CompilerParams(vmem_limit_bytes=24 * 1024 * 1024),
        cost_estimate=pl.CostEstimate(flops=flops, bytes_accessed=2 * count * size * size * 2, transcendentals=0),
    )(table, x, own, other)


def body(start_block, center, half_width, matrix_tiles, tile_row, tile_col, tile_live):
    vectors, width = start_block.shape
    slots_here = tile_row.shape[1]
    row_count, col_count = lax.axis_size("row"), lax.axis_size("col")
    side = row_count
    core = lax.axis_index("col") % 2
    axes = ("row", "col")

    def device(r, c2, h):
        return r * col_count + 2 * c2 + h

    grid = [(r, c2, h) for r in range(side) for c2 in range(side) for h in range(2)]
    swap = [(device(r, c2, h), device(r, c2, 1 - h)) for r, c2, h in grid]
    turn = [(device(r, c2, h), device(c2, r, h)) for r, c2, h in grid]
    along_row = [[[device(r, k, h) for k in range(side)] for r in range(side)] for h in range(2)]
    along_col = [[[device(k, c2, h) for k in range(side)] for c2 in range(side)] for h in range(2)]
    gather_groups = along_row[0] + along_col[1]
    scatter_groups = along_col[0] + along_row[1]

    def exchange(value, groups):
        return lax.all_to_all(value, axes, 0, 0, axis_index_groups=groups, tiled=False)

    own = matrix_tiles[0]
    other = lax.ppermute(own, axes, swap)
    panel = 2 * side
    col_here = tile_col[0] + core * panel
    ids = jnp.stack([tile_row[0], col_here, tile_live[0]])
    ids = jnp.stack([ids, lax.ppermute(ids, axes, swap)], 1)
    alive = ids[2] > 0
    position = jnp.cumsum(alive.astype(jnp.int32), axis=1) - 1
    places = slots_here + GROUP
    hit = (position[:, None, :] == jnp.arange(places)[None, :, None]) & alive[:, None, :]
    counts = jnp.sum(alive.astype(jnp.int32), axis=1)

    def pick(value, empty):
        found = jnp.sum(jnp.where(hit, value[:, None, :], 0), axis=2)
        return jnp.where(jnp.arange(places)[None, :] < counts[:, None], found, empty).astype(jnp.int32)

    slots = pick(jnp.broadcast_to(jnp.arange(slots_here)[None, :], alive.shape), 0)
    ins = pick(jnp.where(core == 0, ids[0], ids[1]), 0)
    outs = pick(jnp.where(core == 0, ids[1], ids[0]), 4 * side)
    info = jnp.concatenate([core[None], (counts + GROUP - 1) // GROUP]).astype(jnp.int32)
    table = jnp.concatenate([jnp.pad(info, (0, places - 3))[None], slots, ins, outs])

    mine = start_block
    theirs = lax.ppermute(mine, axes, swap)
    by_row = jnp.where(core == 0, jnp.stack([mine, theirs]), jnp.stack([theirs, mine]))
    current = jnp.where(core == 0, by_row, lax.ppermute(by_row, axes, turn))
    earlier = current
    center_value, half_value = center[0], half_width[0]
    for degree in range(DEG):
        rounded = current.astype(jnp.bfloat16)
        x = exchange(jnp.broadcast_to(rounded[None], (side, *rounded.shape)), gather_groups)
        partial = products(table, x.reshape(2 * side, vectors, width), own, other)
        parts = exchange(partial.reshape(side, 2, vectors, width), scatter_groups)
        share = jnp.sum(parts.astype(jnp.float32), axis=0).astype(jnp.bfloat16)
        product = lax.ppermute(share, axes, swap).astype(jnp.float32) + lax.ppermute(share, axes, turn).astype(jnp.float32)
        following = (product - center_value * current) / half_value
        if degree > 0:
            following = 2.0 * following - earlier
        earlier, current = current, following

    def own_pair(value):
        sent = lax.ppermute(value[1], axes, swap)
        return jnp.where(core == 0, value[0], sent)

    return own_pair(current), own_pair(earlier)


def solution(mesh):
    in_specs = (
        P(None, ("row", "col")),
        P(),
        P(),
        P("row", "col", None, None),
        P("row", "col"),
        P("row", "col"),
        P("row", "col"),
    )
    out_specs = (P(None, ("row", "col")), P(None, ("row", "col")))
    return jax.shard_map(body, mesh=mesh, in_specs=in_specs, out_specs=out_specs, check_vma=False)
```

time: 2060 us -> 371 us (0.18)
  waiting for transfers between devices: 1700 us -> 28.3 us
  matrix products: 93.3 us -> 0 us
  starting transfers between devices: 2.46 us -> 92.1 us
  Pallas kernels: 0 us -> 50.1 us
  local copies, waits for them, and re-layouts: 41.9 us -> 19.8 us
    psum x16 -> x0, waiting for transfers between devices: 1190 us -> none  [the longest x8 629 us: body(): mirror_total = lax.psum(mirror_part, 'row')]
    reduce_scatter x8 -> x0, waiting for transfers between devices: 505 us -> none  [body(): lax.psum_scatter(partial_sum, 'col', scatter_dimension=1, tiled=True)]
    all_gather x8 -> x0, blocking collectives: 170 us -> none  [body(): lax.all_gather(current.astype(jnp.bfloat16), 'col', axis=1, tiled=True)]
    all_to_all x0 -> x15, blocking collectives: none -> 170 us  [exchange(): lax.all_to_all(value, axes, 0, 0, axis_index_groups=groups, tiled=False)]
    dot_general x32 -> x0, matrix products: 93.3 us -> none  [the longest x8 31 us: body(): jnp.einsum('ksb,sab->ksa', x_col, stored, preferred_element_type=jnp.floa...]
    ppermute x0 -> x22, starting transfers between devices: none -> 87.6 us  [the longest x8 41.7 us: body(): lax.ppermute(share, axes, turn).astype(jnp.float32)]
    pallas_call x0 -> x8, Pallas kernels: none -> 50.1 us  [products(): pl.pallas_call(products_kernel, out_shape=jax.ShapeDtypeStruct(x.shape, j...]
    ppermute x0 -> x22, waiting for transfers between devices: none -> 22.4 us  [the longest x1 7.84 us: body(): current = jnp.where(core == 0, by_row, lax.ppermute(by_row, axes, turn))]
  transfers between devices with their start and end apart: 24 -> 23, of which waited for: 24 -> 13; matrix products, arithmetic and copies ran while one was open for 5% -> 1% of each run, Pallas kernels for 0% -> 0%
where the time goes in v1:
time: 371 us; the launch traced here: 369 us
  blocking collectives  170 us (46%)
  starting transfers between devices  92.1 us (25%)
  Pallas kernels  50.1 us (14%)
  waiting for transfers between devices  28.3 us (8%)
  local copies, waits for them, and re-layouts  19.8 us (5%)
  other arithmetic  5.79 us (2%)
    all_to_all x15, blocking collectives, exchange(): lax.all_to_all(value, axes, 0, 0, axis_index_groups=groups, tiled=False)  170 us
    pallas_call x8, Pallas kernels, products(): pl.pallas_call(products_kernel, out_shape=jax.ShapeDtypeStruct(x.shape, j...  50.1 us
    ppermute x8, starting transfers between devices, body(): lax.ppermute(share, axes, turn).astype(jnp.float32)  41.7 us
    ppermute x8, starting transfers between devices, body(): lax.ppermute(share, axes, swap).astype(jnp.float32)  33.7 us
    unnamed x16, local copies, waits for them, and re-layouts  18.7 us
    ppermute x1, waiting for transfers between devices, body(): current = jnp.where(core == 0, by_row, lax.ppermute(by_row, axes, turn))  7.84 us
  transfers between devices with their start and end apart: 23, of which 13 were waited for; matrix products, arithmetic and copies ran while one was open for 1% of the time, Pallas kernels for 0%

profile of v1, /device:TPU:7, one launch (start us, length us, event | category | flops | bytes accessed | tf_op | source)
XLA Modules:
  0.0 368.6 jit_solution(12897123660851989365)
XLA Ops:
  0.6 0.8 collective-permute-start.3
  3.3 5.6 %collective-permute-done = s32[3,48]{1,0:T(4,128)S(1)} collective-permute-done((s32[3,48]{1,0:T(4,128)S(1)}, s32[3,48]{1,0:T(4,128)S(1)}, u32[]{:S(2)}, u32[]{:S(2)}) %collective-permute-start) | collective-permute-done | bytes 608 | tf_op jit(solution)/shard_map/ppermute | solution.py:110
  9.5 0.9 maximum_select_fusion
  10.4 6.1 %collective-permute-start.2 = (f32[2,32,384]{2,1,0:T(8,128)S(1)}, f32[2,32,384]{2,1,0:T(8,128)S(1)}, u32[]{:S(2)}, u32[]{:S(2)}) collective-permute-start(f32[2,32,384]{2,1,0:T(8,128)S(1)} %maximum_select_fusion), channel_id=1, source_target_pairs={{0,0},{1,1},{2,16},{3,17},{4,32},{5,33},{6,48},{7,49},{8,64},{9,65... | collective-permute-start | bytes 294920 | tf_op jit(solution)/shard_map/ppermute | solution.py:130
  16.5 7.8 %collective-permute-done.2 = f32[2,32,384]{2,1,0:T(8,128)S(1)} collective-permute-done((f32[2,32,384]{2,1,0:T(8,128)S(1)}, f32[2,32,384]{2,1,0:T(8,128)S(1)}, u32[]{:S(2)}, u32[]{:S(2)}) %collective-permute-start.2) | collective-permute-done | bytes 98336 | tf_op jit(solution)/shard_map/ppermute | solution.py:130
  24.4 0.9 fusion.14
  25.3 0.8 broadcast_in_dim.106
  26.1 4.5 %all-to-all-start = ((bf16[8,2,32,384]{3,2,1,0:T(8,128)(2,1)}), bf16[8,2,32,384]{3,2,1,0:T(8,128)(2,1)S(1)}, u32[]{:S(2)}, u32[]{:S(2)}) async-start(bf16[8,2,32,384]{3,2,1,0:T(8,128)(2,1)} %broadcast_in_dim.106), calls=%async_computation | async-start | bytes 786432 | tf_op jit(solution)/shard_map/all_to_all | solution.py:103
  30.6 5.9 %all-to-all-done = bf16[8,2,32,384]{3,2,1,0:T(8,128)(2,1)S(1)} async-done(((bf16[8,2,32,384]{3,2,1,0:T(8,128)(2,1)}), bf16[8,2,32,384]{3,2,1,0:T(8,128)(2,1)S(1)}, u32[]{:S(2)}, u32[]{:S(2)}) %all-to-all-start) | async-done | bytes 393248 | tf_op jit(solution)/shard_map/all_to_all | solution.py:103
  36.5 2.3 copy-done
  38.8 6.3 %shard_map.86 = bf16[16,32,384]{2,1,0:T(8,128)(2,1)S(1)} custom-call(s32[7,56]{1,0:T(8,128)S(1)} %pad_add_fusion.table, bf16[16,32,384]{2,1,0:T(8,128)(2,1)S(1)} %bitcast.69, bf16[48,192,192]{2,1,0:T(8,128)(2,1)S(1)} %bitcast.61, bf16[48,192,192]{2,1,0:T(8,128)(2,1)} %collective-permute-done.3.other_ref), custom_call_target="tpu_custom_call" | custom-call | flops 226492416 | bytes 7077888 | tf_op jit(solution)/shard_map/pallas_call | solution.py:69
  45.1 16.3 %all_to_all.80 = bf16[8,2,32,384]{3,2,1,0:T(8,128)(2,1)S(1)} all-to-all(bf16[8,2,32,384]{3,2,1,0:T(8,128)(2,1)S(1)} %bitcast.72), channel_id=1, replica_groups={{0,16,32,48,64,80,96,112},{2,18,34,50,66,82,98,114},{4,20,36,52,68,84,1..., dimensions={0} | all-to-all | bytes 786432 | tf_op jit(solution)/shard_map/all_to_all | solution.py:103
  61.5 4.9 %collective-permute-start.5 = (bf16[2,32,384]{2,1,0:T(8,128)(2,1)S(1)}, bf16[2,32,384]{2,1,0:T(8,128)(2,1)S(1)}, u32[]{:S(2)}, u32[]{:S(2)}) collective-permute-start(bf16[2,32,384]{2,1,0:T(8,128)(2,1)S(1)} %reduce_sum.136), channel_id=1, source_target_pairs={{0,0},{1,1},{2,16},{3,17},{4,32},{5,33},{6,48},{7,49},{8,64},{9,65... | collective-permute-start | bytes 147464 | tf_op jit(solution)/shard_map/ppermute | solution.py:139
  66.4 1.4 collective-permute-start.4
  69.1 2.7 collective-permute-done.5
  71.8 10.0 %all_to_all.81 = bf16[8,2,32,384]{3,2,1,0:T(8,128)(2,1)S(1)} all-to-all(bf16[8,2,32,384]{3,2,1,0:T(8,128)(2,1)S(1)} %broadcast_in_dim.107), channel_id=1, replica_groups={{0,2,4,6,8,10,12,14},{16,18,20,22,24,26,28,30},{32,34,36,38,40,42,44,46..., dimensions={0} | all-to-all | bytes 786432 | tf_op jit(solution)/shard_map/all_to_all | solution.py:103
  81.8 2.3 copy-done.1
  84.2 6.3 %shard_map.87 = bf16[16,32,384]{2,1,0:T(8,128)(2,1)S(1)} custom-call(s32[7,56]{1,0:T(8,128)S(1)} %pad_add_fusion.table, bf16[16,32,384]{2,1,0:T(8,128)(2,1)S(1)} %bitcast.73, bf16[48,192,192]{2,1,0:T(8,128)(2,1)S(1)} %bitcast.62, bf16[48,192,192]{2,1,0:T(8,128)(2,1)} %collective-permute-done.3.other_ref), custom_call_target="tpu_custom_call" | custom-call | flops 226492416 | bytes 7077888 | tf_op jit(solution)/shard_map/pallas_call | solution.py:69
  90.4 11.4 %all_to_all.82 = bf16[8,2,32,384]{3,2,1,0:T(8,128)(2,1)S(1)} all-to-all(bf16[8,2,32,384]{3,2,1,0:T(8,128)(2,1)S(1)} %bitcast.74), channel_id=1, replica_groups={{0,16,32,48,64,80,96,112},{2,18,34,50,66,82,98,114},{4,20,36,52,68,84,1..., dimensions={0} | all-to-all | bytes 786432 | tf_op jit(solution)/shard_map/all_to_all | solution.py:103
  101.9 7.3 %collective-permute-start.7 = (bf16[2,32,384]{2,1,0:T(8,128)(2,1)S(1)}, bf16[2,32,384]{2,1,0:T(8,128)(2,1)S(1)}, u32[]{:S(2)}, u32[]{:S(2)}) collective-permute-start(bf16[2,32,384]{2,1,0:T(8,128)(2,1)S(1)} %reduce_sum.137), channel_id=1, source_target_pairs={{0,0},{1,1},{2,16},{3,17},{4,32},{5,33},{6,48},{7,49},{8,64},{9,65... | collective-permute-start | bytes 147464 | tf_op jit(solution)/shard_map/ppermute | solution.py:139
  109.2 1.4 collective-permute-start.6
  111.6 11.7 %all_to_all.83 = bf16[8,2,32,384]{3,2,1,0:T(8,128)(2,1)S(1)} all-to-all(bf16[8,2,32,384]{3,2,1,0:T(8,128)(2,1)S(1)} %broadcast_in_dim.108), channel_id=1, replica_groups={{0,2,4,6,8,10,12,14},{16,18,20,22,24,26,28,30},{32,34,36,38,40,42,44,46..., dimensions={0} | all-to-all | bytes 786432 | tf_op jit(solution)/shard_map/all_to_all | solution.py:103
  123.3 2.3 copy-done.2
  125.6 6.3 %shard_map.88 = bf16[16,32,384]{2,1,0:T(8,128)(2,1)S(1)} custom-call(s32[7,56]{1,0:T(8,128)S(1)} %pad_add_fusion.table, bf16[16,32,384]{2,1,0:T(8,128)(2,1)S(1)} %bitcast.75, bf16[48,192,192]{2,1,0:T(8,128)(2,1)S(1)} %bitcast.63, bf16[48,192,192]{2,1,0:T(8,128)(2,1)} %collective-permute-done.3.other_ref), custom_call_target="tpu_custom_call" | custom-call | flops 226492416 | bytes 7077888 | tf_op jit(solution)/shard_map/pallas_call | solution.py:69
  131.9 10.9 %all_to_all.84 = bf16[8,2,32,384]{3,2,1,0:T(8,128)(2,1)S(1)} all-to-all(bf16[8,2,32,384]{3,2,1,0:T(8,128)(2,1)S(1)} %bitcast.76), channel_id=1, replica_groups={{0,16,32,48,64,80,96,112},{2,18,34,50,66,82,98,114},{4,20,36,52,68,84,1..., dimensions={0} | all-to-all | bytes 786432 | tf_op jit(solution)/shard_map/all_to_all | solution.py:103
  142.8 5.1 %collective-permute-start.9 = (bf16[2,32,384]{2,1,0:T(8,128)(2,1)S(1)}, bf16[2,32,384]{2,1,0:T(8,128)(2,1)S(1)}, u32[]{:S(2)}, u32[]{:S(2)}) collective-permute-start(bf16[2,32,384]{2,1,0:T(8,128)(2,1)S(1)} %reduce_sum.138), channel_id=1, source_target_pairs={{0,0},{1,1},{2,16},{3,17},{4,32},{5,33},{6,48},{7,49},{8,64},{9,65... | collective-permute-start | bytes 147464 | tf_op jit(solution)/shard_map/ppermute | solution.py:139
  147.9 5.4 %collective-permute-start.8 = (bf16[2,32,384]{2,1,0:T(8,128)(2,1)S(1)}, bf16[2,32,384]{2,1,0:T(8,128)(2,1)S(1)}, u32[]{:S(2)}, u32[]{:S(2)}) collective-permute-start(bf16[2,32,384]{2,1,0:T(8,128)(2,1)S(1)} %reduce_sum.138), channel_id=1, source_target_pairs={{0,1},{1,0},{2,3},{3,2},{4,5},{5,4},{6,7},{7,6},{8,9},{9,8},{10,11... | collective-permute-start | bytes 147464 | tf_op jit(solution)/shard_map/ppermute | solution.py:139
  153.3 0.9 collective-permute-done.8
  154.3 11.1 %all_to_all.85 = bf16[8,2,32,384]{3,2,1,0:T(8,128)(2,1)S(1)} all-to-all(bf16[8,2,32,384]{3,2,1,0:T(8,128)(2,1)S(1)} %broadcast_in_dim.109), channel_id=1, replica_groups={{0,2,4,6,8,10,12,14},{16,18,20,22,24,26,28,30},{32,34,36,38,40,42,44,46..., dimensions={0} | all-to-all | bytes 786432 | tf_op jit(solution)/shard_map/all_to_all | solution.py:103
  165.5 2.3 copy-done.3
  167.8 6.3 %shard_map.89 = bf16[16,32,384]{2,1,0:T(8,128)(2,1)S(1)} custom-call(s32[7,56]{1,0:T(8,128)S(1)} %pad_add_fusion.table, bf16[16,32,384]{2,1,0:T(8,128)(2,1)S(1)} %bitcast.77, bf16[48,192,192]{2,1,0:T(8,128)(2,1)S(1)} %bitcast.64, bf16[48,192,192]{2,1,0:T(8,128)(2,1)} %collective-permute-done.3.other_ref), custom_call_target="tpu_custom_call" | custom-call | flops 226492416 | bytes 7077888 | tf_op jit(solution)/shard_map/pallas_call | solution.py:69
  174.1 10.7 %all_to_all.86 = bf16[8,2,32,384]{3,2,1,0:T(8,128)(2,1)S(1)} all-to-all(bf16[8,2,32,384]{3,2,1,0:T(8,128)(2,1)S(1)} %bitcast.78), channel_id=1, replica_groups={{0,16,32,48,64,80,96,112},{2,18,34,50,66,82,98,114},{4,20,36,52,68,84,1..., dimensions={0} | all-to-all | bytes 786432 | tf_op jit(solution)/shard_map/all_to_all | solution.py:103
  184.8 4.9 %collective-permute-start.11 = (bf16[2,32,384]{2,1,0:T(8,128)(2,1)S(1)}, bf16[2,32,384]{2,1,0:T(8,128)(2,1)S(1)}, u32[]{:S(2)}, u32[]{:S(2)}) collective-permute-start(bf16[2,32,384]{2,1,0:T(8,128)(2,1)S(1)} %reduce_sum.139), channel_id=1, source_target_pairs={{0,0},{1,1},{2,16},{3,17},{4,32},{5,33},{6,48},{7,49},{8,64},{9,65... | collective-permute-start | bytes 147464 | tf_op jit(solution)/shard_map/ppermute | solution.py:139
  189.7 5.1 %collective-permute-start.10 = (bf16[2,32,384]{2,1,0:T(8,128)(2,1)S(1)}, bf16[2,32,384]{2,1,0:T(8,128)(2,1)S(1)}, u32[]{:S(2)}, u32[]{:S(2)}) collective-permute-start(bf16[2,32,384]{2,1,0:T(8,128)(2,1)S(1)} %reduce_sum.139), channel_id=1, source_target_pairs={{0,1},{1,0},{2,3},{3,2},{4,5},{5,4},{6,7},{7,6},{8,9},{9,8},{10,11... | collective-permute-start | bytes 147464 | tf_op jit(solution)/shard_map/ppermute | solution.py:139
  194.8 0.9 collective-permute-done.10
  195.8 11.7 %all_to_all.87 = bf16[8,2,32,384]{3,2,1,0:T(8,128)(2,1)S(1)} all-to-all(bf16[8,2,32,384]{3,2,1,0:T(8,128)(2,1)S(1)} %broadcast_in_dim.110), channel_id=1, replica_groups={{0,2,4,6,8,10,12,14},{16,18,20,22,24,26,28,30},{32,34,36,38,40,42,44,46..., dimensions={0} | all-to-all | bytes 786432 | tf_op jit(solution)/shard_map/all_to_all | solution.py:103
  207.5 2.3 copy-done.4
  209.8 6.3 %shard_map.90 = bf16[16,32,384]{2,1,0:T(8,128)(2,1)S(1)} custom-call(s32[7,56]{1,0:T(8,128)S(1)} %pad_add_fusion.table, bf16[16,32,384]{2,1,0:T(8,128)(2,1)S(1)} %bitcast.79, bf16[48,192,192]{2,1,0:T(8,128)(2,1)S(1)} %bitcast.65, bf16[48,192,192]{2,1,0:T(8,128)(2,1)} %collective-permute-done.3.other_ref), custom_call_target="tpu_custom_call" | custom-call | flops 226492416 | bytes 7077888 | tf_op jit(solution)/shard_map/pallas_call | solution.py:69
  216.1 10.4 %all_to_all.88 = bf16[8,2,32,384]{3,2,1,0:T(8,128)(2,1)S(1)} all-to-all(bf16[8,2,32,384]{3,2,1,0:T(8,128)(2,1)S(1)} %bitcast.80), channel_id=1, replica_groups={{0,16,32,48,64,80,96,112},{2,18,34,50,66,82,98,114},{4,20,36,52,68,84,1..., dimensions={0} | all-to-all | bytes 786432 | tf_op jit(solution)/shard_map/all_to_all | solution.py:103
  226.5 5.1 %collective-permute-start.13 = (bf16[2,32,384]{2,1,0:T(8,128)(2,1)S(1)}, bf16[2,32,384]{2,1,0:T(8,128)(2,1)S(1)}, u32[]{:S(2)}, u32[]{:S(2)}) collective-permute-start(bf16[2,32,384]{2,1,0:T(8,128)(2,1)S(1)} %reduce_sum.140), channel_id=1, source_target_pairs={{0,0},{1,1},{2,16},{3,17},{4,32},{5,33},{6,48},{7,49},{8,64},{9,65... | collective-permute-start | bytes 147464 | tf_op jit(solution)/shard_map/ppermute | solution.py:139
  231.6 4.8 %collective-permute-start.12 = (bf16[2,32,384]{2,1,0:T(8,128)(2,1)S(1)}, bf16[2,32,384]{2,1,0:T(8,128)(2,1)S(1)}, u32[]{:S(2)}, u32[]{:S(2)}) collective-permute-start(bf16[2,32,384]{2,1,0:T(8,128)(2,1)S(1)} %reduce_sum.140), channel_id=1, source_target_pairs={{0,1},{1,0},{2,3},{3,2},{4,5},{5,4},{6,7},{7,6},{8,9},{9,8},{10,11... | collective-permute-start | bytes 147464 | tf_op jit(solution)/shard_map/ppermute | solution.py:139
  236.4 0.9 collective-permute-done.12
  237.4 11.5 %all_to_all.89 = bf16[8,2,32,384]{3,2,1,0:T(8,128)(2,1)S(1)} all-to-all(bf16[8,2,32,384]{3,2,1,0:T(8,128)(2,1)S(1)} %broadcast_in_dim.111), channel_id=1, replica_groups={{0,2,4,6,8,10,12,14},{16,18,20,22,24,26,28,30},{32,34,36,38,40,42,44,46..., dimensions={0} | all-to-all | bytes 786432 | tf_op jit(solution)/shard_map/all_to_all | solution.py:103
  248.9 2.3 copy-done.5
  251.2 6.3 %shard_map.91 = bf16[16,32,384]{2,1,0:T(8,128)(2,1)S(1)} custom-call(s32[7,56]{1,0:T(8,128)S(1)} %pad_add_fusion.table, bf16[16,32,384]{2,1,0:T(8,128)(2,1)S(1)} %bitcast.81, bf16[48,192,192]{2,1,0:T(8,128)(2,1)S(1)} %bitcast.66, bf16[48,192,192]{2,1,0:T(8,128)(2,1)} %collective-permute-done.3.other_ref), custom_call_target="tpu_custom_call" | custom-call | flops 226492416 | bytes 7077888 | tf_op jit(solution)/shard_map/pallas_call | solution.py:69
  257.5 10.5 %all_to_all.90 = bf16[8,2,32,384]{3,2,1,0:T(8,128)(2,1)S(1)} all-to-all(bf16[8,2,32,384]{3,2,1,0:T(8,128)(2,1)S(1)} %bitcast.82), channel_id=1, replica_groups={{0,16,32,48,64,80,96,112},{2,18,34,50,66,82,98,114},{4,20,36,52,68,84,1..., dimensions={0} | all-to-all | bytes 786432 | tf_op jit(solution)/shard_map/all_to_all | solution.py:103
  268.1 4.5 %collective-permute-start.15 = (bf16[2,32,384]{2,1,0:T(8,128)(2,1)S(1)}, bf16[2,32,384]{2,1,0:T(8,128)(2,1)S(1)}, u32[]{:S(2)}, u32[]{:S(2)}) collective-permute-start(bf16[2,32,384]{2,1,0:T(8,128)(2,1)S(1)} %reduce_sum.141), channel_id=1, source_target_pairs={{0,0},{1,1},{2,16},{3,17},{4,32},{5,33},{6,48},{7,49},{8,64},{9,65... | collective-permute-start | bytes 147464 | tf_op jit(solution)/shard_map/ppermute | solution.py:139
  272.6 5.6 %collective-permute-start.14 = (bf16[2,32,384]{2,1,0:T(8,128)(2,1)S(1)}, bf16[2,32,384]{2,1,0:T(8,128)(2,1)S(1)}, u32[]{:S(2)}, u32[]{:S(2)}) collective-permute-start(bf16[2,32,384]{2,1,0:T(8,128)(2,1)S(1)} %reduce_sum.141), channel_id=1, source_target_pairs={{0,1},{1,0},{2,3},{3,2},{4,5},{5,4},{6,7},{7,6},{8,9},{9,8},{10,11... | collective-permute-start | bytes 147464 | tf_op jit(solution)/shard_map/ppermute | solution.py:139
  278.2 0.9 collective-permute-done.14
  279.2 11.6 %all_to_all.91 = bf16[8,2,32,384]{3,2,1,0:T(8,128)(2,1)S(1)} all-to-all(bf16[8,2,32,384]{3,2,1,0:T(8,128)(2,1)S(1)} %broadcast_in_dim.112), channel_id=1, replica_groups={{0,2,4,6,8,10,12,14},{16,18,20,22,24,26,28,30},{32,34,36,38,40,42,44,46..., dimensions={0} | all-to-all | bytes 786432 | tf_op jit(solution)/shard_map/all_to_all | solution.py:103
  290.8 2.3 copy-done.6
  293.1 6.3 %shard_map.92 = bf16[16,32,384]{2,1,0:T(8,128)(2,1)S(1)} custom-call(s32[7,56]{1,0:T(8,128)S(1)} %pad_add_fusion.table, bf16[16,32,384]{2,1,0:T(8,128)(2,1)S(1)} %bitcast.83, bf16[48,192,192]{2,1,0:T(8,128)(2,1)S(1)} %bitcast.67, bf16[48,192,192]{2,1,0:T(8,128)(2,1)} %collective-permute-done.3.other_ref), custom_call_target="tpu_custom_call" | custom-call | flops 226492416 | bytes 7077888 | tf_op jit(solution)/shard_map/pallas_call | solution.py:69
  299.4 10.4 %all_to_all.92 = bf16[8,2,32,384]{3,2,1,0:T(8,128)(2,1)S(1)} all-to-all(bf16[8,2,32,384]{3,2,1,0:T(8,128)(2,1)S(1)} %bitcast.84), channel_id=1, replica_groups={{0,16,32,48,64,80,96,112},{2,18,34,50,66,82,98,114},{4,20,36,52,68,84,1..., dimensions={0} | all-to-all | bytes 786432 | tf_op jit(solution)/shard_map/all_to_all | solution.py:103
  309.8 5.2 %collective-permute-start.17 = (bf16[2,32,384]{2,1,0:T(8,128)(2,1)S(1)}, bf16[2,32,384]{2,1,0:T(8,128)(2,1)S(1)}, u32[]{:S(2)}, u32[]{:S(2)}) collective-permute-start(bf16[2,32,384]{2,1,0:T(8,128)(2,1)S(1)} %reduce_sum.142), channel_id=1, source_target_pairs={{0,0},{1,1},{2,16},{3,17},{4,32},{5,33},{6,48},{7,49},{8,64},{9,65... | collective-permute-start | bytes 147464 | tf_op jit(solution)/shard_map/ppermute | solution.py:139
  315.0 4.8 %collective-permute-start.16 = (bf16[2,32,384]{2,1,0:T(8,128)(2,1)S(1)}, bf16[2,32,384]{2,1,0:T(8,128)(2,1)S(1)}, u32[]{:S(2)}, u32[]{:S(2)}) collective-permute-start(bf16[2,32,384]{2,1,0:T(8,128)(2,1)S(1)} %reduce_sum.142), channel_id=1, source_target_pairs={{0,1},{1,0},{2,3},{3,2},{4,5},{5,4},{6,7},{7,6},{8,9},{9,8},{10,11... | collective-permute-start | bytes 147464 | tf_op jit(solution)/shard_map/ppermute | solution.py:139
  319.8 0.9 collective-permute-done.16
  320.8 10.9 %all_to_all.93 = bf16[8,2,32,384]{3,2,1,0:T(8,128)(2,1)S(1)} all-to-all(bf16[8,2,32,384]{3,2,1,0:T(8,128)(2,1)S(1)} %broadcast_in_dim.113), channel_id=1, replica_groups={{0,2,4,6,8,10,12,14},{16,18,20,22,24,26,28,30},{32,34,36,38,40,42,44,46..., dimensions={0} | all-to-all | bytes 786432 | tf_op jit(solution)/shard_map/all_to_all | solution.py:103
  331.7 2.3 copy-done.7
  334.1 6.3 %shard_map.93 = bf16[16,32,384]{2,1,0:T(8,128)(2,1)S(1)} custom-call(s32[7,56]{1,0:T(8,128)S(1)} %pad_add_fusion.table, bf16[16,32,384]{2,1,0:T(8,128)(2,1)S(1)} %bitcast.70, bf16[48,192,192]{2,1,0:T(8,128)(2,1)S(1)} %bitcast.68, bf16[48,192,192]{2,1,0:T(8,128)(2,1)} %collective-permute-done.3.other_ref), custom_call_target="tpu_custom_call" | custom-call | flops 226492416 | bytes 7077888 | tf_op jit(solution)/shard_map/pallas_call | solution.py:69
  340.3 11.2 %all_to_all.94 = bf16[8,2,32,384]{3,2,1,0:T(8,128)(2,1)S(1)} all-to-all(bf16[8,2,32,384]{3,2,1,0:T(8,128)(2,1)S(1)} %bitcast.71), channel_id=1, replica_groups={{0,16,32,48,64,80,96,112},{2,18,34,50,66,82,98,114},{4,20,36,52,68,84,1..., dimensions={0} | all-to-all | bytes 786432 | tf_op jit(solution)/shard_map/all_to_all | solution.py:103
  351.6 4.7 %collective-permute-start.19 = (bf16[2,32,384]{2,1,0:T(8,128)(2,1)S(1)}, bf16[2,32,384]{2,1,0:T(8,128)(2,1)S(1)}, u32[]{:S(2)}, u32[]{:S(2)}) collective-permute-start(bf16[2,32,384]{2,1,0:T(8,128)(2,1)S(1)} %reduce_sum.143), channel_id=1, source_target_pairs={{0,0},{1,1},{2,16},{3,17},{4,32},{5,33},{6,48},{7,49},{8,64},{9,65... | collective-permute-start | bytes 147464 | tf_op jit(solution)/shard_map/ppermute | solution.py:139
  356.3 5.2 %collective-permute-start.18 = (bf16[2,32,384]{2,1,0:T(8,128)(2,1)S(1)}, bf16[2,32,384]{2,1,0:T(8,128)(2,1)S(1)}, u32[]{:S(2)}, u32[]{:S(2)}) collective-permute-start(bf16[2,32,384]{2,1,0:T(8,128)(2,1)S(1)} %reduce_sum.143), channel_id=1, source_target_pairs={{0,1},{1,0},{2,3},{3,2},{4,5},{5,4},{6,7},{7,6},{8,9},{9,8},{10,11... | collective-permute-start | bytes 147464 | tf_op jit(solution)/shard_map/ppermute | solution.py:139
  361.6 0.8 collective-permute-done.18
  362.4 4.7 %collective-permute-start.20 = (f32[32,384]{1,0:T(8,128)S(1)}, f32[32,384]{1,0:T(8,128)S(1)}, u32[]{:S(2)}, u32[]{:S(2)}) collective-permute-start(f32[32,384]{1,0:T(8,128)S(1)} %slice_bitcast_fusion.2), channel_id=1, source_target_pairs={{0,1},{1,0},{2,3},{3,2},{4,5},{5,4},{6,7},{7,6},{8,9},{9,8},{10,11... | collective-permute-start | bytes 147464 | tf_op jit(solution)/shard_map/ppermute | solution.py:146
  (66 shorter events, 6.1 us)
Async XLA Ops:
  0.6 35.9 %collective-permute-start.3 = (bf16[48,192,192]{2,1,0:T(8,128)(2,1)}, bf16[48,192,192]{2,1,0:T(8,128)(2,1)}, u32[]{:S(2)}, u32[]{:S(2)}) collective-permute-start(bf16[48,192,192]{2,1,0:T(8,128)(2,1)} %bitcast.60), channel_id=1, source_target_pairs={{0,1},{1,0},{2,3},{3,2},{4,5},{5,4},{6,7},{7,6},{8,9},{9,8},{10,11... | collective-permute-start | bytes 10616840 | tf_op jit(solution)/shard_map/ppermute | solution.py:106
  2.7 6.2 %collective-permute-start = (s32[3,48]{1,0:T(4,128)S(1)}, s32[3,48]{1,0:T(4,128)S(1)}, u32[]{:S(2)}, u32[]{:S(2)}) collective-permute-start(s32[3,48]{1,0:T(4,128)S(1)} %get-tuple-element.25), channel_id=1, source_target_pairs={{0,1},{1,0},{2,3},{3,2},{4,5},{5,4},{6,7},{7,6},{8,9},{9,8},{10,11... | collective-permute-start | bytes 1736 | tf_op jit(solution)/shard_map/ppermute | solution.py:110
  2.8 6.6 %collective-permute-start.1 = (f32[32,384]{1,0:T(8,128)}, f32[32,384]{1,0:T(8,128)S(1)}, u32[]{:S(2)}, u32[]{:S(2)}) collective-permute-start(f32[32,384]{1,0:T(8,128)} %param.7), channel_id=1, source_target_pairs={{0,1},{1,0},{2,3},{3,2},{4,5},{5,4},{6,7},{7,6},{8,9},{9,8},{10,11... | collective-permute-start | bytes 147464 | tf_op jit(solution)/shard_map/ppermute | solution.py:128
  10.4 14.0 %collective-permute-start.2 = (f32[2,32,384]{2,1,0:T(8,128)S(1)}, f32[2,32,384]{2,1,0:T(8,128)S(1)}, u32[]{:S(2)}, u32[]{:S(2)}) collective-permute-start(f32[2,32,384]{2,1,0:T(8,128)S(1)} %maximum_select_fusion), channel_id=1, source_target_pairs={{0,0},{1,1},{2,16},{3,17},{4,32},{5,33},{6,48},{7,49},{8,64},{9,65... | collective-permute-start | bytes 294920 | tf_op jit(solution)/shard_map/ppermute | solution.py:130
  26.1 10.4 %all-to-all-start = ((bf16[8,2,32,384]{3,2,1,0:T(8,128)(2,1)}), bf16[8,2,32,384]{3,2,1,0:T(8,128)(2,1)S(1)}, u32[]{:S(2)}, u32[]{:S(2)}) async-start(bf16[8,2,32,384]{3,2,1,0:T(8,128)(2,1)} %broadcast_in_dim.106), calls=%async_computation | async-start | bytes 786432 | tf_op jit(solution)/shard_map/all_to_all | solution.py:103
  36.5 2.3 copy-start
  61.5 10.2 %collective-permute-start.5 = (bf16[2,32,384]{2,1,0:T(8,128)(2,1)S(1)}, bf16[2,32,384]{2,1,0:T(8,128)(2,1)S(1)}, u32[]{:S(2)}, u32[]{:S(2)}) collective-permute-start(bf16[2,32,384]{2,1,0:T(8,128)(2,1)S(1)} %reduce_sum.136), channel_id=1, source_target_pairs={{0,0},{1,1},{2,16},{3,17},{4,32},{5,33},{6,48},{7,49},{8,64},{9,65... | collective-permute-start | bytes 147464 | tf_op jit(solution)/shard_map/ppermute | solution.py:139
  66.4 5.4 %collective-permute-start.4 = (bf16[2,32,384]{2,1,0:T(8,128)(2,1)S(1)}, bf16[2,32,384]{2,1,0:T(8,128)(2,1)S(1)}, u32[]{:S(2)}, u32[]{:S(2)}) collective-permute-start(bf16[2,32,384]{2,1,0:T(8,128)(2,1)S(1)} %reduce_sum.136), channel_id=1, source_target_pairs={{0,1},{1,0},{2,3},{3,2},{4,5},{5,4},{6,7},{7,6},{8,9},{9,8},{10,11... | collective-permute-start | bytes 147464 | tf_op jit(solution)/shard_map/ppermute | solution.py:139
  81.8 2.3 copy-start.1
  101.9 9.3 %collective-permute-start.7 = (bf16[2,32,384]{2,1,0:T(8,128)(2,1)S(1)}, bf16[2,32,384]{2,1,0:T(8,128)(2,1)S(1)}, u32[]{:S(2)}, u32[]{:S(2)}) collective-permute-start(bf16[2,32,384]{2,1,0:T(8,128)(2,1)S(1)} %reduce_sum.137), channel_id=1, source_target_pairs={{0,0},{1,1},{2,16},{3,17},{4,32},{5,33},{6,48},{7,49},{8,64},{9,65... | collective-permute-start | bytes 147464 | tf_op jit(solution)/shard_map/ppermute | solution.py:139
  109.2 2.3 collective-permute-start.6
  123.3 2.3 copy-start.2
  142.8 10.5 %collective-permute-start.9 = (bf16[2,32,384]{2,1,0:T(8,128)(2,1)S(1)}, bf16[2,32,384]{2,1,0:T(8,128)(2,1)S(1)}, u32[]{:S(2)}, u32[]{:S(2)}) collective-permute-start(bf16[2,32,384]{2,1,0:T(8,128)(2,1)S(1)} %reduce_sum.138), channel_id=1, source_target_pairs={{0,0},{1,1},{2,16},{3,17},{4,32},{5,33},{6,48},{7,49},{8,64},{9,65... | collective-permute-start | bytes 147464 | tf_op jit(solution)/shard_map/ppermute | solution.py:139
  147.9 6.3 %collective-permute-start.8 = (bf16[2,32,384]{2,1,0:T(8,128)(2,1)S(1)}, bf16[2,32,384]{2,1,0:T(8,128)(2,1)S(1)}, u32[]{:S(2)}, u32[]{:S(2)}) collective-permute-start(bf16[2,32,384]{2,1,0:T(8,128)(2,1)S(1)} %reduce_sum.138), channel_id=1, source_target_pairs={{0,1},{1,0},{2,3},{3,2},{4,5},{5,4},{6,7},{7,6},{8,9},{9,8},{10,11... | collective-permute-start | bytes 147464 | tf_op jit(solution)/shard_map/ppermute | solution.py:139
  165.5 2.3 copy-start.3
  184.8 10.0 %collective-permute-start.11 = (bf16[2,32,384]{2,1,0:T(8,128)(2,1)S(1)}, bf16[2,32,384]{2,1,0:T(8,128)(2,1)S(1)}, u32[]{:S(2)}, u32[]{:S(2)}) collective-permute-start(bf16[2,32,384]{2,1,0:T(8,128)(2,1)S(1)} %reduce_sum.139), channel_id=1, source_target_pairs={{0,0},{1,1},{2,16},{3,17},{4,32},{5,33},{6,48},{7,49},{8,64},{9,65... | collective-permute-start | bytes 147464 | tf_op jit(solution)/shard_map/ppermute | solution.py:139
  189.7 6.0 %collective-permute-start.10 = (bf16[2,32,384]{2,1,0:T(8,128)(2,1)S(1)}, bf16[2,32,384]{2,1,0:T(8,128)(2,1)S(1)}, u32[]{:S(2)}, u32[]{:S(2)}) collective-permute-start(bf16[2,32,384]{2,1,0:T(8,128)(2,1)S(1)} %reduce_sum.139), channel_id=1, source_target_pairs={{0,1},{1,0},{2,3},{3,2},{4,5},{5,4},{6,7},{7,6},{8,9},{9,8},{10,11... | collective-permute-start | bytes 147464 | tf_op jit(solution)/shard_map/ppermute | solution.py:139
  207.4 2.3 copy-start.4
  226.5 9.9 %collective-permute-start.13 = (bf16[2,32,384]{2,1,0:T(8,128)(2,1)S(1)}, bf16[2,32,384]{2,1,0:T(8,128)(2,1)S(1)}, u32[]{:S(2)}, u32[]{:S(2)}) collective-permute-start(bf16[2,32,384]{2,1,0:T(8,128)(2,1)S(1)} %reduce_sum.140), channel_id=1, source_target_pairs={{0,0},{1,1},{2,16},{3,17},{4,32},{5,33},{6,48},{7,49},{8,64},{9,65... | collective-permute-start | bytes 147464 | tf_op jit(solution)/shard_map/ppermute | solution.py:139
  231.6 5.7 %collective-permute-start.12 = (bf16[2,32,384]{2,1,0:T(8,128)(2,1)S(1)}, bf16[2,32,384]{2,1,0:T(8,128)(2,1)S(1)}, u32[]{:S(2)}, u32[]{:S(2)}) collective-permute-start(bf16[2,32,384]{2,1,0:T(8,128)(2,1)S(1)} %reduce_sum.140), channel_id=1, source_target_pairs={{0,1},{1,0},{2,3},{3,2},{4,5},{5,4},{6,7},{7,6},{8,9},{9,8},{10,11... | collective-permute-start | bytes 147464 | tf_op jit(solution)/shard_map/ppermute | solution.py:139
  248.9 2.3 copy-start.5
  268.1 10.1 %collective-permute-start.15 = (bf16[2,32,384]{2,1,0:T(8,128)(2,1)S(1)}, bf16[2,32,384]{2,1,0:T(8,128)(2,1)S(1)}, u32[]{:S(2)}, u32[]{:S(2)}) collective-permute-start(bf16[2,32,384]{2,1,0:T(8,128)(2,1)S(1)} %reduce_sum.141), channel_id=1, source_target_pairs={{0,0},{1,1},{2,16},{3,17},{4,32},{5,33},{6,48},{7,49},{8,64},{9,65... | collective-permute-start | bytes 147464 | tf_op jit(solution)/shard_map/ppermute | solution.py:139
  272.6 6.5 %collective-permute-start.14 = (bf16[2,32,384]{2,1,0:T(8,128)(2,1)S(1)}, bf16[2,32,384]{2,1,0:T(8,128)(2,1)S(1)}, u32[]{:S(2)}, u32[]{:S(2)}) collective-permute-start(bf16[2,32,384]{2,1,0:T(8,128)(2,1)S(1)} %reduce_sum.141), channel_id=1, source_target_pairs={{0,1},{1,0},{2,3},{3,2},{4,5},{5,4},{6,7},{7,6},{8,9},{9,8},{10,11... | collective-permute-start | bytes 147464 | tf_op jit(solution)/shard_map/ppermute | solution.py:139
  290.8 2.3 copy-start.6
  309.8 10.0 %collective-permute-start.17 = (bf16[2,32,384]{2,1,0:T(8,128)(2,1)S(1)}, bf16[2,32,384]{2,1,0:T(8,128)(2,1)S(1)}, u32[]{:S(2)}, u32[]{:S(2)}) collective-permute-start(bf16[2,32,384]{2,1,0:T(8,128)(2,1)S(1)} %reduce_sum.142), channel_id=1, source_target_pairs={{0,0},{1,1},{2,16},{3,17},{4,32},{5,33},{6,48},{7,49},{8,64},{9,65... | collective-permute-start | bytes 147464 | tf_op jit(solution)/shard_map/ppermute | solution.py:139
  315.0 5.7 %collective-permute-start.16 = (bf16[2,32,384]{2,1,0:T(8,128)(2,1)S(1)}, bf16[2,32,384]{2,1,0:T(8,128)(2,1)S(1)}, u32[]{:S(2)}, u32[]{:S(2)}) collective-permute-start(bf16[2,32,384]{2,1,0:T(8,128)(2,1)S(1)} %reduce_sum.142), channel_id=1, source_target_pairs={{0,1},{1,0},{2,3},{3,2},{4,5},{5,4},{6,7},{7,6},{8,9},{9,8},{10,11... | collective-permute-start | bytes 147464 | tf_op jit(solution)/shard_map/ppermute | solution.py:139
  331.7 2.3 copy-start.7
  351.6 10.0 %collective-permute-start.19 = (bf16[2,32,384]{2,1,0:T(8,128)(2,1)S(1)}, bf16[2,32,384]{2,1,0:T(8,128)(2,1)S(1)}, u32[]{:S(2)}, u32[]{:S(2)}) collective-permute-start(bf16[2,32,384]{2,1,0:T(8,128)(2,1)S(1)} %reduce_sum.143), channel_id=1, source_target_pairs={{0,0},{1,1},{2,16},{3,17},{4,32},{5,33},{6,48},{7,49},{8,64},{9,65... | collective-permute-start | bytes 147464 | tf_op jit(solution)/shard_map/ppermute | solution.py:139
  356.3 6.0 %collective-permute-start.18 = (bf16[2,32,384]{2,1,0:T(8,128)(2,1)S(1)}, bf16[2,32,384]{2,1,0:T(8,128)(2,1)S(1)}, u32[]{:S(2)}, u32[]{:S(2)}) collective-permute-start(bf16[2,32,384]{2,1,0:T(8,128)(2,1)S(1)} %reduce_sum.143), channel_id=1, source_target_pairs={{0,1},{1,0},{2,3},{3,2},{4,5},{5,4},{6,7},{7,6},{8,9},{9,8},{10,11... | collective-permute-start | bytes 147464 | tf_op jit(solution)/shard_map/ppermute | solution.py:139
  361.5 5.7 %collective-permute-start.21 = (f32[32,384]{1,0:T(8,128)S(1)}, f32[32,384]{1,0:T(8,128)S(1)}, u32[]{:S(2)}, u32[]{:S(2)}) collective-permute-start(f32[32,384]{1,0:T(8,128)S(1)} %slice_bitcast_fusion), channel_id=1, source_target_pairs={{0,1},{1,0},{2,3},{3,2},{4,5},{5,4},{6,7},{7,6},{8,9},{9,8},{10,11... | collective-permute-start | bytes 147464 | tf_op jit(solution)/shard_map/ppermute | solution.py:146
  362.4 5.6 %collective-permute-start.20 = (f32[32,384]{1,0:T(8,128)S(1)}, f32[32,384]{1,0:T(8,128)S(1)}, u32[]{:S(2)}, u32[]{:S(2)}) collective-permute-start(f32[32,384]{1,0:T(8,128)S(1)} %slice_bitcast_fusion.2), channel_id=1, source_target_pairs={{0,1},{1,0},{2,3},{3,2},{4,5},{5,4},{6,7},{7,6},{8,9},{9,8},{10,11... | collective-permute-start | bytes 147464 | tf_op jit(solution)/shard_map/ppermute | solution.py:146

commit v2 on v1

v2 whole, which is shorter than its diff:
```python
import jax
import jax.numpy as jnp
from jax import lax
from jax.experimental import pallas as pl
from jax.experimental.pallas import tpu as pltpu
from jax.sharding import PartitionSpec as P

DEG = 8
GROUP = 8


def keep_kernel(own_ref, other_ref, kept_ref, sems):
    count = own_ref.shape[0]
    copies = [
        pltpu.make_async_copy(ref, kept_ref.at[pl.ds(part * count, count)], sems.at[part])
        for part, ref in enumerate((own_ref, other_ref))
    ]
    for copy in copies:
        copy.start()
    for copy in copies:
        copy.wait()


def keep(own, other):
    count, size, _ = own.shape
    any_space = pl.BlockSpec(memory_space=pl.ANY)
    return pl.pallas_call(
        keep_kernel,
        out_shape=jax.ShapeDtypeStruct((2 * count, size, size), own.dtype),
        in_specs=[any_space, any_space],
        out_specs=pl.BlockSpec(memory_space=pltpu.VMEM),
        scratch_shapes=[pltpu.SemaphoreType.DMA((2,))],
        compiler_params=pltpu.CompilerParams(vmem_limit_bytes=16 * 1024 * 1024),
        cost_estimate=pl.CostEstimate(flops=0, bytes_accessed=4 * count * size * size * 2, transcendentals=0),
    )(own, other)


def products_kernel(table, fold_ref, x_ref, tiles_ref, out_ref, x_wide, total):
    vectors, size = x_wide.shape[1], tiles_ref.shape[-1]
    pairs = x_ref.shape[0]
    low = lax.broadcasted_iota(jnp.int32, (vectors, 128), 1) < 64
    fold = fold_ref[:1, :]

    def place(cluster, half, value):
        x_wide[cluster, :, 128 * half : 128 * (half + 1)] = value.astype(jnp.bfloat16)
        total[cluster, :, 128 * half : 128 * (half + 1)] = value * fold

    for pair in range(pairs):
        first, middle, last = (x_ref[pair, :, 128 * i : 128 * (i + 1)].astype(jnp.float32) for i in range(3))
        middle_rolled, last_rolled = pltpu.roll(middle, 64, 1), pltpu.roll(last, 64, 1)
        place(2 * pair, 0, first)
        place(2 * pair, 1, middle)
        place(2 * pair + 1, 0, jnp.where(low, middle_rolled, last_rolled))
        place(2 * pair + 1, 1, last_rolled)
    for half in range(2):
        place(2 * pairs, half, jnp.zeros((vectors, 128), jnp.float32))

    def run(contract):
        @pl.loop(0, table[0, 1])
        def _(group):
            sums = [
                lax.dot_general(
                    x_wide[table[2, group * GROUP + member], :, :size],
                    tiles_ref[table[1, group * GROUP + member]],
                    (((1,), (contract,)), ((), ())),
                    preferred_element_type=jnp.float32,
                )
                for member in range(GROUP)
            ]
            for member in range(GROUP):
                total[table[3, group * GROUP + member], :, :size] += sums[member]

    @pl.when(table[0, 0] == 0)
    def _():
        run(0)

    @pl.when(table[0, 0] == 1)
    def _():
        run(1)

    for pair in range(pairs):
        even_a, even_b = total[2 * pair, :, :128], total[2 * pair, :, 128:]
        odd_a = pltpu.roll(total[2 * pair + 1, :, :128], 64, 1)
        odd_b = pltpu.roll(total[2 * pair + 1, :, 128:], 64, 1)
        out_ref[pair, :, :128] = even_a.astype(jnp.bfloat16)
        out_ref[pair, :, 128:256] = jnp.where(low, even_b, odd_a).astype(jnp.bfloat16)
        out_ref[pair, :, 256:] = jnp.where(low, odd_a, odd_b).astype(jnp.bfloat16)


def products(table, fold, x, tiles):
    pairs, vectors, width = x.shape
    count, size, _ = tiles.shape
    vmem = pl.BlockSpec(memory_space=pltpu.VMEM)
    return pl.pallas_call(
        products_kernel,
        out_shape=jax.ShapeDtypeStruct(x.shape, jnp.bfloat16),
        in_specs=[pl.BlockSpec(memory_space=pltpu.SMEM), vmem, vmem, vmem],
        out_specs=vmem,
        scratch_shapes=[
            pltpu.VMEM((2 * pairs + 1, vectors, 256), jnp.bfloat16),
            pltpu.VMEM((2 * pairs + 1, vectors, 256), jnp.float32),
        ],
        compiler_params=pltpu.CompilerParams(vmem_limit_bytes=16 * 1024 * 1024),
        cost_estimate=pl.CostEstimate(
            flops=2 * count * size * size * vectors, bytes_accessed=count * size * size * 2, transcendentals=0
        ),
    )(table, fold, x, tiles)


def column_owner(side):
    def ring(a, b, n):
        return min((a - b) % n, (b - a) % n)

    half = side // 2
    owner = []
    for s in range(side):
        away = sorted(range(side), key=lambda k: (ring(k % half, s % half, half) + (k // half != s // half), k))
        near = sorted(range(side), key=lambda q: (ring(q // 2, s // 2, half) + 2 * (q % 2 != s % 2), q))
        pairing = dict(zip(away, reversed(near)))
        owner.append([pairing[k] for k in range(side)])
    return owner


def body(start_block, center, half_width, matrix_tiles, tile_row, tile_col, tile_live):
    vectors, width = start_block.shape
    slots_here = tile_row.shape[1]
    row_count, col_count = lax.axis_size("row"), lax.axis_size("col")
    side = row_count
    core = lax.axis_index("col") % 2
    diagonal = lax.axis_index("row") == lax.axis_index("col") // 2
    axes = ("row", "col")
    owner = column_owner(side)

    def device(r, c2, h):
        return r * col_count + 2 * c2 + h

    span = range(side)
    swap = [(device(r, c2, h), device(r, c2, 1 - h)) for r in span for c2 in span for h in range(2)]
    along_row = [[[device(s, k, h) for k in span] for s in span] for h in range(2)]
    along_col = [[[device(owner[s][k], s, h) for k in span] for s in span] for h in range(2)]
    gather_groups = [along_row[h] + along_col[1 - h] for h in range(2)]
    turns = [
        [pair for s in span for k in span for a, b in [(along_row[h][s][k], along_col[1 - h][s][k])] for pair in ((a, b), (b, a))]
        for h in range(2)
    ]

    def exchange(value, groups):
        return lax.all_to_all(value, axes, 0, 0, axis_index_groups=groups, tiled=False)

    def send(value, pairs):
        return lax.ppermute(value, axes, pairs)

    panel = 2 * side
    ids = jnp.stack([tile_row[0], tile_col[0] + core * panel, tile_live[0]])
    theirs, ids_there = send(start_block, swap), send(ids, swap)
    by_row = jnp.where(core == 0, jnp.stack([start_block, theirs]), jnp.stack([theirs, start_block]))
    own, by_row, ids_there = lax.optimization_barrier((matrix_tiles[0], by_row, ids_there))
    to_column = [pair for s in span for k in span for pair in [(device(s, k, 1), along_col[1][s][k])]]
    start_turned = send(by_row, to_column + [(device(s, k, 0), device(s, k, 0)) for s in span for k in span])
    tiles = keep(own, send(own, swap))

    ids = jnp.concatenate([ids, ids_there], 1)
    alive = ids[2] > 0
    position = jnp.cumsum(alive.astype(jnp.int32)) - 1
    places = 2 * slots_here + GROUP
    hit = (position[None, :] == jnp.arange(places)[:, None]) & alive[None, :]
    count = jnp.sum(alive.astype(jnp.int32))

    def pick(value, empty):
        found = jnp.sum(jnp.where(hit, value[None, :], 0), axis=1)
        return jnp.where(jnp.arange(places) < count, found, empty).astype(jnp.int32)

    slots = pick(jnp.arange(2 * slots_here), 0)
    rows, cols = pick(ids[0], 4 * side), pick(ids[1], 4 * side)

    def table_of(role):
        head = jnp.pad(jnp.stack([role, (count + GROUP - 1) // GROUP]).astype(jnp.int32), (0, places - 2))
        first = role == 0
        return jnp.stack([head, slots, jnp.where(first, rows, cols), jnp.where(first, cols, rows)])

    center_value, half_value = center[0], half_width[0]
    folds = [jnp.full((8, 128), jnp.where(diagonal & (core == h), -center_value, 0.0)) for h in range(2)]
    tables = [table_of(core), table_of(1 - core)]

    start_turned, tiles, tables, folds = lax.optimization_barrier((start_turned, tiles, tables, folds))
    current = start_turned
    earlier = current
    for degree in range(DEG):
        lead = degree % 2
        rounded = current.astype(jnp.bfloat16)
        x = exchange(jnp.broadcast_to(rounded[None], (side, *rounded.shape)), gather_groups[lead])
        partial = products(tables[lead], folds[lead], x.reshape(2 * side, vectors, width), tiles)
        parts = exchange(partial.reshape(side, 2, vectors, width), gather_groups[1 - lead])
        share = jnp.sum(parts.astype(jnp.float32), axis=0)
        product = share + send(share.astype(jnp.bfloat16), turns[1 - lead]).astype(jnp.float32)
        following = product / half_value if degree == 0 else 2.0 * product / half_value - earlier
        earlier, current = current, following

    got = send(jnp.where(core == 0, current[1], earlier[0]), swap)
    return jnp.where(core == 0, current[0], got), jnp.where(core == 0, got, earlier[1])


def solution(mesh):
    in_specs = (
        P(None, ("row", "col")),
        P(),
        P(),
        P("row", "col", None, None),
        P("row", "col"),
        P("row", "col"),
        P("row", "col"),
    )
    out_specs = (P(None, ("row", "col")), P(None, ("row", "col")))
    return jax.shard_map(body, mesh=mesh, in_specs=in_specs, out_specs=out_specs, check_vma=False)
```

time: 371 us -> 312 us (0.84)
  starting transfers between devices: 92.1 us -> 56.9 us
  local copies, waits for them, and re-layouts: 19.8 us -> 2.77 us
  blocking collectives: 170 us -> 186 us
  Pallas kernels: 50.1 us -> 34.4 us
  waiting for transfers between devices: 28.3 us -> 19.8 us
    ppermute x22 -> x13, starting transfers between devices: 87.6 us -> 56.9 us  [send(): return lax.ppermute(value, axes, pairs)]
    pallas_call x8, Pallas kernels: 50.1 us -> 31.7 us  [products(): pl.pallas_call(products_kernel, out_shape=jax.ShapeDtypeStruct(x.shape, j...]
    unnamed x16 -> x2, local copies, waits for them, and re-layouts: 18.7 us -> 2.33 us
    all_to_all x15 -> x16, blocking collectives: 170 us -> 186 us  [exchange(): lax.all_to_all(value, axes, 0, 0, axis_index_groups=groups, tiled=False)]
    all_to_all x1 -> x0, waiting for transfers between devices: 5.86 us -> none  [exchange(): lax.all_to_all(value, axes, 0, 0, axis_index_groups=groups, tiled=False)]
    all_to_all x1 -> x0, starting transfers between devices: 4.47 us -> none  [exchange(): lax.all_to_all(value, axes, 0, 0, axis_index_groups=groups, tiled=False)]
    ppermute x22 -> x13, waiting for transfers between devices: 22.4 us -> 19.8 us  [send(): return lax.ppermute(value, axes, pairs)]
  transfers between devices with their start and end apart: 23 -> 13, of which waited for: 13 -> 10; matrix products, arithmetic and copies ran while one was open for 1% -> 2% of each run, Pallas kernels for 0% -> 1%
where the time goes in v2:
time: 312 us; the launch traced here: 308 us
  blocking collectives  186 us (60%)
  starting transfers between devices  56.9 us (18%)
  Pallas kernels  34.4 us (11%)
  waiting for transfers between devices  19.8 us (6%)
  other arithmetic  6.01 us (2%)
    all_to_all x16, blocking collectives, exchange(): lax.all_to_all(value, axes, 0, 0, axis_index_groups=groups, tiled=False)  186 us
    ppermute x13, starting transfers between devices, send(): return lax.ppermute(value, axes, pairs)  56.9 us
    pallas_call x8, Pallas kernels, products(): pl.pallas_call(products_kernel, out_shape=jax.ShapeDtypeStruct(x.shape, j...  31.7 us
    ppermute x13, waiting for transfers between devices, send(): return lax.ppermute(value, axes, pairs)  19.8 us
  transfers between devices with their start and end apart: 13, of which 10 were waited for; matrix products, arithmetic and copies ran while one was open for 2% of the time, Pallas kernels for 1%

profile of v2, /device:TPU:7, one launch (start us, length us, event | category | flops | bytes accessed | tf_op | source)
XLA Modules:
  0.0 308.3 jit_solution(8977359187177378840)
XLA Ops:
  0.6 0.8 collective-permute-start
  1.4 0.7 broadcast_add_fusion
  2.0 0.7 pad_add_fusion.2
  2.7 0.1 collective-permute-start.1
  2.8 0.9 maximum_select_fusion
  3.7 0.2 collective-permute-done.1
  3.9 0.3 collective-permute-start.3
  4.9 0.7 pad_add_fusion.3
  5.7 0.6 fusion.10
  6.8 6.3 %collective-permute-start.2 = (f32[2,32,384]{2,1,0:T(8,128)S(1)}, f32[2,32,384]{2,1,0:T(8,128)S(1)}, u32[]{:S(2)}, u32[]{:S(2)}) collective-permute-start(f32[2,32,384]{2,1,0:T(8,128)S(1)} %maximum_select_fusion), channel_id=1, source_target_pairs={{1,81},{3,113},{5,17},{7,49},{9,65},{11,97},{13,1},{15,33},{17,99}... | collective-permute-start | bytes 294920 | tf_op jit(solution)/shard_map/ppermute | solution.py:151
  13.1 0.1 copy.11
  13.2 0.1 reduce-window.8
  13.4 0.1 pad_add_fusion.4
  13.5 0.1 add_reduce_fusion
  13.6 0.1 select_reduce_fusion.1
  13.7 0.5 broadcast_select_fusion.1
  14.3 2.3 copy-done
  16.7 2.7 shard_map.86.tiles_ref
  19.4 13.9 %all_to_all.80 = bf16[8,2,32,384]{3,2,1,0:T(8,128)(2,1)S(1)} all-to-all(bf16[8,2,32,384]{3,2,1,0:T(8,128)(2,1)S(1)} %broadcast_in_dim.104), channel_id=1, replica_groups={{0,2,4,6,8,10,12,14},{16,18,20,22,24,26,28,30},{32,34,36,38,40,42,44,46..., dimensions={0} | all-to-all | bytes 786432 | tf_op jit(solution)/shard_map/all_to_all | solution.py:148
  33.3 4.5 %shard_map.87 = bf16[16,32,384]{2,1,0:T(8,128)(2,1)S(1)} custom-call(s32[4,104]{1,0:T(4,128)S(1)} %get-tuple-element.16.table, f32[8,128]{1,0:T(8,128)S(1)} %broadcast_in_dim.102.fold_ref, bf16[16,32,384]{2,1,0:T(8,128)(2,1)S(1)} %bitcast.68, bf16[96,192,192]{2,1,0:T(8,128)(2,1)S(1)} %shard_map.86.tiles_ref), custom_call_target="tpu_custom_call" | custom-call | flops 226492416 | bytes 7077888 | tf_op jit(solution)/shard_map/pallas_call | solution.py:94
  37.8 11.6 %all_to_all.81 = bf16[8,2,32,384]{3,2,1,0:T(8,128)(2,1)S(1)} all-to-all(bf16[8,2,32,384]{3,2,1,0:T(8,128)(2,1)S(1)} %bitcast.69), channel_id=1, replica_groups={{1,3,5,7,9,11,13,15},{17,19,21,23,25,27,29,31},{33,35,37,39,41,43,45,47..., dimensions={0} | all-to-all | bytes 786432 | tf_op jit(solution)/shard_map/all_to_all | solution.py:148
  49.4 0.1 convert_reduce_fusion.7
  49.5 2.0 collective-permute-start.4
  52.2 4.2 %collective-permute-done.4 = bf16[2,32,384]{2,1,0:T(8,128)(2,1)S(1)} collective-permute-done((bf16[2,32,384]{2,1,0:T(8,128)(2,1)S(1)}, bf16[2,32,384]{2,1,0:T(8,128)(2,1)S(1)}, u32[]{:S(2)}, u32[]{:S(2)}) %collective-permute-start.4) | collective-permute-done | bytes 49184 | tf_op jit(solution)/shard_map/ppermute | solution.py:151
  56.5 9.9 %all_to_all.82 = bf16[8,2,32,384]{3,2,1,0:T(8,128)(2,1)S(1)} all-to-all(bf16[8,2,32,384]{3,2,1,0:T(8,128)(2,1)S(1)} %broadcast_in_dim.105), channel_id=1, replica_groups={{1,3,5,7,9,11,13,15},{17,19,21,23,25,27,29,31},{33,35,37,39,41,43,45,47..., dimensions={0} | all-to-all | bytes 786432 | tf_op jit(solution)/shard_map/all_to_all | solution.py:148
  66.4 3.5 %shard_map.88 = bf16[16,32,384]{2,1,0:T(8,128)(2,1)S(1)} custom-call(s32[4,104]{1,0:T(4,128)S(1)} %get-tuple-element.14.table, f32[8,128]{1,0:T(8,128)S(1)} %broadcast_in_dim.103.fold_ref, bf16[16,32,384]{2,1,0:T(8,128)(2,1)S(1)} %bitcast.70, bf16[96,192,192]{2,1,0:T(8,128)(2,1)S(1)} %shard_map.86.tiles_ref), custom_call_target="tpu_custom_call" | custom-call | flops 226492416 | bytes 7077888 | tf_op jit(solution)/shard_map/pallas_call | solution.py:94
  69.9 12.5 %all_to_all.83 = bf16[8,2,32,384]{3,2,1,0:T(8,128)(2,1)S(1)} all-to-all(bf16[8,2,32,384]{3,2,1,0:T(8,128)(2,1)S(1)} %bitcast.71), channel_id=1, replica_groups={{0,2,4,6,8,10,12,14},{16,18,20,22,24,26,28,30},{32,34,36,38,40,42,44,46..., dimensions={0} | all-to-all | bytes 786432 | tf_op jit(solution)/shard_map/all_to_all | solution.py:148
  82.4 5.9 %collective-permute-start.5 = (bf16[2,32,384]{2,1,0:T(8,128)(2,1)S(1)}, bf16[2,32,384]{2,1,0:T(8,128)(2,1)S(1)}, u32[]{:S(2)}, u32[]{:S(2)}) collective-permute-start(bf16[2,32,384]{2,1,0:T(8,128)(2,1)S(1)} %convert_element_type.112), channel_id=1, source_target_pairs={{0,81},{81,0},{2,113},{113,2},{4,17},{17,4},{6,49},{49,6},{8,65},{... | collective-permute-start | bytes 147464 | tf_op jit(solution)/shard_map/ppermute | solution.py:151
  88.4 1.9 collective-permute-done.5
  90.3 12.7 %all_to_all.84 = bf16[8,2,32,384]{3,2,1,0:T(8,128)(2,1)S(1)} all-to-all(bf16[8,2,32,384]{3,2,1,0:T(8,128)(2,1)S(1)} %broadcast_in_dim.106), channel_id=1, replica_groups={{0,2,4,6,8,10,12,14},{16,18,20,22,24,26,28,30},{32,34,36,38,40,42,44,46..., dimensions={0} | all-to-all | bytes 786432 | tf_op jit(solution)/shard_map/all_to_all | solution.py:148
  103.0 4.5 %shard_map.89 = bf16[16,32,384]{2,1,0:T(8,128)(2,1)S(1)} custom-call(s32[4,104]{1,0:T(4,128)S(1)} %get-tuple-element.16.table, f32[8,128]{1,0:T(8,128)S(1)} %broadcast_in_dim.102.fold_ref, bf16[16,32,384]{2,1,0:T(8,128)(2,1)S(1)} %bitcast.72, bf16[96,192,192]{2,1,0:T(8,128)(2,1)S(1)} %shard_map.86.tiles_ref), custom_call_target="tpu_custom_call" | custom-call | flops 226492416 | bytes 7077888 | tf_op jit(solution)/shard_map/pallas_call | solution.py:94
  107.4 9.5 %all_to_all.85 = bf16[8,2,32,384]{3,2,1,0:T(8,128)(2,1)S(1)} all-to-all(bf16[8,2,32,384]{3,2,1,0:T(8,128)(2,1)S(1)} %bitcast.73), channel_id=1, replica_groups={{1,3,5,7,9,11,13,15},{17,19,21,23,25,27,29,31},{33,35,37,39,41,43,45,47..., dimensions={0} | all-to-all | bytes 786432 | tf_op jit(solution)/shard_map/all_to_all | solution.py:148
  117.0 5.0 %collective-permute-start.6 = (bf16[2,32,384]{2,1,0:T(8,128)(2,1)S(1)}, bf16[2,32,384]{2,1,0:T(8,128)(2,1)S(1)}, u32[]{:S(2)}, u32[]{:S(2)}) collective-permute-start(bf16[2,32,384]{2,1,0:T(8,128)(2,1)S(1)} %convert_element_type.116), channel_id=1, source_target_pairs={{1,80},{80,1},{3,112},{112,3},{5,16},{16,5},{7,48},{48,7},{9,64},{... | collective-permute-start | bytes 147464 | tf_op jit(solution)/shard_map/ppermute | solution.py:151
  122.0 2.1 collective-permute-done.6
  124.2 11.1 %all_to_all.86 = bf16[8,2,32,384]{3,2,1,0:T(8,128)(2,1)S(1)} all-to-all(bf16[8,2,32,384]{3,2,1,0:T(8,128)(2,1)S(1)} %broadcast_in_dim.107), channel_id=1, replica_groups={{1,3,5,7,9,11,13,15},{17,19,21,23,25,27,29,31},{33,35,37,39,41,43,45,47..., dimensions={0} | all-to-all | bytes 786432 | tf_op jit(solution)/shard_map/all_to_all | solution.py:148
  135.3 3.5 %shard_map.90 = bf16[16,32,384]{2,1,0:T(8,128)(2,1)S(1)} custom-call(s32[4,104]{1,0:T(4,128)S(1)} %get-tuple-element.14.table, f32[8,128]{1,0:T(8,128)S(1)} %broadcast_in_dim.103.fold_ref, bf16[16,32,384]{2,1,0:T(8,128)(2,1)S(1)} %bitcast.74, bf16[96,192,192]{2,1,0:T(8,128)(2,1)S(1)} %shard_map.86.tiles_ref), custom_call_target="tpu_custom_call" | custom-call | flops 226492416 | bytes 7077888 | tf_op jit(solution)/shard_map/pallas_call | solution.py:94
  138.8 11.5 %all_to_all.87 = bf16[8,2,32,384]{3,2,1,0:T(8,128)(2,1)S(1)} all-to-all(bf16[8,2,32,384]{3,2,1,0:T(8,128)(2,1)S(1)} %bitcast.75), channel_id=1, replica_groups={{0,2,4,6,8,10,12,14},{16,18,20,22,24,26,28,30},{32,34,36,38,40,42,44,46..., dimensions={0} | all-to-all | bytes 786432 | tf_op jit(solution)/shard_map/all_to_all | solution.py:148
  150.3 9.5 %collective-permute-start.7 = (bf16[2,32,384]{2,1,0:T(8,128)(2,1)S(1)}, bf16[2,32,384]{2,1,0:T(8,128)(2,1)S(1)}, u32[]{:S(2)}, u32[]{:S(2)}) collective-permute-start(bf16[2,32,384]{2,1,0:T(8,128)(2,1)S(1)} %convert_element_type.120), channel_id=1, source_target_pairs={{0,81},{81,0},{2,113},{113,2},{4,17},{17,4},{6,49},{49,6},{8,65},{... | collective-permute-start | bytes 147464 | tf_op jit(solution)/shard_map/ppermute | solution.py:151
  159.8 1.9 collective-permute-done.7
  161.7 12.5 %all_to_all.88 = bf16[8,2,32,384]{3,2,1,0:T(8,128)(2,1)S(1)} all-to-all(bf16[8,2,32,384]{3,2,1,0:T(8,128)(2,1)S(1)} %broadcast_in_dim.108), channel_id=1, replica_groups={{0,2,4,6,8,10,12,14},{16,18,20,22,24,26,28,30},{32,34,36,38,40,42,44,46..., dimensions={0} | all-to-all | bytes 786432 | tf_op jit(solution)/shard_map/all_to_all | solution.py:148
  174.3 4.5 %shard_map.91 = bf16[16,32,384]{2,1,0:T(8,128)(2,1)S(1)} custom-call(s32[4,104]{1,0:T(4,128)S(1)} %get-tuple-element.16.table, f32[8,128]{1,0:T(8,128)S(1)} %broadcast_in_dim.102.fold_ref, bf16[16,32,384]{2,1,0:T(8,128)(2,1)S(1)} %bitcast.76, bf16[96,192,192]{2,1,0:T(8,128)(2,1)S(1)} %shard_map.86.tiles_ref), custom_call_target="tpu_custom_call" | custom-call | flops 226492416 | bytes 7077888 | tf_op jit(solution)/shard_map/pallas_call | solution.py:94
  178.7 9.4 %all_to_all.89 = bf16[8,2,32,384]{3,2,1,0:T(8,128)(2,1)S(1)} all-to-all(bf16[8,2,32,384]{3,2,1,0:T(8,128)(2,1)S(1)} %bitcast.77), channel_id=1, replica_groups={{1,3,5,7,9,11,13,15},{17,19,21,23,25,27,29,31},{33,35,37,39,41,43,45,47..., dimensions={0} | all-to-all | bytes 786432 | tf_op jit(solution)/shard_map/all_to_all | solution.py:148
  188.2 5.9 %collective-permute-start.8 = (bf16[2,32,384]{2,1,0:T(8,128)(2,1)S(1)}, bf16[2,32,384]{2,1,0:T(8,128)(2,1)S(1)}, u32[]{:S(2)}, u32[]{:S(2)}) collective-permute-start(bf16[2,32,384]{2,1,0:T(8,128)(2,1)S(1)} %convert_element_type.124), channel_id=1, source_target_pairs={{1,80},{80,1},{3,112},{112,3},{5,16},{16,5},{7,48},{48,7},{9,64},{... | collective-permute-start | bytes 147464 | tf_op jit(solution)/shard_map/ppermute | solution.py:151
  194.1 2.2 collective-permute-done.8
  196.3 9.7 %all_to_all.90 = bf16[8,2,32,384]{3,2,1,0:T(8,128)(2,1)S(1)} all-to-all(bf16[8,2,32,384]{3,2,1,0:T(8,128)(2,1)S(1)} %broadcast_in_dim.109), channel_id=1, replica_groups={{1,3,5,7,9,11,13,15},{17,19,21,23,25,27,29,31},{33,35,37,39,41,43,45,47..., dimensions={0} | all-to-all | bytes 786432 | tf_op jit(solution)/shard_map/all_to_all | solution.py:148
  206.1 3.5 %shard_map.92 = bf16[16,32,384]{2,1,0:T(8,128)(2,1)S(1)} custom-call(s32[4,104]{1,0:T(4,128)S(1)} %get-tuple-element.14.table, f32[8,128]{1,0:T(8,128)S(1)} %broadcast_in_dim.103.fold_ref, bf16[16,32,384]{2,1,0:T(8,128)(2,1)S(1)} %bitcast.78, bf16[96,192,192]{2,1,0:T(8,128)(2,1)S(1)} %shard_map.86.tiles_ref), custom_call_target="tpu_custom_call" | custom-call | flops 226492416 | bytes 7077888 | tf_op jit(solution)/shard_map/pallas_call | solution.py:94
  209.6 15.0 %all_to_all.91 = bf16[8,2,32,384]{3,2,1,0:T(8,128)(2,1)S(1)} all-to-all(bf16[8,2,32,384]{3,2,1,0:T(8,128)(2,1)S(1)} %bitcast.79), channel_id=1, replica_groups={{0,2,4,6,8,10,12,14},{16,18,20,22,24,26,28,30},{32,34,36,38,40,42,44,46..., dimensions={0} | all-to-all | bytes 786432 | tf_op jit(solution)/shard_map/all_to_all | solution.py:148
  224.6 0.1 convert_reduce_fusion.2
  224.6 7.1 %collective-permute-start.9 = (bf16[2,32,384]{2,1,0:T(8,128)(2,1)S(1)}, bf16[2,32,384]{2,1,0:T(8,128)(2,1)S(1)}, u32[]{:S(2)}, u32[]{:S(2)}) collective-permute-start(bf16[2,32,384]{2,1,0:T(8,128)(2,1)S(1)} %convert_element_type.128), channel_id=1, source_target_pairs={{0,81},{81,0},{2,113},{113,2},{4,17},{17,4},{6,49},{49,6},{8,65},{... | collective-permute-start | bytes 147464 | tf_op jit(solution)/shard_map/ppermute | solution.py:151
  231.7 1.9 collective-permute-done.9
  233.7 11.6 %all_to_all.92 = bf16[8,2,32,384]{3,2,1,0:T(8,128)(2,1)S(1)} all-to-all(bf16[8,2,32,384]{3,2,1,0:T(8,128)(2,1)S(1)} %broadcast_in_dim.110), channel_id=1, replica_groups={{0,2,4,6,8,10,12,14},{16,18,20,22,24,26,28,30},{32,34,36,38,40,42,44,46..., dimensions={0} | all-to-all | bytes 786432 | tf_op jit(solution)/shard_map/all_to_all | solution.py:148
  245.3 4.5 %shard_map.93 = bf16[16,32,384]{2,1,0:T(8,128)(2,1)S(1)} custom-call(s32[4,104]{1,0:T(4,128)S(1)} %get-tuple-element.16.table, f32[8,128]{1,0:T(8,128)S(1)} %broadcast_in_dim.102.fold_ref, bf16[16,32,384]{2,1,0:T(8,128)(2,1)S(1)} %bitcast.66, bf16[96,192,192]{2,1,0:T(8,128)(2,1)S(1)} %shard_map.86.tiles_ref), custom_call_target="tpu_custom_call" | custom-call | flops 226492416 | bytes 7077888 | tf_op jit(solution)/shard_map/pallas_call | solution.py:94
  249.8 10.8 %all_to_all.93 = bf16[8,2,32,384]{3,2,1,0:T(8,128)(2,1)S(1)} all-to-all(bf16[8,2,32,384]{3,2,1,0:T(8,128)(2,1)S(1)} %bitcast.67), channel_id=1, replica_groups={{1,3,5,7,9,11,13,15},{17,19,21,23,25,27,29,31},{33,35,37,39,41,43,45,47..., dimensions={0} | all-to-all | bytes 786432 | tf_op jit(solution)/shard_map/all_to_all | solution.py:148
  260.6 5.6 %collective-permute-start.10 = (bf16[2,32,384]{2,1,0:T(8,128)(2,1)S(1)}, bf16[2,32,384]{2,1,0:T(8,128)(2,1)S(1)}, u32[]{:S(2)}, u32[]{:S(2)}) collective-permute-start(bf16[2,32,384]{2,1,0:T(8,128)(2,1)S(1)} %convert_element_type.132), channel_id=1, source_target_pairs={{1,80},{80,1},{3,112},{112,3},{5,16},{16,5},{7,48},{48,7},{9,64},{... | collective-permute-start | bytes 147464 | tf_op jit(solution)/shard_map/ppermute | solution.py:151
  266.2 2.2 collective-permute-done.10
  268.5 9.6 %all_to_all.94 = bf16[8,2,32,384]{3,2,1,0:T(8,128)(2,1)S(1)} all-to-all(bf16[8,2,32,384]{3,2,1,0:T(8,128)(2,1)S(1)} %broadcast_in_dim.111), channel_id=1, replica_groups={{1,3,5,7,9,11,13,15},{17,19,21,23,25,27,29,31},{33,35,37,39,41,43,45,47..., dimensions={0} | all-to-all | bytes 786432 | tf_op jit(solution)/shard_map/all_to_all | solution.py:148
  278.1 3.5 %shard_map.94 = bf16[16,32,384]{2,1,0:T(8,128)(2,1)S(1)} custom-call(s32[4,104]{1,0:T(4,128)S(1)} %get-tuple-element.14.table, f32[8,128]{1,0:T(8,128)S(1)} %broadcast_in_dim.103.fold_ref, bf16[16,32,384]{2,1,0:T(8,128)(2,1)S(1)} %bitcast.64, bf16[96,192,192]{2,1,0:T(8,128)(2,1)S(1)} %shard_map.86.tiles_ref), custom_call_target="tpu_custom_call" | custom-call | flops 226492416 | bytes 7077888 | tf_op jit(solution)/shard_map/pallas_call | solution.py:94
  281.5 14.2 %all_to_all.95 = bf16[8,2,32,384]{3,2,1,0:T(8,128)(2,1)S(1)} all-to-all(bf16[8,2,32,384]{3,2,1,0:T(8,128)(2,1)S(1)} %bitcast.65), channel_id=1, replica_groups={{0,2,4,6,8,10,12,14},{16,18,20,22,24,26,28,30},{32,34,36,38,40,42,44,46..., dimensions={0} | all-to-all | bytes 786432 | tf_op jit(solution)/shard_map/all_to_all | solution.py:148
  295.8 0.1 convert_reduce_fusion
  295.8 6.2 %collective-permute-start.11 = (bf16[2,32,384]{2,1,0:T(8,128)(2,1)S(1)}, bf16[2,32,384]{2,1,0:T(8,128)(2,1)S(1)}, u32[]{:S(2)}, u32[]{:S(2)}) collective-permute-start(bf16[2,32,384]{2,1,0:T(8,128)(2,1)S(1)} %convert_element_type.136), channel_id=1, source_target_pairs={{0,81},{81,0},{2,113},{113,2},{4,17},{17,4},{6,49},{49,6},{8,65},{... | collective-permute-start | bytes 147464 | tf_op jit(solution)/shard_map/ppermute | solution.py:151
  302.0 2.4 collective-permute-done.11
  304.5 2.3 collective-permute-start.12
  306.8 0.9 collective-permute-done.12
  307.7 0.6 fusion
  (42 shorter events, 1.0 us)
Async XLA Ops:
  0.6 2.2 collective-permute-start
  2.7 1.2 collective-permute-start.1
  3.9 10.4 %collective-permute-start.3 = (bf16[48,192,192]{2,1,0:T(8,128)(2,1)}, bf16[48,192,192]{2,1,0:T(8,128)(2,1)}, u32[]{:S(2)}, u32[]{:S(2)}) collective-permute-start(bf16[48,192,192]{2,1,0:T(8,128)(2,1)} %bitcast.62), channel_id=1, source_target_pairs={{0,1},{1,0},{2,3},{3,2},{4,5},{5,4},{6,7},{7,6},{8,9},{9,8},{10,11... | collective-permute-start | bytes 10616840 | tf_op jit(solution)/shard_map/ppermute | solution.py:151
  6.8 12.5 %collective-permute-start.2 = (f32[2,32,384]{2,1,0:T(8,128)S(1)}, f32[2,32,384]{2,1,0:T(8,128)S(1)}, u32[]{:S(2)}, u32[]{:S(2)}) collective-permute-start(f32[2,32,384]{2,1,0:T(8,128)S(1)} %maximum_select_fusion), channel_id=1, source_target_pairs={{1,81},{3,113},{5,17},{7,49},{9,65},{11,97},{13,1},{15,33},{17,99}... | collective-permute-start | bytes 294920 | tf_op jit(solution)/shard_map/ppermute | solution.py:151
  14.3 2.3 copy-start
  49.5 6.9 %collective-permute-start.4 = (bf16[2,32,384]{2,1,0:T(8,128)(2,1)S(1)}, bf16[2,32,384]{2,1,0:T(8,128)(2,1)S(1)}, u32[]{:S(2)}, u32[]{:S(2)}) collective-permute-start(bf16[2,32,384]{2,1,0:T(8,128)(2,1)S(1)} %convert_element_type.108), channel_id=1, source_target_pairs={{1,80},{80,1},{3,112},{112,3},{5,16},{16,5},{7,48},{48,7},{9,64},{... | collective-permute-start | bytes 147464 | tf_op jit(solution)/shard_map/ppermute | solution.py:151
  82.4 7.8 %collective-permute-start.5 = (bf16[2,32,384]{2,1,0:T(8,128)(2,1)S(1)}, bf16[2,32,384]{2,1,0:T(8,128)(2,1)S(1)}, u32[]{:S(2)}, u32[]{:S(2)}) collective-permute-start(bf16[2,32,384]{2,1,0:T(8,128)(2,1)S(1)} %convert_element_type.112), channel_id=1, source_target_pairs={{0,81},{81,0},{2,113},{113,2},{4,17},{17,4},{6,49},{49,6},{8,65},{... | collective-permute-start | bytes 147464 | tf_op jit(solution)/shard_map/ppermute | solution.py:151
  117.0 7.1 %collective-permute-start.6 = (bf16[2,32,384]{2,1,0:T(8,128)(2,1)S(1)}, bf16[2,32,384]{2,1,0:T(8,128)(2,1)S(1)}, u32[]{:S(2)}, u32[]{:S(2)}) collective-permute-start(bf16[2,32,384]{2,1,0:T(8,128)(2,1)S(1)} %convert_element_type.116), channel_id=1, source_target_pairs={{1,80},{80,1},{3,112},{112,3},{5,16},{16,5},{7,48},{48,7},{9,64},{... | collective-permute-start | bytes 147464 | tf_op jit(solution)/shard_map/ppermute | solution.py:151
  150.3 11.4 %collective-permute-start.7 = (bf16[2,32,384]{2,1,0:T(8,128)(2,1)S(1)}, bf16[2,32,384]{2,1,0:T(8,128)(2,1)S(1)}, u32[]{:S(2)}, u32[]{:S(2)}) collective-permute-start(bf16[2,32,384]{2,1,0:T(8,128)(2,1)S(1)} %convert_element_type.120), channel_id=1, source_target_pairs={{0,81},{81,0},{2,113},{113,2},{4,17},{17,4},{6,49},{49,6},{8,65},{... | collective-permute-start | bytes 147464 | tf_op jit(solution)/shard_map/ppermute | solution.py:151
  188.2 8.0 %collective-permute-start.8 = (bf16[2,32,384]{2,1,0:T(8,128)(2,1)S(1)}, bf16[2,32,384]{2,1,0:T(8,128)(2,1)S(1)}, u32[]{:S(2)}, u32[]{:S(2)}) collective-permute-start(bf16[2,32,384]{2,1,0:T(8,128)(2,1)S(1)} %convert_element_type.124), channel_id=1, source_target_pairs={{1,80},{80,1},{3,112},{112,3},{5,16},{16,5},{7,48},{48,7},{9,64},{... | collective-permute-start | bytes 147464 | tf_op jit(solution)/shard_map/ppermute | solution.py:151
  224.6 9.0 %collective-permute-start.9 = (bf16[2,32,384]{2,1,0:T(8,128)(2,1)S(1)}, bf16[2,32,384]{2,1,0:T(8,128)(2,1)S(1)}, u32[]{:S(2)}, u32[]{:S(2)}) collective-permute-start(bf16[2,32,384]{2,1,0:T(8,128)(2,1)S(1)} %convert_element_type.128), channel_id=1, source_target_pairs={{0,81},{81,0},{2,113},{113,2},{4,17},{17,4},{6,49},{49,6},{8,65},{... | collective-permute-start | bytes 147464 | tf_op jit(solution)/shard_map/ppermute | solution.py:151
  260.6 7.8 %collective-permute-start.10 = (bf16[2,32,384]{2,1,0:T(8,128)(2,1)S(1)}, bf16[2,32,384]{2,1,0:T(8,128)(2,1)S(1)}, u32[]{:S(2)}, u32[]{:S(2)}) collective-permute-start(bf16[2,32,384]{2,1,0:T(8,128)(2,1)S(1)} %convert_element_type.132), channel_id=1, source_target_pairs={{1,80},{80,1},{3,112},{112,3},{5,16},{16,5},{7,48},{48,7},{9,64},{... | collective-permute-start | bytes 147464 | tf_op jit(solution)/shard_map/ppermute | solution.py:151
  295.8 8.6 %collective-permute-start.11 = (bf16[2,32,384]{2,1,0:T(8,128)(2,1)S(1)}, bf16[2,32,384]{2,1,0:T(8,128)(2,1)S(1)}, u32[]{:S(2)}, u32[]{:S(2)}) collective-permute-start(bf16[2,32,384]{2,1,0:T(8,128)(2,1)S(1)} %convert_element_type.136), channel_id=1, source_target_pairs={{0,81},{81,0},{2,113},{113,2},{4,17},{17,4},{6,49},{49,6},{8,65},{... | collective-permute-start | bytes 147464 | tf_op jit(solution)/shard_map/ppermute | solution.py:151
  304.5 3.1 %collective-permute-start.12 = (f32[32,384]{1,0:T(8,128)S(1)}, f32[32,384]{1,0:T(8,128)S(1)}, u32[]{:S(2)}, u32[]{:S(2)}) collective-permute-start(f32[32,384]{1,0:T(8,128)S(1)} %fusion.1), channel_id=1, source_target_pairs={{0,1},{1,0},{2,3},{3,2},{4,5},{5,4},{6,7},{7,6},{8,9},{9,8},{10,11... | collective-permute-start | bytes 147464 | tf_op jit(solution)/shard_map/ppermute | solution.py:151

commit v3 on v2

--- a/solution.py
+++ b/solution.py
@@ -6,7 +6,8 @@
 from jax.sharding import PartitionSpec as P
 
 DEG = 8
-GROUP = 8
+GROUP = 24
+REST = 4
 
 
 def keep_kernel(own_ref, other_ref, kept_ref, sems):
@@ -56,19 +57,26 @@
         place(2 * pairs, half, jnp.zeros((vectors, 128), jnp.float32))
 
     def run(contract):
-        @pl.loop(0, table[0, 1])
-        def _(group):
+        def add(start, members):
             sums = [
                 lax.dot_general(
-                    x_wide[table[2, group * GROUP + member], :, :size],
-                    tiles_ref[table[1, group * GROUP + member]],
+                    x_wide[table[2, start + member], :, :size],
+                    tiles_ref[table[1, start + member]],
                     (((1,), (contract,)), ((), ())),
                     preferred_element_type=jnp.float32,
                 )
-                for member in range(GROUP)
+                for member in range(members)
             ]
-            for member in range(GROUP):
-                total[table[3, group * GROUP + member], :, :size] += sums[member]
+            for member in range(members):
+                total[table[3, start + member], :, :size] += sums[member]
+
+        @pl.loop(0, table[0, 1])
+        def _(group):
+            add(group * GROUP, GROUP)
+
+        @pl.loop(0, table[0, 2])
+        def _(group):
+            add(table[0, 1] * GROUP + group * REST, REST)
 
     @pl.when(table[0, 0] == 0)
     def _():
@@ -108,17 +116,13 @@
 
 
 def column_owner(side):
-    def ring(a, b, n):
-        return min((a - b) % n, (b - a) % n)
-
-    half = side // 2
-    owner = []
-    for s in range(side):
-        away = sorted(range(side), key=lambda k: (ring(k % half, s % half, half) + (k // half != s // half), k))
-        near = sorted(range(side), key=lambda q: (ring(q // 2, s // 2, half) + 2 * (q % 2 != s % 2), q))
-        pairing = dict(zip(away, reversed(near)))
-        owner.append([pairing[k] for k in range(side)])
-    return owner
+    ring = side // 2
+
+    def place(s, k):
+        step = (k - s) % ring
+        return 2 * ((s // 2 + ring // 2 - step) % ring) + ((s % 2) ^ (k // ring) ^ (s // ring))
+
+    return [[place(s, k) for k in range(side)] for s in range(side)]
 
 
 def body(start_block, center, half_width, matrix_tiles, tile_row, tile_col, tile_live):
@@ -162,7 +166,7 @@
     ids = jnp.concatenate([ids, ids_there], 1)
     alive = ids[2] > 0
     position = jnp.cumsum(alive.astype(jnp.int32)) - 1
-    places = 2 * slots_here + GROUP
+    places = 2 * slots_here + REST
     hit = (position[None, :] == jnp.arange(places)[:, None]) & alive[None, :]
     count = jnp.sum(alive.astype(jnp.int32))
 
@@ -174,22 +178,23 @@
     rows, cols = pick(ids[0], 4 * side), pick(ids[1], 4 * side)
 
     def table_of(role):
-        head = jnp.pad(jnp.stack([role, (count + GROUP - 1) // GROUP]).astype(jnp.int32), (0, places - 2))
+        rest = (count % GROUP + REST - 1) // REST
+        head = jnp.pad(jnp.stack([role, count // GROUP, rest]).astype(jnp.int32), (0, places - 3))
         first = role == 0
         return jnp.stack([head, slots, jnp.where(first, rows, cols), jnp.where(first, cols, rows)])
 
     center_value, half_value = center[0], half_width[0]
-    folds = [jnp.full((8, 128), jnp.where(diagonal & (core == h), -center_value, 0.0)) for h in range(2)]
+    fold = jnp.full((8, 128), jnp.where(diagonal, -0.5 * center_value, 0.0))
     tables = [table_of(core), table_of(1 - core)]
 
-    start_turned, tiles, tables, folds = lax.optimization_barrier((start_turned, tiles, tables, folds))
+    start_turned, tiles, tables, fold = lax.optimization_barrier((start_turned, tiles, tables, fold))
     current = start_turned
     earlier = current
     for degree in range(DEG):
         lead = degree % 2
         rounded = current.astype(jnp.bfloat16)
         x = exchange(jnp.broadcast_to(rounded[None], (side, *rounded.shape)), gather_groups[lead])
-        partial = products(tables[lead], folds[lead], x.reshape(2 * side, vectors, width), tiles)
+        partial = products(tables[lead], fold, x.reshape(2 * side, vectors, width), tiles)
         parts = exchange(partial.reshape(side, 2, vectors, width), gather_groups[1 - lead])
         share = jnp.sum(parts.astype(jnp.float32), axis=0)
         product = share + send(share.astype(jnp.bfloat16), turns[1 - lead]).astype(jnp.float32)

time: 312 us -> 300 us (0.962)
  Pallas kernels: 34.4 us -> 28.2 us
  blocking collectives: 186 us -> 181 us
    pallas_call x8, Pallas kernels: 31.7 us -> 25.5 us  [products(): pl.pallas_call(products_kernel, out_shape=jax.ShapeDtypeStruct(x.shape, j...]
    all_to_all x16, blocking collectives: 186 us -> 181 us  [exchange(): lax.all_to_all(value, axes, 0, 0, axis_index_groups=groups, tiled=False)]
where the time goes in v3:
time: 300 us; the launch traced here: 299 us
  blocking collectives  181 us (60%)
  starting transfers between devices  57.1 us (19%)
  Pallas kernels  28.2 us (9%)
  waiting for transfers between devices  20.6 us (7%)
  other arithmetic  6.03 us (2%)
  between operations  4 us (1%)
    all_to_all x16, blocking collectives, exchange(): lax.all_to_all(value, axes, 0, 0, axis_index_groups=groups, tiled=False)  181 us
    ppermute x13, starting transfers between devices, send(): return lax.ppermute(value, axes, pairs)  57.1 us
    pallas_call x8, Pallas kernels, products(): pl.pallas_call(products_kernel, out_shape=jax.ShapeDtypeStruct(x.shape, j...  25.5 us
    ppermute x13, waiting for transfers between devices, send(): return lax.ppermute(value, axes, pairs)  20.6 us
  transfers between devices with their start and end apart: 13, of which 10 were waited for; matrix products, arithmetic and copies ran while one was open for 2% of the time, Pallas kernels for 1%

profile of v3, /device:TPU:7, one launch (start us, length us, event | category | flops | bytes accessed | tf_op | source)
XLA Modules:
  0.0 299.2 jit_solution(6885955050327786442)
XLA Ops:
  0.6 0.8 collective-permute-start
  1.4 0.7 broadcast_add_fusion
  2.0 0.7 pad_add_fusion.2
  2.7 0.1 collective-permute-start.1
  2.8 0.9 maximum_select_fusion
  3.7 0.2 collective-permute-done.1
  3.9 0.3 collective-permute-start.3
  4.9 0.7 pad_add_fusion.3
  5.7 0.6 fusion.10
  8.0 5.9 %collective-permute-start.2 = (f32[2,32,384]{2,1,0:T(8,128)S(1)}, f32[2,32,384]{2,1,0:T(8,128)S(1)}, u32[]{:S(2)}, u32[]{:S(2)}) collective-permute-start(f32[2,32,384]{2,1,0:T(8,128)S(1)} %maximum_select_fusion), channel_id=1, source_target_pairs={{1,65},{3,33},{5,1},{7,97},{9,81},{11,49},{13,17},{15,113},{17,115... | collective-permute-start | bytes 294920 | tf_op jit(solution)/shard_map/ppermute | solution.py:155
  13.9 0.1 copy.11
  14.0 0.1 reduce-window.8
  14.2 0.1 add_add_fusion
  14.3 0.1 add_reduce_fusion
  14.4 0.1 select_reduce_fusion.1
  14.5 0.5 broadcast_select_fusion.1
  15.1 2.3 copy-done
  17.5 2.7 shard_map.86.tiles_ref
  20.2 12.9 %all_to_all.80 = bf16[8,2,32,384]{3,2,1,0:T(8,128)(2,1)S(1)} all-to-all(bf16[8,2,32,384]{3,2,1,0:T(8,128)(2,1)S(1)} %broadcast_in_dim.100), channel_id=1, replica_groups={{0,2,4,6,8,10,12,14},{16,18,20,22,24,26,28,30},{32,34,36,38,40,42,44,46..., dimensions={0} | all-to-all | bytes 786432 | tf_op jit(solution)/shard_map/all_to_all | solution.py:152
  33.2 3.7 %shard_map.87 = bf16[16,32,384]{2,1,0:T(8,128)(2,1)S(1)} custom-call(s32[4,100]{1,0:T(4,128)S(1)} %get-tuple-element.15.table, f32[8,128]{1,0:T(8,128)S(1)} %broadcast_in_dim.99.fold_ref, bf16[16,32,384]{2,1,0:T(8,128)(2,1)S(1)} %bitcast.69, bf16[96,192,192]{2,1,0:T(8,128)(2,1)S(1)} %shard_map.86.tiles_ref), custom_call_target="tpu_custom_call" | custom-call | flops 226492416 | bytes 7077888 | tf_op jit(solution)/shard_map/pallas_call | solution.py:102
  36.8 11.6 %all_to_all.81 = bf16[8,2,32,384]{3,2,1,0:T(8,128)(2,1)S(1)} all-to-all(bf16[8,2,32,384]{3,2,1,0:T(8,128)(2,1)S(1)} %bitcast.70), channel_id=1, replica_groups={{1,3,5,7,9,11,13,15},{17,19,21,23,25,27,29,31},{33,35,37,39,41,43,45,47..., dimensions={0} | all-to-all | bytes 786432 | tf_op jit(solution)/shard_map/all_to_all | solution.py:152
  48.4 0.1 convert_reduce_fusion.7
  48.5 1.5 collective-permute-start.4
  50.6 5.7 %collective-permute-done.4 = bf16[2,32,384]{2,1,0:T(8,128)(2,1)S(1)} collective-permute-done((bf16[2,32,384]{2,1,0:T(8,128)(2,1)S(1)}, bf16[2,32,384]{2,1,0:T(8,128)(2,1)S(1)}, u32[]{:S(2)}, u32[]{:S(2)}) %collective-permute-start.4) | collective-permute-done | bytes 49184 | tf_op jit(solution)/shard_map/ppermute | solution.py:155
  56.4 10.0 %all_to_all.82 = bf16[8,2,32,384]{3,2,1,0:T(8,128)(2,1)S(1)} all-to-all(bf16[8,2,32,384]{3,2,1,0:T(8,128)(2,1)S(1)} %broadcast_in_dim.101), channel_id=1, replica_groups={{1,3,5,7,9,11,13,15},{17,19,21,23,25,27,29,31},{33,35,37,39,41,43,45,47..., dimensions={0} | all-to-all | bytes 786432 | tf_op jit(solution)/shard_map/all_to_all | solution.py:152
  66.4 2.7 shard_map.88
  69.1 12.9 %all_to_all.83 = bf16[8,2,32,384]{3,2,1,0:T(8,128)(2,1)S(1)} all-to-all(bf16[8,2,32,384]{3,2,1,0:T(8,128)(2,1)S(1)} %bitcast.72), channel_id=1, replica_groups={{0,2,4,6,8,10,12,14},{16,18,20,22,24,26,28,30},{32,34,36,38,40,42,44,46..., dimensions={0} | all-to-all | bytes 786432 | tf_op jit(solution)/shard_map/all_to_all | solution.py:152
  82.0 0.1 convert_reduce_fusion.6
  82.1 5.6 %collective-permute-start.5 = (bf16[2,32,384]{2,1,0:T(8,128)(2,1)S(1)}, bf16[2,32,384]{2,1,0:T(8,128)(2,1)S(1)}, u32[]{:S(2)}, u32[]{:S(2)}) collective-permute-start(bf16[2,32,384]{2,1,0:T(8,128)(2,1)S(1)} %convert_element_type.112), channel_id=1, source_target_pairs={{0,65},{65,0},{2,33},{33,2},{4,1},{1,4},{6,97},{97,6},{8,81},{81,8... | collective-permute-start | bytes 147464 | tf_op jit(solution)/shard_map/ppermute | solution.py:155
  87.7 1.8 collective-permute-done.5
  89.6 10.7 %all_to_all.84 = bf16[8,2,32,384]{3,2,1,0:T(8,128)(2,1)S(1)} all-to-all(bf16[8,2,32,384]{3,2,1,0:T(8,128)(2,1)S(1)} %broadcast_in_dim.102), channel_id=1, replica_groups={{0,2,4,6,8,10,12,14},{16,18,20,22,24,26,28,30},{32,34,36,38,40,42,44,46..., dimensions={0} | all-to-all | bytes 786432 | tf_op jit(solution)/shard_map/all_to_all | solution.py:152
  100.2 3.7 %shard_map.89 = bf16[16,32,384]{2,1,0:T(8,128)(2,1)S(1)} custom-call(s32[4,100]{1,0:T(4,128)S(1)} %get-tuple-element.15.table, f32[8,128]{1,0:T(8,128)S(1)} %broadcast_in_dim.99.fold_ref, bf16[16,32,384]{2,1,0:T(8,128)(2,1)S(1)} %bitcast.73, bf16[96,192,192]{2,1,0:T(8,128)(2,1)S(1)} %shard_map.86.tiles_ref), custom_call_target="tpu_custom_call" | custom-call | flops 226492416 | bytes 7077888 | tf_op jit(solution)/shard_map/pallas_call | solution.py:102
  103.9 9.4 %all_to_all.85 = bf16[8,2,32,384]{3,2,1,0:T(8,128)(2,1)S(1)} all-to-all(bf16[8,2,32,384]{3,2,1,0:T(8,128)(2,1)S(1)} %bitcast.74), channel_id=1, replica_groups={{1,3,5,7,9,11,13,15},{17,19,21,23,25,27,29,31},{33,35,37,39,41,43,45,47..., dimensions={0} | all-to-all | bytes 786432 | tf_op jit(solution)/shard_map/all_to_all | solution.py:152
  113.4 7.4 %collective-permute-start.6 = (bf16[2,32,384]{2,1,0:T(8,128)(2,1)S(1)}, bf16[2,32,384]{2,1,0:T(8,128)(2,1)S(1)}, u32[]{:S(2)}, u32[]{:S(2)}) collective-permute-start(bf16[2,32,384]{2,1,0:T(8,128)(2,1)S(1)} %convert_element_type.116), channel_id=1, source_target_pairs={{1,64},{64,1},{3,32},{32,3},{5,0},{0,5},{7,96},{96,7},{9,80},{80,9... | collective-permute-start | bytes 147464 | tf_op jit(solution)/shard_map/ppermute | solution.py:155
  120.8 2.3 collective-permute-done.6
  123.2 8.5 %all_to_all.86 = bf16[8,2,32,384]{3,2,1,0:T(8,128)(2,1)S(1)} all-to-all(bf16[8,2,32,384]{3,2,1,0:T(8,128)(2,1)S(1)} %broadcast_in_dim.103), channel_id=1, replica_groups={{1,3,5,7,9,11,13,15},{17,19,21,23,25,27,29,31},{33,35,37,39,41,43,45,47..., dimensions={0} | all-to-all | bytes 786432 | tf_op jit(solution)/shard_map/all_to_all | solution.py:152
  131.8 2.7 shard_map.90
  134.5 15.4 %all_to_all.87 = bf16[8,2,32,384]{3,2,1,0:T(8,128)(2,1)S(1)} all-to-all(bf16[8,2,32,384]{3,2,1,0:T(8,128)(2,1)S(1)} %bitcast.76), channel_id=1, replica_groups={{0,2,4,6,8,10,12,14},{16,18,20,22,24,26,28,30},{32,34,36,38,40,42,44,46..., dimensions={0} | all-to-all | bytes 786432 | tf_op jit(solution)/shard_map/all_to_all | solution.py:152
  149.9 5.6 %collective-permute-start.7 = (bf16[2,32,384]{2,1,0:T(8,128)(2,1)S(1)}, bf16[2,32,384]{2,1,0:T(8,128)(2,1)S(1)}, u32[]{:S(2)}, u32[]{:S(2)}) collective-permute-start(bf16[2,32,384]{2,1,0:T(8,128)(2,1)S(1)} %convert_element_type.120), channel_id=1, source_target_pairs={{0,65},{65,0},{2,33},{33,2},{4,1},{1,4},{6,97},{97,6},{8,81},{81,8... | collective-permute-start | bytes 147464 | tf_op jit(solution)/shard_map/ppermute | solution.py:155
  155.6 1.8 collective-permute-done.7
  157.4 10.7 %all_to_all.88 = bf16[8,2,32,384]{3,2,1,0:T(8,128)(2,1)S(1)} all-to-all(bf16[8,2,32,384]{3,2,1,0:T(8,128)(2,1)S(1)} %broadcast_in_dim.104), channel_id=1, replica_groups={{0,2,4,6,8,10,12,14},{16,18,20,22,24,26,28,30},{32,34,36,38,40,42,44,46..., dimensions={0} | all-to-all | bytes 786432 | tf_op jit(solution)/shard_map/all_to_all | solution.py:152
  168.1 3.7 %shard_map.91 = bf16[16,32,384]{2,1,0:T(8,128)(2,1)S(1)} custom-call(s32[4,100]{1,0:T(4,128)S(1)} %get-tuple-element.15.table, f32[8,128]{1,0:T(8,128)S(1)} %broadcast_in_dim.99.fold_ref, bf16[16,32,384]{2,1,0:T(8,128)(2,1)S(1)} %bitcast.77, bf16[96,192,192]{2,1,0:T(8,128)(2,1)S(1)} %shard_map.86.tiles_ref), custom_call_target="tpu_custom_call" | custom-call | flops 226492416 | bytes 7077888 | tf_op jit(solution)/shard_map/pallas_call | solution.py:102
  171.8 9.7 %all_to_all.89 = bf16[8,2,32,384]{3,2,1,0:T(8,128)(2,1)S(1)} all-to-all(bf16[8,2,32,384]{3,2,1,0:T(8,128)(2,1)S(1)} %bitcast.78), channel_id=1, replica_groups={{1,3,5,7,9,11,13,15},{17,19,21,23,25,27,29,31},{33,35,37,39,41,43,45,47..., dimensions={0} | all-to-all | bytes 786432 | tf_op jit(solution)/shard_map/all_to_all | solution.py:152
  181.5 7.3 %collective-permute-start.8 = (bf16[2,32,384]{2,1,0:T(8,128)(2,1)S(1)}, bf16[2,32,384]{2,1,0:T(8,128)(2,1)S(1)}, u32[]{:S(2)}, u32[]{:S(2)}) collective-permute-start(bf16[2,32,384]{2,1,0:T(8,128)(2,1)S(1)} %convert_element_type.124), channel_id=1, source_target_pairs={{1,64},{64,1},{3,32},{32,3},{5,0},{0,5},{7,96},{96,7},{9,80},{80,9... | collective-permute-start | bytes 147464 | tf_op jit(solution)/shard_map/ppermute | solution.py:155
  188.8 2.1 collective-permute-done.8
  191.0 8.7 %all_to_all.90 = bf16[8,2,32,384]{3,2,1,0:T(8,128)(2,1)S(1)} all-to-all(bf16[8,2,32,384]{3,2,1,0:T(8,128)(2,1)S(1)} %broadcast_in_dim.105), channel_id=1, replica_groups={{1,3,5,7,9,11,13,15},{17,19,21,23,25,27,29,31},{33,35,37,39,41,43,45,47..., dimensions={0} | all-to-all | bytes 786432 | tf_op jit(solution)/shard_map/all_to_all | solution.py:152
  199.7 2.7 shard_map.92
  202.5 16.0 %all_to_all.91 = bf16[8,2,32,384]{3,2,1,0:T(8,128)(2,1)S(1)} all-to-all(bf16[8,2,32,384]{3,2,1,0:T(8,128)(2,1)S(1)} %bitcast.80), channel_id=1, replica_groups={{0,2,4,6,8,10,12,14},{16,18,20,22,24,26,28,30},{32,34,36,38,40,42,44,46..., dimensions={0} | all-to-all | bytes 786432 | tf_op jit(solution)/shard_map/all_to_all | solution.py:152
  218.6 5.4 %collective-permute-start.9 = (bf16[2,32,384]{2,1,0:T(8,128)(2,1)S(1)}, bf16[2,32,384]{2,1,0:T(8,128)(2,1)S(1)}, u32[]{:S(2)}, u32[]{:S(2)}) collective-permute-start(bf16[2,32,384]{2,1,0:T(8,128)(2,1)S(1)} %convert_element_type.128), channel_id=1, source_target_pairs={{0,65},{65,0},{2,33},{33,2},{4,1},{1,4},{6,97},{97,6},{8,81},{81,8... | collective-permute-start | bytes 147464 | tf_op jit(solution)/shard_map/ppermute | solution.py:155
  223.9 1.8 collective-permute-done.9
  225.9 10.7 %all_to_all.92 = bf16[8,2,32,384]{3,2,1,0:T(8,128)(2,1)S(1)} all-to-all(bf16[8,2,32,384]{3,2,1,0:T(8,128)(2,1)S(1)} %broadcast_in_dim.106), channel_id=1, replica_groups={{0,2,4,6,8,10,12,14},{16,18,20,22,24,26,28,30},{32,34,36,38,40,42,44,46..., dimensions={0} | all-to-all | bytes 786432 | tf_op jit(solution)/shard_map/all_to_all | solution.py:152
  236.5 3.7 %shard_map.93 = bf16[16,32,384]{2,1,0:T(8,128)(2,1)S(1)} custom-call(s32[4,100]{1,0:T(4,128)S(1)} %get-tuple-element.15.table, f32[8,128]{1,0:T(8,128)S(1)} %broadcast_in_dim.99.fold_ref, bf16[16,32,384]{2,1,0:T(8,128)(2,1)S(1)} %bitcast.67, bf16[96,192,192]{2,1,0:T(8,128)(2,1)S(1)} %shard_map.86.tiles_ref), custom_call_target="tpu_custom_call" | custom-call | flops 226492416 | bytes 7077888 | tf_op jit(solution)/shard_map/pallas_call | solution.py:102
  240.2 9.7 %all_to_all.93 = bf16[8,2,32,384]{3,2,1,0:T(8,128)(2,1)S(1)} all-to-all(bf16[8,2,32,384]{3,2,1,0:T(8,128)(2,1)S(1)} %bitcast.68), channel_id=1, replica_groups={{1,3,5,7,9,11,13,15},{17,19,21,23,25,27,29,31},{33,35,37,39,41,43,45,47..., dimensions={0} | all-to-all | bytes 786432 | tf_op jit(solution)/shard_map/all_to_all | solution.py:152
  250.0 7.4 %collective-permute-start.10 = (bf16[2,32,384]{2,1,0:T(8,128)(2,1)S(1)}, bf16[2,32,384]{2,1,0:T(8,128)(2,1)S(1)}, u32[]{:S(2)}, u32[]{:S(2)}) collective-permute-start(bf16[2,32,384]{2,1,0:T(8,128)(2,1)S(1)} %convert_element_type.132), channel_id=1, source_target_pairs={{1,64},{64,1},{3,32},{32,3},{5,0},{0,5},{7,96},{96,7},{9,80},{80,9... | collective-permute-start | bytes 147464 | tf_op jit(solution)/shard_map/ppermute | solution.py:155
  257.3 2.1 collective-permute-done.10
  259.6 8.7 %all_to_all.94 = bf16[8,2,32,384]{3,2,1,0:T(8,128)(2,1)S(1)} all-to-all(bf16[8,2,32,384]{3,2,1,0:T(8,128)(2,1)S(1)} %broadcast_in_dim.107), channel_id=1, replica_groups={{1,3,5,7,9,11,13,15},{17,19,21,23,25,27,29,31},{33,35,37,39,41,43,45,47..., dimensions={0} | all-to-all | bytes 786432 | tf_op jit(solution)/shard_map/all_to_all | solution.py:152
  268.3 2.7 shard_map.94
  271.0 14.9 %all_to_all.95 = bf16[8,2,32,384]{3,2,1,0:T(8,128)(2,1)S(1)} all-to-all(bf16[8,2,32,384]{3,2,1,0:T(8,128)(2,1)S(1)} %bitcast.66), channel_id=1, replica_groups={{0,2,4,6,8,10,12,14},{16,18,20,22,24,26,28,30},{32,34,36,38,40,42,44,46..., dimensions={0} | all-to-all | bytes 786432 | tf_op jit(solution)/shard_map/all_to_all | solution.py:152
  285.9 0.1 convert_reduce_fusion
  286.0 6.6 %collective-permute-start.11 = (bf16[2,32,384]{2,1,0:T(8,128)(2,1)S(1)}, bf16[2,32,384]{2,1,0:T(8,128)(2,1)S(1)}, u32[]{:S(2)}, u32[]{:S(2)}) collective-permute-start(bf16[2,32,384]{2,1,0:T(8,128)(2,1)S(1)} %convert_element_type.136), channel_id=1, source_target_pairs={{0,65},{65,0},{2,33},{33,2},{4,1},{1,4},{6,97},{97,6},{8,81},{81,8... | collective-permute-start | bytes 147464 | tf_op jit(solution)/shard_map/ppermute | solution.py:155
  292.6 1.8 collective-permute-done.11
  294.4 3.2 %collective-permute-start.12 = (f32[32,384]{1,0:T(8,128)S(1)}, f32[32,384]{1,0:T(8,128)S(1)}, u32[]{:S(2)}, u32[]{:S(2)}) collective-permute-start(f32[32,384]{1,0:T(8,128)S(1)} %fusion.1), channel_id=1, source_target_pairs={{0,1},{1,0},{2,3},{3,2},{4,5},{5,4},{6,7},{7,6},{8,9},{9,8},{10,11... | collective-permute-start | bytes 147464 | tf_op jit(solution)/shard_map/ppermute | solution.py:155
  297.7 0.9 collective-permute-done.12
  298.5 0.6 fusion
  (41 shorter events, 1.0 us)
Async XLA Ops:
  0.6 2.2 collective-permute-start
  2.7 1.2 collective-permute-start.1
  3.9 11.2 %collective-permute-start.3 = (bf16[48,192,192]{2,1,0:T(8,128)(2,1)}, bf16[48,192,192]{2,1,0:T(8,128)(2,1)}, u32[]{:S(2)}, u32[]{:S(2)}) collective-permute-start(bf16[48,192,192]{2,1,0:T(8,128)(2,1)} %bitcast.63), channel_id=1, source_target_pairs={{0,1},{1,0},{2,3},{3,2},{4,5},{5,4},{6,7},{7,6},{8,9},{9,8},{10,11... | collective-permute-start | bytes 10616840 | tf_op jit(solution)/shard_map/ppermute | solution.py:155
  8.0 12.2 %collective-permute-start.2 = (f32[2,32,384]{2,1,0:T(8,128)S(1)}, f32[2,32,384]{2,1,0:T(8,128)S(1)}, u32[]{:S(2)}, u32[]{:S(2)}) collective-permute-start(f32[2,32,384]{2,1,0:T(8,128)S(1)} %maximum_select_fusion), channel_id=1, source_target_pairs={{1,65},{3,33},{5,1},{7,97},{9,81},{11,49},{13,17},{15,113},{17,115... | collective-permute-start | bytes 294920 | tf_op jit(solution)/shard_map/ppermute | solution.py:155
  15.1 2.3 copy-start
  48.5 7.8 %collective-permute-start.4 = (bf16[2,32,384]{2,1,0:T(8,128)(2,1)S(1)}, bf16[2,32,384]{2,1,0:T(8,128)(2,1)S(1)}, u32[]{:S(2)}, u32[]{:S(2)}) collective-permute-start(bf16[2,32,384]{2,1,0:T(8,128)(2,1)S(1)} %convert_element_type.108), channel_id=1, source_target_pairs={{1,64},{64,1},{3,32},{32,3},{5,0},{0,5},{7,96},{96,7},{9,80},{80,9... | collective-permute-start | bytes 147464 | tf_op jit(solution)/shard_map/ppermute | solution.py:155
  82.1 7.4 %collective-permute-start.5 = (bf16[2,32,384]{2,1,0:T(8,128)(2,1)S(1)}, bf16[2,32,384]{2,1,0:T(8,128)(2,1)S(1)}, u32[]{:S(2)}, u32[]{:S(2)}) collective-permute-start(bf16[2,32,384]{2,1,0:T(8,128)(2,1)S(1)} %convert_element_type.112), channel_id=1, source_target_pairs={{0,65},{65,0},{2,33},{33,2},{4,1},{1,4},{6,97},{97,6},{8,81},{81,8... | collective-permute-start | bytes 147464 | tf_op jit(solution)/shard_map/ppermute | solution.py:155
  113.4 9.7 %collective-permute-start.6 = (bf16[2,32,384]{2,1,0:T(8,128)(2,1)S(1)}, bf16[2,32,384]{2,1,0:T(8,128)(2,1)S(1)}, u32[]{:S(2)}, u32[]{:S(2)}) collective-permute-start(bf16[2,32,384]{2,1,0:T(8,128)(2,1)S(1)} %convert_element_type.116), channel_id=1, source_target_pairs={{1,64},{64,1},{3,32},{32,3},{5,0},{0,5},{7,96},{96,7},{9,80},{80,9... | collective-permute-start | bytes 147464 | tf_op jit(solution)/shard_map/ppermute | solution.py:155
  149.9 7.4 %collective-permute-start.7 = (bf16[2,32,384]{2,1,0:T(8,128)(2,1)S(1)}, bf16[2,32,384]{2,1,0:T(8,128)(2,1)S(1)}, u32[]{:S(2)}, u32[]{:S(2)}) collective-permute-start(bf16[2,32,384]{2,1,0:T(8,128)(2,1)S(1)} %convert_element_type.120), channel_id=1, source_target_pairs={{0,65},{65,0},{2,33},{33,2},{4,1},{1,4},{6,97},{97,6},{8,81},{81,8... | collective-permute-start | bytes 147464 | tf_op jit(solution)/shard_map/ppermute | solution.py:155
  181.5 9.4 %collective-permute-start.8 = (bf16[2,32,384]{2,1,0:T(8,128)(2,1)S(1)}, bf16[2,32,384]{2,1,0:T(8,128)(2,1)S(1)}, u32[]{:S(2)}, u32[]{:S(2)}) collective-permute-start(bf16[2,32,384]{2,1,0:T(8,128)(2,1)S(1)} %convert_element_type.124), channel_id=1, source_target_pairs={{1,64},{64,1},{3,32},{32,3},{5,0},{0,5},{7,96},{96,7},{9,80},{80,9... | collective-permute-start | bytes 147464 | tf_op jit(solution)/shard_map/ppermute | solution.py:155
  218.6 7.2 %collective-permute-start.9 = (bf16[2,32,384]{2,1,0:T(8,128)(2,1)S(1)}, bf16[2,32,384]{2,1,0:T(8,128)(2,1)S(1)}, u32[]{:S(2)}, u32[]{:S(2)}) collective-permute-start(bf16[2,32,384]{2,1,0:T(8,128)(2,1)S(1)} %convert_element_type.128), channel_id=1, source_target_pairs={{0,65},{65,0},{2,33},{33,2},{4,1},{1,4},{6,97},{97,6},{8,81},{81,8... | collective-permute-start | bytes 147464 | tf_op jit(solution)/shard_map/ppermute | solution.py:155
  250.0 9.5 %collective-permute-start.10 = (bf16[2,32,384]{2,1,0:T(8,128)(2,1)S(1)}, bf16[2,32,384]{2,1,0:T(8,128)(2,1)S(1)}, u32[]{:S(2)}, u32[]{:S(2)}) collective-permute-start(bf16[2,32,384]{2,1,0:T(8,128)(2,1)S(1)} %convert_element_type.132), channel_id=1, source_target_pairs={{1,64},{64,1},{3,32},{32,3},{5,0},{0,5},{7,96},{96,7},{9,80},{80,9... | collective-permute-start | bytes 147464 | tf_op jit(solution)/shard_map/ppermute | solution.py:155
  286.0 8.4 %collective-permute-start.11 = (bf16[2,32,384]{2,1,0:T(8,128)(2,1)S(1)}, bf16[2,32,384]{2,1,0:T(8,128)(2,1)S(1)}, u32[]{:S(2)}, u32[]{:S(2)}) collective-permute-start(bf16[2,32,384]{2,1,0:T(8,128)(2,1)S(1)} %convert_element_type.136), channel_id=1, source_target_pairs={{0,65},{65,0},{2,33},{33,2},{4,1},{1,4},{6,97},{97,6},{8,81},{81,8... | collective-permute-start | bytes 147464 | tf_op jit(solution)/shard_map/ppermute | solution.py:155
  294.4 4.1 %collective-permute-start.12 = (f32[32,384]{1,0:T(8,128)S(1)}, f32[32,384]{1,0:T(8,128)S(1)}, u32[]{:S(2)}, u32[]{:S(2)}) collective-permute-start(f32[32,384]{1,0:T(8,128)S(1)} %fusion.1), channel_id=1, source_target_pairs={{0,1},{1,0},{2,3},{3,2},{4,5},{5,4},{6,7},{7,6},{8,9},{9,8},{10,11... | collective-permute-start | bytes 147464 | tf_op jit(solution)/shard_map/ppermute | solution.py:155

commit v4 on v3

--- a/solution.py
+++ b/solution.py
@@ -158,14 +158,15 @@
     ids = jnp.stack([tile_row[0], tile_col[0] + core * panel, tile_live[0]])
     theirs, ids_there = send(start_block, swap), send(ids, swap)
     by_row = jnp.where(core == 0, jnp.stack([start_block, theirs]), jnp.stack([theirs, start_block]))
-    own, by_row, ids_there = lax.optimization_barrier((matrix_tiles[0], by_row, ids_there))
     to_column = [pair for s in span for k in span for pair in [(device(s, k, 1), along_col[1][s][k])]]
     start_turned = send(by_row, to_column + [(device(s, k, 0), device(s, k, 0)) for s in span for k in span])
-    tiles = keep(own, send(own, swap))
-
+
+    by_row, ids_there, own = lax.optimization_barrier((by_row, ids_there, matrix_tiles[0]))
+    other = send(own, swap)
     ids = jnp.concatenate([ids, ids_there], 1)
     alive = ids[2] > 0
-    position = jnp.cumsum(alive.astype(jnp.int32)) - 1
+    order = jnp.arange(2 * slots_here)
+    position = jnp.sum(jnp.where((order[None, :] < order[:, None]) & alive[None, :], 1, 0), axis=1)
     places = 2 * slots_here + REST
     hit = (position[None, :] == jnp.arange(places)[:, None]) & alive[None, :]
     count = jnp.sum(alive.astype(jnp.int32))
@@ -187,13 +188,16 @@
     fold = jnp.full((8, 128), jnp.where(diagonal, -0.5 * center_value, 0.0))
     tables = [table_of(core), table_of(1 - core)]
 
-    start_turned, tiles, tables, fold = lax.optimization_barrier((start_turned, tiles, tables, fold))
+    start_turned, tables, fold = lax.optimization_barrier((start_turned, tables, fold))
     current = start_turned
     earlier = current
     for degree in range(DEG):
         lead = degree % 2
         rounded = current.astype(jnp.bfloat16)
         x = exchange(jnp.broadcast_to(rounded[None], (side, *rounded.shape)), gather_groups[lead])
+        if degree == 0:
+            x, own, other = lax.optimization_barrier((x, own, other))
+            tiles = keep(own, other)
         partial = products(tables[lead], fold, x.reshape(2 * side, vectors, width), tiles)
         parts = exchange(partial.reshape(side, 2, vectors, width), gather_groups[1 - lead])
         share = jnp.sum(parts.astype(jnp.float32), axis=0)

time: 300 us -> 299 us (level)
  blocking collectives: 181 us -> 177 us
    all_to_all x16, blocking collectives: 181 us -> 177 us  [exchange(): lax.all_to_all(value, axes, 0, 0, axis_index_groups=groups, tiled=False)]
  transfers between devices with their start and end apart: 13 -> 13, of which waited for: 10 -> 10; matrix products, arithmetic and copies ran while one was open for 2% -> 2% of each run, Pallas kernels for 1% -> 0%
where the time goes in v4:
time: 299 us; the launch traced here: 298 us
  blocking collectives  177 us (59%)
  starting transfers between devices  54.7 us (18%)
  Pallas kernels  29.5 us (10%)
  waiting for transfers between devices  23.2 us (8%)
  other arithmetic  6.74 us (2%)
  between operations  4.28 us (1%)
    all_to_all x16, blocking collectives, exchange(): lax.all_to_all(value, axes, 0, 0, axis_index_groups=groups, tiled=False)  177 us
    ppermute x13, starting transfers between devices, send(): return lax.ppermute(value, axes, pairs)  54.7 us
    pallas_call x8, Pallas kernels, products(): pl.pallas_call(products_kernel, out_shape=jax.ShapeDtypeStruct(x.shape, j...  26.9 us
    ppermute x13, waiting for transfers between devices, send(): return lax.ppermute(value, axes, pairs)  23.2 us
  transfers between devices with their start and end apart: 13, of which 10 were waited for; matrix products, arithmetic and copies ran while one was open for 2% of the time, Pallas kernels for 0%

profile of v4, /device:TPU:7, one launch (start us, length us, event | category | flops | bytes accessed | tf_op | source)
XLA Modules:
  0.0 297.8 jit_solution(11602598103931803628)
XLA Ops:
  0.6 0.8 collective-permute-start
  1.4 0.7 broadcast_add_fusion
  2.0 0.7 pad_add_fusion.2
  2.7 0.1 collective-permute-start.2
  2.8 0.9 maximum_select_fusion
  3.7 0.2 collective-permute-done.2
  3.9 0.3 collective-permute-start.3
  4.9 5.9 %collective-permute-start.1 = (f32[2,32,384]{2,1,0:T(8,128)S(1)}, f32[2,32,384]{2,1,0:T(8,128)S(1)}, u32[]{:S(2)}, u32[]{:S(2)}) collective-permute-start(f32[2,32,384]{2,1,0:T(8,128)S(1)} %maximum_select_fusion), channel_id=1, source_target_pairs={{1,65},{3,33},{5,1},{7,97},{9,81},{11,49},{13,17},{15,113},{17,115... | collective-permute-start | bytes 294920 | tf_op jit(solution)/shard_map/ppermute | solution.py:155
  10.9 0.7 pad_add_fusion.3
  11.6 0.6 fusion.10
  14.2 0.1 add_add_fusion.1
  14.3 0.1 add_add_fusion
  14.4 0.1 select_reduce_fusion.3
  14.5 0.1 select_reduce_fusion.1
  14.7 0.7 bitcast_select_fusion.2
  15.3 0.7 broadcast_select_fusion.1
  16.1 12.5 %all_to_all.80 = bf16[8,2,32,384]{3,2,1,0:T(8,128)(2,1)S(1)} all-to-all(bf16[8,2,32,384]{3,2,1,0:T(8,128)(2,1)S(1)} %broadcast_in_dim.113), channel_id=1, replica_groups={{0,2,4,6,8,10,12,14},{16,18,20,22,24,26,28,30},{32,34,36,38,40,42,44,46..., dimensions={0} | all-to-all | bytes 786432 | tf_op jit(solution)/shard_map/all_to_all | solution.py:152
  28.6 2.3 copy-done
  31.0 2.7 shard_map.86.tiles_ref
  33.6 3.8 %shard_map.87 = bf16[16,32,384]{2,1,0:T(8,128)(2,1)S(1)} custom-call(s32[4,100]{1,0:T(4,128)S(1)} %get-tuple-element.14.table, f32[8,128]{1,0:T(8,128)S(1)} %broadcast_in_dim.112.fold_ref, bf16[16,32,384]{2,1,0:T(8,128)(2,1)S(1)} %bitcast.63, bf16[96,192,192]{2,1,0:T(8,128)(2,1)S(1)} %shard_map.86.tiles_ref), custom_call_target="tpu_custom_call" | custom-call | flops 226492416 | bytes 7077888 | tf_op jit(solution)/shard_map/pallas_call | solution.py:102
  37.4 10.4 %all_to_all.81 = bf16[8,2,32,384]{3,2,1,0:T(8,128)(2,1)S(1)} all-to-all(bf16[8,2,32,384]{3,2,1,0:T(8,128)(2,1)S(1)} %bitcast.68), channel_id=1, replica_groups={{1,3,5,7,9,11,13,15},{17,19,21,23,25,27,29,31},{33,35,37,39,41,43,45,47..., dimensions={0} | all-to-all | bytes 786432 | tf_op jit(solution)/shard_map/all_to_all | solution.py:152
  47.8 0.1 convert_reduce_fusion.7
  47.9 0.1 collective-permute-start.4
  48.6 7.2 %collective-permute-done.4 = bf16[2,32,384]{2,1,0:T(8,128)(2,1)S(1)} collective-permute-done((bf16[2,32,384]{2,1,0:T(8,128)(2,1)S(1)}, bf16[2,32,384]{2,1,0:T(8,128)(2,1)S(1)}, u32[]{:S(2)}, u32[]{:S(2)}) %collective-permute-start.4) | collective-permute-done | bytes 49184 | tf_op jit(solution)/shard_map/ppermute | solution.py:155
  55.9 8.8 %all_to_all.82 = bf16[8,2,32,384]{3,2,1,0:T(8,128)(2,1)S(1)} all-to-all(bf16[8,2,32,384]{3,2,1,0:T(8,128)(2,1)S(1)} %broadcast_in_dim.114), channel_id=1, replica_groups={{1,3,5,7,9,11,13,15},{17,19,21,23,25,27,29,31},{33,35,37,39,41,43,45,47..., dimensions={0} | all-to-all | bytes 786432 | tf_op jit(solution)/shard_map/all_to_all | solution.py:152
  64.7 2.9 shard_map.88
  67.6 12.3 %all_to_all.83 = bf16[8,2,32,384]{3,2,1,0:T(8,128)(2,1)S(1)} all-to-all(bf16[8,2,32,384]{3,2,1,0:T(8,128)(2,1)S(1)} %bitcast.70), channel_id=1, replica_groups={{0,2,4,6,8,10,12,14},{16,18,20,22,24,26,28,30},{32,34,36,38,40,42,44,46..., dimensions={0} | all-to-all | bytes 786432 | tf_op jit(solution)/shard_map/all_to_all | solution.py:152
  80.0 6.1 %collective-permute-start.5 = (bf16[2,32,384]{2,1,0:T(8,128)(2,1)S(1)}, bf16[2,32,384]{2,1,0:T(8,128)(2,1)S(1)}, u32[]{:S(2)}, u32[]{:S(2)}) collective-permute-start(bf16[2,32,384]{2,1,0:T(8,128)(2,1)S(1)} %convert_element_type.107), channel_id=1, source_target_pairs={{0,65},{65,0},{2,33},{33,2},{4,1},{1,4},{6,97},{97,6},{8,81},{81,8... | collective-permute-start | bytes 147464 | tf_op jit(solution)/shard_map/ppermute | solution.py:155
  86.0 1.8 collective-permute-done.5
  87.9 10.9 %all_to_all.84 = bf16[8,2,32,384]{3,2,1,0:T(8,128)(2,1)S(1)} all-to-all(bf16[8,2,32,384]{3,2,1,0:T(8,128)(2,1)S(1)} %broadcast_in_dim.115), channel_id=1, replica_groups={{0,2,4,6,8,10,12,14},{16,18,20,22,24,26,28,30},{32,34,36,38,40,42,44,46..., dimensions={0} | all-to-all | bytes 786432 | tf_op jit(solution)/shard_map/all_to_all | solution.py:152
  98.8 3.8 %shard_map.89 = bf16[16,32,384]{2,1,0:T(8,128)(2,1)S(1)} custom-call(s32[4,100]{1,0:T(4,128)S(1)} %get-tuple-element.14.table, f32[8,128]{1,0:T(8,128)S(1)} %broadcast_in_dim.112.fold_ref, bf16[16,32,384]{2,1,0:T(8,128)(2,1)S(1)} %bitcast.71, bf16[96,192,192]{2,1,0:T(8,128)(2,1)S(1)} %shard_map.86.tiles_ref), custom_call_target="tpu_custom_call" | custom-call | flops 226492416 | bytes 7077888 | tf_op jit(solution)/shard_map/pallas_call | solution.py:102
  102.5 10.0 %all_to_all.85 = bf16[8,2,32,384]{3,2,1,0:T(8,128)(2,1)S(1)} all-to-all(bf16[8,2,32,384]{3,2,1,0:T(8,128)(2,1)S(1)} %bitcast.72), channel_id=1, replica_groups={{1,3,5,7,9,11,13,15},{17,19,21,23,25,27,29,31},{33,35,37,39,41,43,45,47..., dimensions={0} | all-to-all | bytes 786432 | tf_op jit(solution)/shard_map/all_to_all | solution.py:152
  112.6 6.6 %collective-permute-start.6 = (bf16[2,32,384]{2,1,0:T(8,128)(2,1)S(1)}, bf16[2,32,384]{2,1,0:T(8,128)(2,1)S(1)}, u32[]{:S(2)}, u32[]{:S(2)}) collective-permute-start(bf16[2,32,384]{2,1,0:T(8,128)(2,1)S(1)} %convert_element_type.111), channel_id=1, source_target_pairs={{1,64},{64,1},{3,32},{32,3},{5,0},{0,5},{7,96},{96,7},{9,80},{80,9... | collective-permute-start | bytes 147464 | tf_op jit(solution)/shard_map/ppermute | solution.py:155
  119.2 2.4 collective-permute-done.6
  121.6 8.5 %all_to_all.86 = bf16[8,2,32,384]{3,2,1,0:T(8,128)(2,1)S(1)} all-to-all(bf16[8,2,32,384]{3,2,1,0:T(8,128)(2,1)S(1)} %broadcast_in_dim.116), channel_id=1, replica_groups={{1,3,5,7,9,11,13,15},{17,19,21,23,25,27,29,31},{33,35,37,39,41,43,45,47..., dimensions={0} | all-to-all | bytes 786432 | tf_op jit(solution)/shard_map/all_to_all | solution.py:152
  130.1 2.9 shard_map.90
  133.1 16.0 %all_to_all.87 = bf16[8,2,32,384]{3,2,1,0:T(8,128)(2,1)S(1)} all-to-all(bf16[8,2,32,384]{3,2,1,0:T(8,128)(2,1)S(1)} %bitcast.74), channel_id=1, replica_groups={{0,2,4,6,8,10,12,14},{16,18,20,22,24,26,28,30},{32,34,36,38,40,42,44,46..., dimensions={0} | all-to-all | bytes 786432 | tf_op jit(solution)/shard_map/all_to_all | solution.py:152
  149.1 4.4 %collective-permute-start.7 = (bf16[2,32,384]{2,1,0:T(8,128)(2,1)S(1)}, bf16[2,32,384]{2,1,0:T(8,128)(2,1)S(1)}, u32[]{:S(2)}, u32[]{:S(2)}) collective-permute-start(bf16[2,32,384]{2,1,0:T(8,128)(2,1)S(1)} %convert_element_type.115), channel_id=1, source_target_pairs={{0,65},{65,0},{2,33},{33,2},{4,1},{1,4},{6,97},{97,6},{8,81},{81,8... | collective-permute-start | bytes 147464 | tf_op jit(solution)/shard_map/ppermute | solution.py:155
  153.6 2.8 collective-permute-done.7
  156.4 11.6 %all_to_all.88 = bf16[8,2,32,384]{3,2,1,0:T(8,128)(2,1)S(1)} all-to-all(bf16[8,2,32,384]{3,2,1,0:T(8,128)(2,1)S(1)} %broadcast_in_dim.117), channel_id=1, replica_groups={{0,2,4,6,8,10,12,14},{16,18,20,22,24,26,28,30},{32,34,36,38,40,42,44,46..., dimensions={0} | all-to-all | bytes 786432 | tf_op jit(solution)/shard_map/all_to_all | solution.py:152
  168.0 3.8 %shard_map.91 = bf16[16,32,384]{2,1,0:T(8,128)(2,1)S(1)} custom-call(s32[4,100]{1,0:T(4,128)S(1)} %get-tuple-element.14.table, f32[8,128]{1,0:T(8,128)S(1)} %broadcast_in_dim.112.fold_ref, bf16[16,32,384]{2,1,0:T(8,128)(2,1)S(1)} %bitcast.75, bf16[96,192,192]{2,1,0:T(8,128)(2,1)S(1)} %shard_map.86.tiles_ref), custom_call_target="tpu_custom_call" | custom-call | flops 226492416 | bytes 7077888 | tf_op jit(solution)/shard_map/pallas_call | solution.py:102
  171.8 8.9 %all_to_all.89 = bf16[8,2,32,384]{3,2,1,0:T(8,128)(2,1)S(1)} all-to-all(bf16[8,2,32,384]{3,2,1,0:T(8,128)(2,1)S(1)} %bitcast.76), channel_id=1, replica_groups={{1,3,5,7,9,11,13,15},{17,19,21,23,25,27,29,31},{33,35,37,39,41,43,45,47..., dimensions={0} | all-to-all | bytes 786432 | tf_op jit(solution)/shard_map/all_to_all | solution.py:152
  180.7 0.1 convert_reduce_fusion.3
  180.7 6.7 %collective-permute-start.8 = (bf16[2,32,384]{2,1,0:T(8,128)(2,1)S(1)}, bf16[2,32,384]{2,1,0:T(8,128)(2,1)S(1)}, u32[]{:S(2)}, u32[]{:S(2)}) collective-permute-start(bf16[2,32,384]{2,1,0:T(8,128)(2,1)S(1)} %convert_element_type.119), channel_id=1, source_target_pairs={{1,64},{64,1},{3,32},{32,3},{5,0},{0,5},{7,96},{96,7},{9,80},{80,9... | collective-permute-start | bytes 147464 | tf_op jit(solution)/shard_map/ppermute | solution.py:155
  187.4 2.2 collective-permute-done.8
  189.7 9.0 %all_to_all.90 = bf16[8,2,32,384]{3,2,1,0:T(8,128)(2,1)S(1)} all-to-all(bf16[8,2,32,384]{3,2,1,0:T(8,128)(2,1)S(1)} %broadcast_in_dim.118), channel_id=1, replica_groups={{1,3,5,7,9,11,13,15},{17,19,21,23,25,27,29,31},{33,35,37,39,41,43,45,47..., dimensions={0} | all-to-all | bytes 786432 | tf_op jit(solution)/shard_map/all_to_all | solution.py:152
  198.7 2.9 shard_map.92
  201.6 14.3 %all_to_all.91 = bf16[8,2,32,384]{3,2,1,0:T(8,128)(2,1)S(1)} all-to-all(bf16[8,2,32,384]{3,2,1,0:T(8,128)(2,1)S(1)} %bitcast.78), channel_id=1, replica_groups={{0,2,4,6,8,10,12,14},{16,18,20,22,24,26,28,30},{32,34,36,38,40,42,44,46..., dimensions={0} | all-to-all | bytes 786432 | tf_op jit(solution)/shard_map/all_to_all | solution.py:152
  216.0 6.3 %collective-permute-start.9 = (bf16[2,32,384]{2,1,0:T(8,128)(2,1)S(1)}, bf16[2,32,384]{2,1,0:T(8,128)(2,1)S(1)}, u32[]{:S(2)}, u32[]{:S(2)}) collective-permute-start(bf16[2,32,384]{2,1,0:T(8,128)(2,1)S(1)} %convert_element_type.123), channel_id=1, source_target_pairs={{0,65},{65,0},{2,33},{33,2},{4,1},{1,4},{6,97},{97,6},{8,81},{81,8... | collective-permute-start | bytes 147464 | tf_op jit(solution)/shard_map/ppermute | solution.py:155
  222.2 1.8 collective-permute-done.9
  224.1 10.7 %all_to_all.92 = bf16[8,2,32,384]{3,2,1,0:T(8,128)(2,1)S(1)} all-to-all(bf16[8,2,32,384]{3,2,1,0:T(8,128)(2,1)S(1)} %broadcast_in_dim.119), channel_id=1, replica_groups={{0,2,4,6,8,10,12,14},{16,18,20,22,24,26,28,30},{32,34,36,38,40,42,44,46..., dimensions={0} | all-to-all | bytes 786432 | tf_op jit(solution)/shard_map/all_to_all | solution.py:152
  234.8 3.8 %shard_map.93 = bf16[16,32,384]{2,1,0:T(8,128)(2,1)S(1)} custom-call(s32[4,100]{1,0:T(4,128)S(1)} %get-tuple-element.14.table, f32[8,128]{1,0:T(8,128)S(1)} %broadcast_in_dim.112.fold_ref, bf16[16,32,384]{2,1,0:T(8,128)(2,1)S(1)} %bitcast.66, bf16[96,192,192]{2,1,0:T(8,128)(2,1)S(1)} %shard_map.86.tiles_ref), custom_call_target="tpu_custom_call" | custom-call | flops 226492416 | bytes 7077888 | tf_op jit(solution)/shard_map/pallas_call | solution.py:102
  238.5 10.0 %all_to_all.93 = bf16[8,2,32,384]{3,2,1,0:T(8,128)(2,1)S(1)} all-to-all(bf16[8,2,32,384]{3,2,1,0:T(8,128)(2,1)S(1)} %bitcast.67), channel_id=1, replica_groups={{1,3,5,7,9,11,13,15},{17,19,21,23,25,27,29,31},{33,35,37,39,41,43,45,47..., dimensions={0} | all-to-all | bytes 786432 | tf_op jit(solution)/shard_map/all_to_all | solution.py:152
  248.7 7.2 %collective-permute-start.10 = (bf16[2,32,384]{2,1,0:T(8,128)(2,1)S(1)}, bf16[2,32,384]{2,1,0:T(8,128)(2,1)S(1)}, u32[]{:S(2)}, u32[]{:S(2)}) collective-permute-start(bf16[2,32,384]{2,1,0:T(8,128)(2,1)S(1)} %convert_element_type.127), channel_id=1, source_target_pairs={{1,64},{64,1},{3,32},{32,3},{5,0},{0,5},{7,96},{96,7},{9,80},{80,9... | collective-permute-start | bytes 147464 | tf_op jit(solution)/shard_map/ppermute | solution.py:155
  255.8 2.3 collective-permute-done.10
  258.2 8.6 %all_to_all.94 = bf16[8,2,32,384]{3,2,1,0:T(8,128)(2,1)S(1)} all-to-all(bf16[8,2,32,384]{3,2,1,0:T(8,128)(2,1)S(1)} %broadcast_in_dim.120), channel_id=1, replica_groups={{1,3,5,7,9,11,13,15},{17,19,21,23,25,27,29,31},{33,35,37,39,41,43,45,47..., dimensions={0} | all-to-all | bytes 786432 | tf_op jit(solution)/shard_map/all_to_all | solution.py:152
  266.8 2.9 shard_map.94
  269.7 14.3 %all_to_all.95 = bf16[8,2,32,384]{3,2,1,0:T(8,128)(2,1)S(1)} all-to-all(bf16[8,2,32,384]{3,2,1,0:T(8,128)(2,1)S(1)} %bitcast.65), channel_id=1, replica_groups={{0,2,4,6,8,10,12,14},{16,18,20,22,24,26,28,30},{32,34,36,38,40,42,44,46..., dimensions={0} | all-to-all | bytes 786432 | tf_op jit(solution)/shard_map/all_to_all | solution.py:152
  284.1 0.1 convert_reduce_fusion
  284.1 6.0 %collective-permute-start.11 = (bf16[2,32,384]{2,1,0:T(8,128)(2,1)S(1)}, bf16[2,32,384]{2,1,0:T(8,128)(2,1)S(1)}, u32[]{:S(2)}, u32[]{:S(2)}) collective-permute-start(bf16[2,32,384]{2,1,0:T(8,128)(2,1)S(1)} %convert_element_type.131), channel_id=1, source_target_pairs={{0,65},{65,0},{2,33},{33,2},{4,1},{1,4},{6,97},{97,6},{8,81},{81,8... | collective-permute-start | bytes 147464 | tf_op jit(solution)/shard_map/ppermute | solution.py:155
  290.2 1.8 collective-permute-done.11
  292.0 4.3 %collective-permute-start.12 = (f32[32,384]{1,0:T(8,128)S(1)}, f32[32,384]{1,0:T(8,128)S(1)}, u32[]{:S(2)}, u32[]{:S(2)}) collective-permute-start(f32[32,384]{1,0:T(8,128)S(1)} %fusion.1), channel_id=1, source_target_pairs={{0,1},{1,0},{2,3},{3,2},{4,5},{5,4},{6,7},{7,6},{8,9},{9,8},{10,11... | collective-permute-start | bytes 147464 | tf_op jit(solution)/shard_map/ppermute | solution.py:155
  296.2 0.9 collective-permute-done.12
  297.1 0.6 fusion
  (40 shorter events, 1.0 us)
Async XLA Ops:
  0.6 2.2 collective-permute-start
  2.7 1.2 collective-permute-start.2
  3.9 24.7 %collective-permute-start.3 = (bf16[48,192,192]{2,1,0:T(8,128)(2,1)}, bf16[48,192,192]{2,1,0:T(8,128)(2,1)}, u32[]{:S(2)}, u32[]{:S(2)}) collective-permute-start(bf16[48,192,192]{2,1,0:T(8,128)(2,1)} %bitcast.61), channel_id=1, source_target_pairs={{0,1},{1,0},{2,3},{3,2},{4,5},{5,4},{6,7},{7,6},{8,9},{9,8},{10,11... | collective-permute-start | bytes 10616840 | tf_op jit(solution)/shard_map/ppermute | solution.py:155
  4.9 11.1 %collective-permute-start.1 = (f32[2,32,384]{2,1,0:T(8,128)S(1)}, f32[2,32,384]{2,1,0:T(8,128)S(1)}, u32[]{:S(2)}, u32[]{:S(2)}) collective-permute-start(f32[2,32,384]{2,1,0:T(8,128)S(1)} %maximum_select_fusion), channel_id=1, source_target_pairs={{1,65},{3,33},{5,1},{7,97},{9,81},{11,49},{13,17},{15,113},{17,115... | collective-permute-start | bytes 294920 | tf_op jit(solution)/shard_map/ppermute | solution.py:155
  28.6 2.3 copy-start
  47.9 7.9 %collective-permute-start.4 = (bf16[2,32,384]{2,1,0:T(8,128)(2,1)S(1)}, bf16[2,32,384]{2,1,0:T(8,128)(2,1)S(1)}, u32[]{:S(2)}, u32[]{:S(2)}) collective-permute-start(bf16[2,32,384]{2,1,0:T(8,128)(2,1)S(1)} %convert_element_type.103), channel_id=1, source_target_pairs={{1,64},{64,1},{3,32},{32,3},{5,0},{0,5},{7,96},{96,7},{9,80},{80,9... | collective-permute-start | bytes 147464 | tf_op jit(solution)/shard_map/ppermute | solution.py:155
  80.0 7.8 %collective-permute-start.5 = (bf16[2,32,384]{2,1,0:T(8,128)(2,1)S(1)}, bf16[2,32,384]{2,1,0:T(8,128)(2,1)S(1)}, u32[]{:S(2)}, u32[]{:S(2)}) collective-permute-start(bf16[2,32,384]{2,1,0:T(8,128)(2,1)S(1)} %convert_element_type.107), channel_id=1, source_target_pairs={{0,65},{65,0},{2,33},{33,2},{4,1},{1,4},{6,97},{97,6},{8,81},{81,8... | collective-permute-start | bytes 147464 | tf_op jit(solution)/shard_map/ppermute | solution.py:155
  112.6 8.9 %collective-permute-start.6 = (bf16[2,32,384]{2,1,0:T(8,128)(2,1)S(1)}, bf16[2,32,384]{2,1,0:T(8,128)(2,1)S(1)}, u32[]{:S(2)}, u32[]{:S(2)}) collective-permute-start(bf16[2,32,384]{2,1,0:T(8,128)(2,1)S(1)} %convert_element_type.111), channel_id=1, source_target_pairs={{1,64},{64,1},{3,32},{32,3},{5,0},{0,5},{7,96},{96,7},{9,80},{80,9... | collective-permute-start | bytes 147464 | tf_op jit(solution)/shard_map/ppermute | solution.py:155
  149.1 7.2 %collective-permute-start.7 = (bf16[2,32,384]{2,1,0:T(8,128)(2,1)S(1)}, bf16[2,32,384]{2,1,0:T(8,128)(2,1)S(1)}, u32[]{:S(2)}, u32[]{:S(2)}) collective-permute-start(bf16[2,32,384]{2,1,0:T(8,128)(2,1)S(1)} %convert_element_type.115), channel_id=1, source_target_pairs={{0,65},{65,0},{2,33},{33,2},{4,1},{1,4},{6,97},{97,6},{8,81},{81,8... | collective-permute-start | bytes 147464 | tf_op jit(solution)/shard_map/ppermute | solution.py:155
  180.7 8.9 %collective-permute-start.8 = (bf16[2,32,384]{2,1,0:T(8,128)(2,1)S(1)}, bf16[2,32,384]{2,1,0:T(8,128)(2,1)S(1)}, u32[]{:S(2)}, u32[]{:S(2)}) collective-permute-start(bf16[2,32,384]{2,1,0:T(8,128)(2,1)S(1)} %convert_element_type.119), channel_id=1, source_target_pairs={{1,64},{64,1},{3,32},{32,3},{5,0},{0,5},{7,96},{96,7},{9,80},{80,9... | collective-permute-start | bytes 147464 | tf_op jit(solution)/shard_map/ppermute | solution.py:155
  216.0 8.0 %collective-permute-start.9 = (bf16[2,32,384]{2,1,0:T(8,128)(2,1)S(1)}, bf16[2,32,384]{2,1,0:T(8,128)(2,1)S(1)}, u32[]{:S(2)}, u32[]{:S(2)}) collective-permute-start(bf16[2,32,384]{2,1,0:T(8,128)(2,1)S(1)} %convert_element_type.123), channel_id=1, source_target_pairs={{0,65},{65,0},{2,33},{33,2},{4,1},{1,4},{6,97},{97,6},{8,81},{81,8... | collective-permute-start | bytes 147464 | tf_op jit(solution)/shard_map/ppermute | solution.py:155
  248.7 9.5 %collective-permute-start.10 = (bf16[2,32,384]{2,1,0:T(8,128)(2,1)S(1)}, bf16[2,32,384]{2,1,0:T(8,128)(2,1)S(1)}, u32[]{:S(2)}, u32[]{:S(2)}) collective-permute-start(bf16[2,32,384]{2,1,0:T(8,128)(2,1)S(1)} %convert_element_type.127), channel_id=1, source_target_pairs={{1,64},{64,1},{3,32},{32,3},{5,0},{0,5},{7,96},{96,7},{9,80},{80,9... | collective-permute-start | bytes 147464 | tf_op jit(solution)/shard_map/ppermute | solution.py:155
  284.1 7.8 %collective-permute-start.11 = (bf16[2,32,384]{2,1,0:T(8,128)(2,1)S(1)}, bf16[2,32,384]{2,1,0:T(8,128)(2,1)S(1)}, u32[]{:S(2)}, u32[]{:S(2)}) collective-permute-start(bf16[2,32,384]{2,1,0:T(8,128)(2,1)S(1)} %convert_element_type.131), channel_id=1, source_target_pairs={{0,65},{65,0},{2,33},{33,2},{4,1},{1,4},{6,97},{97,6},{8,81},{81,8... | collective-permute-start | bytes 147464 | tf_op jit(solution)/shard_map/ppermute | solution.py:155
  292.0 5.1 %collective-permute-start.12 = (f32[32,384]{1,0:T(8,128)S(1)}, f32[32,384]{1,0:T(8,128)S(1)}, u32[]{:S(2)}, u32[]{:S(2)}) collective-permute-start(f32[32,384]{1,0:T(8,128)S(1)} %fusion.1), channel_id=1, source_target_pairs={{0,1},{1,0},{2,3},{3,2},{4,5},{5,4},{6,7},{7,6},{8,9},{9,8},{10,11... | collective-permute-start | bytes 147464 | tf_op jit(solution)/shard_map/ppermute | solution.py:155

commit v5 on v4

--- a/solution.py
+++ b/solution.py
@@ -6,8 +6,8 @@
 from jax.sharding import PartitionSpec as P
 
 DEG = 8
-GROUP = 24
-REST = 4
+GROUP = 32
+REST = 8
 
 
 def keep_kernel(own_ref, other_ref, kept_ref, sems):
@@ -36,11 +36,13 @@
     )(own, other)
 
 
-def products_kernel(table, fold_ref, x_ref, tiles_ref, out_ref, x_wide, total):
+def products_kernel(table_ref, fold_ref, x_ref, tiles_ref, out_ref, x_wide, total, table, sem):
     vectors, size = x_wide.shape[1], tiles_ref.shape[-1]
     pairs = x_ref.shape[0]
     low = lax.broadcasted_iota(jnp.int32, (vectors, 128), 1) < 64
     fold = fold_ref[:1, :]
+    fetch = pltpu.make_async_copy(table_ref, table, sem)
+    fetch.start()
 
     def place(cluster, half, value):
         x_wide[cluster, :, 128 * half : 128 * (half + 1)] = value.astype(jnp.bfloat16)
@@ -55,6 +57,8 @@
         place(2 * pair + 1, 1, last_rolled)
     for half in range(2):
         place(2 * pairs, half, jnp.zeros((vectors, 128), jnp.float32))
+
+    fetch.wait()
 
     def run(contract):
         def add(start, members):
@@ -102,11 +106,13 @@
     return pl.pallas_call(
         products_kernel,
         out_shape=jax.ShapeDtypeStruct(x.shape, jnp.bfloat16),
-        in_specs=[pl.BlockSpec(memory_space=pltpu.SMEM), vmem, vmem, vmem],
+        in_specs=[pl.BlockSpec(memory_space=pl.ANY), vmem, vmem, vmem],
         out_specs=vmem,
         scratch_shapes=[
             pltpu.VMEM((2 * pairs + 1, vectors, 256), jnp.bfloat16),
             pltpu.VMEM((2 * pairs + 1, vectors, 256), jnp.float32),
+            pltpu.SMEM(table.shape, jnp.int32),
+            pltpu.SemaphoreType.DMA,
         ],
         compiler_params=pltpu.CompilerParams(vmem_limit_bytes=16 * 1024 * 1024),
         cost_estimate=pl.CostEstimate(

time: 299 us -> 296 us (0.990)
  Pallas kernels: 29.5 us -> 25.4 us
    pallas_call x8, Pallas kernels: 26.9 us -> 22.7 us  [products(): pl.pallas_call(products_kernel, out_shape=jax.ShapeDtypeStruct(x.shape, j...]
where the time goes in v5:
time: 296 us; the launch traced here: 295 us
  blocking collectives  178 us (60%)
  starting transfers between devices  53.6 us (18%)
  Pallas kernels  25.4 us (9%)
  waiting for transfers between devices  24.1 us (8%)
  other arithmetic  6.74 us (2%)
  between operations  4.92 us (2%)
    all_to_all x16, blocking collectives, exchange(): lax.all_to_all(value, axes, 0, 0, axis_index_groups=groups, tiled=False)  178 us
    ppermute x13, starting transfers between devices, send(): return lax.ppermute(value, axes, pairs)  53.6 us
    ppermute x13, waiting for transfers between devices, send(): return lax.ppermute(value, axes, pairs)  24.1 us
    pallas_call x8, Pallas kernels, products(): pl.pallas_call(products_kernel, out_shape=jax.ShapeDtypeStruct(x.shape, j...  22.7 us
  transfers between devices with their start and end apart: 13, of which 10 were waited for; matrix products, arithmetic and copies ran while one was open for 2% of the time, Pallas kernels for 0%

profile of v5, /device:TPU:7, one launch (start us, length us, event | category | flops | bytes accessed | tf_op | source)
XLA Modules:
  0.0 295.1 jit_solution(4089025894191032786)
XLA Ops:
  0.6 0.8 collective-permute-start
  1.4 0.7 broadcast_add_fusion
  2.0 0.7 pad_add_fusion.2
  2.7 0.1 collective-permute-start.2
  2.8 0.9 maximum_select_fusion
  3.7 0.2 collective-permute-done.2
  3.9 0.3 collective-permute-start.3
  4.9 5.9 %collective-permute-start.1 = (f32[2,32,384]{2,1,0:T(8,128)S(1)}, f32[2,32,384]{2,1,0:T(8,128)S(1)}, u32[]{:S(2)}, u32[]{:S(2)}) collective-permute-start(f32[2,32,384]{2,1,0:T(8,128)S(1)} %maximum_select_fusion), channel_id=1, source_target_pairs={{1,65},{3,33},{5,1},{7,97},{9,81},{11,49},{13,17},{15,113},{17,115... | collective-permute-start | bytes 294920 | tf_op jit(solution)/shard_map/ppermute | solution.py:161
  10.9 0.7 pad_add_fusion.3
  11.6 0.6 fusion.10
  14.9 0.1 add_add_fusion.1
  15.0 0.1 add_add_fusion
  15.0 0.1 select_reduce_fusion.3
  15.2 0.1 select_reduce_fusion.1
  15.3 0.7 bitcast_select_fusion.2
  16.0 0.7 broadcast_select_fusion.1
  16.7 12.5 %all_to_all.80 = bf16[8,2,32,384]{3,2,1,0:T(8,128)(2,1)S(1)} all-to-all(bf16[8,2,32,384]{3,2,1,0:T(8,128)(2,1)S(1)} %broadcast_in_dim.113), channel_id=1, replica_groups={{0,2,4,6,8,10,12,14},{16,18,20,22,24,26,28,30},{32,34,36,38,40,42,44,46..., dimensions={0} | all-to-all | bytes 786432 | tf_op jit(solution)/shard_map/all_to_all | solution.py:158
  29.3 2.3 copy-done
  31.6 2.7 shard_map.86.tiles_ref
  34.3 3.3 %shard_map.87 = bf16[16,32,384]{2,1,0:T(8,128)(2,1)S(1)} custom-call(s32[4,104]{1,0:T(4,128)S(1)} %get-tuple-element.14.table_ref, f32[8,128]{1,0:T(8,128)S(1)} %broadcast_in_dim.112.fold_ref, bf16[16,32,384]{2,1,0:T(8,128)(2,1)S(1)} %bitcast.63, bf16[96,192,192]{2,1,0:T(8,128)(2,1)S(1)} %shard_map.86.tiles_ref), custom_call_target="tpu_custom_call" | custom-call | flops 226492416 | bytes 7077888 | tf_op jit(solution)/shard_map/pallas_call | solution.py:106
  37.6 10.5 %all_to_all.81 = bf16[8,2,32,384]{3,2,1,0:T(8,128)(2,1)S(1)} all-to-all(bf16[8,2,32,384]{3,2,1,0:T(8,128)(2,1)S(1)} %bitcast.68), channel_id=1, replica_groups={{1,3,5,7,9,11,13,15},{17,19,21,23,25,27,29,31},{33,35,37,39,41,43,45,47..., dimensions={0} | all-to-all | bytes 786432 | tf_op jit(solution)/shard_map/all_to_all | solution.py:158
  48.1 0.1 convert_reduce_fusion.7
  48.2 0.1 collective-permute-start.4
  48.9 7.2 %collective-permute-done.4 = bf16[2,32,384]{2,1,0:T(8,128)(2,1)S(1)} collective-permute-done((bf16[2,32,384]{2,1,0:T(8,128)(2,1)S(1)}, bf16[2,32,384]{2,1,0:T(8,128)(2,1)S(1)}, u32[]{:S(2)}, u32[]{:S(2)}) %collective-permute-start.4) | collective-permute-done | bytes 49184 | tf_op jit(solution)/shard_map/ppermute | solution.py:161
  56.1 8.5 %all_to_all.82 = bf16[8,2,32,384]{3,2,1,0:T(8,128)(2,1)S(1)} all-to-all(bf16[8,2,32,384]{3,2,1,0:T(8,128)(2,1)S(1)} %broadcast_in_dim.114), channel_id=1, replica_groups={{1,3,5,7,9,11,13,15},{17,19,21,23,25,27,29,31},{33,35,37,39,41,43,45,47..., dimensions={0} | all-to-all | bytes 786432 | tf_op jit(solution)/shard_map/all_to_all | solution.py:158
  64.7 2.4 shard_map.88
  67.1 13.1 %all_to_all.83 = bf16[8,2,32,384]{3,2,1,0:T(8,128)(2,1)S(1)} all-to-all(bf16[8,2,32,384]{3,2,1,0:T(8,128)(2,1)S(1)} %bitcast.70), channel_id=1, replica_groups={{0,2,4,6,8,10,12,14},{16,18,20,22,24,26,28,30},{32,34,36,38,40,42,44,46..., dimensions={0} | all-to-all | bytes 786432 | tf_op jit(solution)/shard_map/all_to_all | solution.py:158
  80.3 5.4 %collective-permute-start.5 = (bf16[2,32,384]{2,1,0:T(8,128)(2,1)S(1)}, bf16[2,32,384]{2,1,0:T(8,128)(2,1)S(1)}, u32[]{:S(2)}, u32[]{:S(2)}) collective-permute-start(bf16[2,32,384]{2,1,0:T(8,128)(2,1)S(1)} %convert_element_type.107), channel_id=1, source_target_pairs={{0,65},{65,0},{2,33},{33,2},{4,1},{1,4},{6,97},{97,6},{8,81},{81,8... | collective-permute-start | bytes 147464 | tf_op jit(solution)/shard_map/ppermute | solution.py:161
  85.6 1.8 collective-permute-done.5
  87.5 11.0 %all_to_all.84 = bf16[8,2,32,384]{3,2,1,0:T(8,128)(2,1)S(1)} all-to-all(bf16[8,2,32,384]{3,2,1,0:T(8,128)(2,1)S(1)} %broadcast_in_dim.115), channel_id=1, replica_groups={{0,2,4,6,8,10,12,14},{16,18,20,22,24,26,28,30},{32,34,36,38,40,42,44,46..., dimensions={0} | all-to-all | bytes 786432 | tf_op jit(solution)/shard_map/all_to_all | solution.py:158
  98.5 3.3 %shard_map.89 = bf16[16,32,384]{2,1,0:T(8,128)(2,1)S(1)} custom-call(s32[4,104]{1,0:T(4,128)S(1)} %get-tuple-element.14.table_ref, f32[8,128]{1,0:T(8,128)S(1)} %broadcast_in_dim.112.fold_ref, bf16[16,32,384]{2,1,0:T(8,128)(2,1)S(1)} %bitcast.71, bf16[96,192,192]{2,1,0:T(8,128)(2,1)S(1)} %shard_map.86.tiles_ref), custom_call_target="tpu_custom_call" | custom-call | flops 226492416 | bytes 7077888 | tf_op jit(solution)/shard_map/pallas_call | solution.py:106
  101.8 9.6 %all_to_all.85 = bf16[8,2,32,384]{3,2,1,0:T(8,128)(2,1)S(1)} all-to-all(bf16[8,2,32,384]{3,2,1,0:T(8,128)(2,1)S(1)} %bitcast.72), channel_id=1, replica_groups={{1,3,5,7,9,11,13,15},{17,19,21,23,25,27,29,31},{33,35,37,39,41,43,45,47..., dimensions={0} | all-to-all | bytes 786432 | tf_op jit(solution)/shard_map/all_to_all | solution.py:158
  111.4 0.1 convert_reduce_fusion.5
  111.5 7.2 %collective-permute-start.6 = (bf16[2,32,384]{2,1,0:T(8,128)(2,1)S(1)}, bf16[2,32,384]{2,1,0:T(8,128)(2,1)S(1)}, u32[]{:S(2)}, u32[]{:S(2)}) collective-permute-start(bf16[2,32,384]{2,1,0:T(8,128)(2,1)S(1)} %convert_element_type.111), channel_id=1, source_target_pairs={{1,64},{64,1},{3,32},{32,3},{5,0},{0,5},{7,96},{96,7},{9,80},{80,9... | collective-permute-start | bytes 147464 | tf_op jit(solution)/shard_map/ppermute | solution.py:161
  118.7 2.3 collective-permute-done.6
  121.1 8.5 %all_to_all.86 = bf16[8,2,32,384]{3,2,1,0:T(8,128)(2,1)S(1)} all-to-all(bf16[8,2,32,384]{3,2,1,0:T(8,128)(2,1)S(1)} %broadcast_in_dim.116), channel_id=1, replica_groups={{1,3,5,7,9,11,13,15},{17,19,21,23,25,27,29,31},{33,35,37,39,41,43,45,47..., dimensions={0} | all-to-all | bytes 786432 | tf_op jit(solution)/shard_map/all_to_all | solution.py:158
  129.7 2.4 shard_map.90
  132.1 16.6 %all_to_all.87 = bf16[8,2,32,384]{3,2,1,0:T(8,128)(2,1)S(1)} all-to-all(bf16[8,2,32,384]{3,2,1,0:T(8,128)(2,1)S(1)} %bitcast.74), channel_id=1, replica_groups={{0,2,4,6,8,10,12,14},{16,18,20,22,24,26,28,30},{32,34,36,38,40,42,44,46..., dimensions={0} | all-to-all | bytes 786432 | tf_op jit(solution)/shard_map/all_to_all | solution.py:158
  148.7 4.0 %collective-permute-start.7 = (bf16[2,32,384]{2,1,0:T(8,128)(2,1)S(1)}, bf16[2,32,384]{2,1,0:T(8,128)(2,1)S(1)}, u32[]{:S(2)}, u32[]{:S(2)}) collective-permute-start(bf16[2,32,384]{2,1,0:T(8,128)(2,1)S(1)} %convert_element_type.115), channel_id=1, source_target_pairs={{0,65},{65,0},{2,33},{33,2},{4,1},{1,4},{6,97},{97,6},{8,81},{81,8... | collective-permute-start | bytes 147464 | tf_op jit(solution)/shard_map/ppermute | solution.py:161
  152.7 3.4 %collective-permute-done.7 = bf16[2,32,384]{2,1,0:T(8,128)(2,1)S(1)} collective-permute-done((bf16[2,32,384]{2,1,0:T(8,128)(2,1)S(1)}, bf16[2,32,384]{2,1,0:T(8,128)(2,1)S(1)}, u32[]{:S(2)}, u32[]{:S(2)}) %collective-permute-start.7) | collective-permute-done | bytes 49184 | tf_op jit(solution)/shard_map/ppermute | solution.py:161
  156.2 11.7 %all_to_all.88 = bf16[8,2,32,384]{3,2,1,0:T(8,128)(2,1)S(1)} all-to-all(bf16[8,2,32,384]{3,2,1,0:T(8,128)(2,1)S(1)} %broadcast_in_dim.117), channel_id=1, replica_groups={{0,2,4,6,8,10,12,14},{16,18,20,22,24,26,28,30},{32,34,36,38,40,42,44,46..., dimensions={0} | all-to-all | bytes 786432 | tf_op jit(solution)/shard_map/all_to_all | solution.py:158
  167.9 3.3 %shard_map.91 = bf16[16,32,384]{2,1,0:T(8,128)(2,1)S(1)} custom-call(s32[4,104]{1,0:T(4,128)S(1)} %get-tuple-element.14.table_ref, f32[8,128]{1,0:T(8,128)S(1)} %broadcast_in_dim.112.fold_ref, bf16[16,32,384]{2,1,0:T(8,128)(2,1)S(1)} %bitcast.75, bf16[96,192,192]{2,1,0:T(8,128)(2,1)S(1)} %shard_map.86.tiles_ref), custom_call_target="tpu_custom_call" | custom-call | flops 226492416 | bytes 7077888 | tf_op jit(solution)/shard_map/pallas_call | solution.py:106
  171.2 8.3 %all_to_all.89 = bf16[8,2,32,384]{3,2,1,0:T(8,128)(2,1)S(1)} all-to-all(bf16[8,2,32,384]{3,2,1,0:T(8,128)(2,1)S(1)} %bitcast.76), channel_id=1, replica_groups={{1,3,5,7,9,11,13,15},{17,19,21,23,25,27,29,31},{33,35,37,39,41,43,45,47..., dimensions={0} | all-to-all | bytes 786432 | tf_op jit(solution)/shard_map/all_to_all | solution.py:158
  179.6 6.6 %collective-permute-start.8 = (bf16[2,32,384]{2,1,0:T(8,128)(2,1)S(1)}, bf16[2,32,384]{2,1,0:T(8,128)(2,1)S(1)}, u32[]{:S(2)}, u32[]{:S(2)}) collective-permute-start(bf16[2,32,384]{2,1,0:T(8,128)(2,1)S(1)} %convert_element_type.119), channel_id=1, source_target_pairs={{1,64},{64,1},{3,32},{32,3},{5,0},{0,5},{7,96},{96,7},{9,80},{80,9... | collective-permute-start | bytes 147464 | tf_op jit(solution)/shard_map/ppermute | solution.py:161
  186.2 2.3 collective-permute-done.8
  188.6 8.5 %all_to_all.90 = bf16[8,2,32,384]{3,2,1,0:T(8,128)(2,1)S(1)} all-to-all(bf16[8,2,32,384]{3,2,1,0:T(8,128)(2,1)S(1)} %broadcast_in_dim.118), channel_id=1, replica_groups={{1,3,5,7,9,11,13,15},{17,19,21,23,25,27,29,31},{33,35,37,39,41,43,45,47..., dimensions={0} | all-to-all | bytes 786432 | tf_op jit(solution)/shard_map/all_to_all | solution.py:158
  197.2 2.4 shard_map.92
  199.6 14.2 %all_to_all.91 = bf16[8,2,32,384]{3,2,1,0:T(8,128)(2,1)S(1)} all-to-all(bf16[8,2,32,384]{3,2,1,0:T(8,128)(2,1)S(1)} %bitcast.78), channel_id=1, replica_groups={{0,2,4,6,8,10,12,14},{16,18,20,22,24,26,28,30},{32,34,36,38,40,42,44,46..., dimensions={0} | all-to-all | bytes 786432 | tf_op jit(solution)/shard_map/all_to_all | solution.py:158
  213.8 6.3 %collective-permute-start.9 = (bf16[2,32,384]{2,1,0:T(8,128)(2,1)S(1)}, bf16[2,32,384]{2,1,0:T(8,128)(2,1)S(1)}, u32[]{:S(2)}, u32[]{:S(2)}) collective-permute-start(bf16[2,32,384]{2,1,0:T(8,128)(2,1)S(1)} %convert_element_type.123), channel_id=1, source_target_pairs={{0,65},{65,0},{2,33},{33,2},{4,1},{1,4},{6,97},{97,6},{8,81},{81,8... | collective-permute-start | bytes 147464 | tf_op jit(solution)/shard_map/ppermute | solution.py:161
  220.2 1.8 collective-permute-done.9
  222.0 10.7 %all_to_all.92 = bf16[8,2,32,384]{3,2,1,0:T(8,128)(2,1)S(1)} all-to-all(bf16[8,2,32,384]{3,2,1,0:T(8,128)(2,1)S(1)} %broadcast_in_dim.119), channel_id=1, replica_groups={{0,2,4,6,8,10,12,14},{16,18,20,22,24,26,28,30},{32,34,36,38,40,42,44,46..., dimensions={0} | all-to-all | bytes 786432 | tf_op jit(solution)/shard_map/all_to_all | solution.py:158
  232.7 3.3 %shard_map.93 = bf16[16,32,384]{2,1,0:T(8,128)(2,1)S(1)} custom-call(s32[4,104]{1,0:T(4,128)S(1)} %get-tuple-element.14.table_ref, f32[8,128]{1,0:T(8,128)S(1)} %broadcast_in_dim.112.fold_ref, bf16[16,32,384]{2,1,0:T(8,128)(2,1)S(1)} %bitcast.66, bf16[96,192,192]{2,1,0:T(8,128)(2,1)S(1)} %shard_map.86.tiles_ref), custom_call_target="tpu_custom_call" | custom-call | flops 226492416 | bytes 7077888 | tf_op jit(solution)/shard_map/pallas_call | solution.py:106
  236.0 10.4 %all_to_all.93 = bf16[8,2,32,384]{3,2,1,0:T(8,128)(2,1)S(1)} all-to-all(bf16[8,2,32,384]{3,2,1,0:T(8,128)(2,1)S(1)} %bitcast.67), channel_id=1, replica_groups={{1,3,5,7,9,11,13,15},{17,19,21,23,25,27,29,31},{33,35,37,39,41,43,45,47..., dimensions={0} | all-to-all | bytes 786432 | tf_op jit(solution)/shard_map/all_to_all | solution.py:158
  246.5 7.2 %collective-permute-start.10 = (bf16[2,32,384]{2,1,0:T(8,128)(2,1)S(1)}, bf16[2,32,384]{2,1,0:T(8,128)(2,1)S(1)}, u32[]{:S(2)}, u32[]{:S(2)}) collective-permute-start(bf16[2,32,384]{2,1,0:T(8,128)(2,1)S(1)} %convert_element_type.127), channel_id=1, source_target_pairs={{1,64},{64,1},{3,32},{32,3},{5,0},{0,5},{7,96},{96,7},{9,80},{80,9... | collective-permute-start | bytes 147464 | tf_op jit(solution)/shard_map/ppermute | solution.py:161
  253.7 2.4 collective-permute-done.10
  256.1 8.5 %all_to_all.94 = bf16[8,2,32,384]{3,2,1,0:T(8,128)(2,1)S(1)} all-to-all(bf16[8,2,32,384]{3,2,1,0:T(8,128)(2,1)S(1)} %broadcast_in_dim.120), channel_id=1, replica_groups={{1,3,5,7,9,11,13,15},{17,19,21,23,25,27,29,31},{33,35,37,39,41,43,45,47..., dimensions={0} | all-to-all | bytes 786432 | tf_op jit(solution)/shard_map/all_to_all | solution.py:158
  264.7 2.4 shard_map.94
  267.1 14.8 %all_to_all.95 = bf16[8,2,32,384]{3,2,1,0:T(8,128)(2,1)S(1)} all-to-all(bf16[8,2,32,384]{3,2,1,0:T(8,128)(2,1)S(1)} %bitcast.65), channel_id=1, replica_groups={{0,2,4,6,8,10,12,14},{16,18,20,22,24,26,28,30},{32,34,36,38,40,42,44,46..., dimensions={0} | all-to-all | bytes 786432 | tf_op jit(solution)/shard_map/all_to_all | solution.py:158
  281.9 0.1 convert_reduce_fusion
  282.0 5.5 %collective-permute-start.11 = (bf16[2,32,384]{2,1,0:T(8,128)(2,1)S(1)}, bf16[2,32,384]{2,1,0:T(8,128)(2,1)S(1)}, u32[]{:S(2)}, u32[]{:S(2)}) collective-permute-start(bf16[2,32,384]{2,1,0:T(8,128)(2,1)S(1)} %convert_element_type.131), channel_id=1, source_target_pairs={{0,65},{65,0},{2,33},{33,2},{4,1},{1,4},{6,97},{97,6},{8,81},{81,8... | collective-permute-start | bytes 147464 | tf_op jit(solution)/shard_map/ppermute | solution.py:161
  287.5 1.8 collective-permute-done.11
  289.3 4.3 %collective-permute-start.12 = (f32[32,384]{1,0:T(8,128)S(1)}, f32[32,384]{1,0:T(8,128)S(1)}, u32[]{:S(2)}, u32[]{:S(2)}) collective-permute-start(f32[32,384]{1,0:T(8,128)S(1)} %fusion.1), channel_id=1, source_target_pairs={{0,1},{1,0},{2,3},{3,2},{4,5},{5,4},{6,7},{7,6},{8,9},{9,8},{10,11... | collective-permute-start | bytes 147464 | tf_op jit(solution)/shard_map/ppermute | solution.py:161
  293.6 0.9 collective-permute-done.12
  294.4 0.6 fusion
  (40 shorter events, 1.0 us)
Async XLA Ops:
  0.6 2.2 collective-permute-start
  2.7 1.2 collective-permute-start.2
  3.9 25.3 %collective-permute-start.3 = (bf16[48,192,192]{2,1,0:T(8,128)(2,1)}, bf16[48,192,192]{2,1,0:T(8,128)(2,1)}, u32[]{:S(2)}, u32[]{:S(2)}) collective-permute-start(bf16[48,192,192]{2,1,0:T(8,128)(2,1)} %bitcast.61), channel_id=1, source_target_pairs={{0,1},{1,0},{2,3},{3,2},{4,5},{5,4},{6,7},{7,6},{8,9},{9,8},{10,11... | collective-permute-start | bytes 10616840 | tf_op jit(solution)/shard_map/ppermute | solution.py:161
  4.9 11.7 %collective-permute-start.1 = (f32[2,32,384]{2,1,0:T(8,128)S(1)}, f32[2,32,384]{2,1,0:T(8,128)S(1)}, u32[]{:S(2)}, u32[]{:S(2)}) collective-permute-start(f32[2,32,384]{2,1,0:T(8,128)S(1)} %maximum_select_fusion), channel_id=1, source_target_pairs={{1,65},{3,33},{5,1},{7,97},{9,81},{11,49},{13,17},{15,113},{17,115... | collective-permute-start | bytes 294920 | tf_op jit(solution)/shard_map/ppermute | solution.py:161
  29.3 2.3 copy-start
  48.2 7.9 %collective-permute-start.4 = (bf16[2,32,384]{2,1,0:T(8,128)(2,1)S(1)}, bf16[2,32,384]{2,1,0:T(8,128)(2,1)S(1)}, u32[]{:S(2)}, u32[]{:S(2)}) collective-permute-start(bf16[2,32,384]{2,1,0:T(8,128)(2,1)S(1)} %convert_element_type.103), channel_id=1, source_target_pairs={{1,64},{64,1},{3,32},{32,3},{5,0},{0,5},{7,96},{96,7},{9,80},{80,9... | collective-permute-start | bytes 147464 | tf_op jit(solution)/shard_map/ppermute | solution.py:161
  80.3 7.2 %collective-permute-start.5 = (bf16[2,32,384]{2,1,0:T(8,128)(2,1)S(1)}, bf16[2,32,384]{2,1,0:T(8,128)(2,1)S(1)}, u32[]{:S(2)}, u32[]{:S(2)}) collective-permute-start(bf16[2,32,384]{2,1,0:T(8,128)(2,1)S(1)} %convert_element_type.107), channel_id=1, source_target_pairs={{0,65},{65,0},{2,33},{33,2},{4,1},{1,4},{6,97},{97,6},{8,81},{81,8... | collective-permute-start | bytes 147464 | tf_op jit(solution)/shard_map/ppermute | solution.py:161
  111.5 9.5 %collective-permute-start.6 = (bf16[2,32,384]{2,1,0:T(8,128)(2,1)S(1)}, bf16[2,32,384]{2,1,0:T(8,128)(2,1)S(1)}, u32[]{:S(2)}, u32[]{:S(2)}) collective-permute-start(bf16[2,32,384]{2,1,0:T(8,128)(2,1)S(1)} %convert_element_type.111), channel_id=1, source_target_pairs={{1,64},{64,1},{3,32},{32,3},{5,0},{0,5},{7,96},{96,7},{9,80},{80,9... | collective-permute-start | bytes 147464 | tf_op jit(solution)/shard_map/ppermute | solution.py:161
  148.7 7.4 %collective-permute-start.7 = (bf16[2,32,384]{2,1,0:T(8,128)(2,1)S(1)}, bf16[2,32,384]{2,1,0:T(8,128)(2,1)S(1)}, u32[]{:S(2)}, u32[]{:S(2)}) collective-permute-start(bf16[2,32,384]{2,1,0:T(8,128)(2,1)S(1)} %convert_element_type.115), channel_id=1, source_target_pairs={{0,65},{65,0},{2,33},{33,2},{4,1},{1,4},{6,97},{97,6},{8,81},{81,8... | collective-permute-start | bytes 147464 | tf_op jit(solution)/shard_map/ppermute | solution.py:161
  179.6 8.9 %collective-permute-start.8 = (bf16[2,32,384]{2,1,0:T(8,128)(2,1)S(1)}, bf16[2,32,384]{2,1,0:T(8,128)(2,1)S(1)}, u32[]{:S(2)}, u32[]{:S(2)}) collective-permute-start(bf16[2,32,384]{2,1,0:T(8,128)(2,1)S(1)} %convert_element_type.119), channel_id=1, source_target_pairs={{1,64},{64,1},{3,32},{32,3},{5,0},{0,5},{7,96},{96,7},{9,80},{80,9... | collective-permute-start | bytes 147464 | tf_op jit(solution)/shard_map/ppermute | solution.py:161
  213.8 8.1 %collective-permute-start.9 = (bf16[2,32,384]{2,1,0:T(8,128)(2,1)S(1)}, bf16[2,32,384]{2,1,0:T(8,128)(2,1)S(1)}, u32[]{:S(2)}, u32[]{:S(2)}) collective-permute-start(bf16[2,32,384]{2,1,0:T(8,128)(2,1)S(1)} %convert_element_type.123), channel_id=1, source_target_pairs={{0,65},{65,0},{2,33},{33,2},{4,1},{1,4},{6,97},{97,6},{8,81},{81,8... | collective-permute-start | bytes 147464 | tf_op jit(solution)/shard_map/ppermute | solution.py:161
  246.5 9.6 %collective-permute-start.10 = (bf16[2,32,384]{2,1,0:T(8,128)(2,1)S(1)}, bf16[2,32,384]{2,1,0:T(8,128)(2,1)S(1)}, u32[]{:S(2)}, u32[]{:S(2)}) collective-permute-start(bf16[2,32,384]{2,1,0:T(8,128)(2,1)S(1)} %convert_element_type.127), channel_id=1, source_target_pairs={{1,64},{64,1},{3,32},{32,3},{5,0},{0,5},{7,96},{96,7},{9,80},{80,9... | collective-permute-start | bytes 147464 | tf_op jit(solution)/shard_map/ppermute | solution.py:161
  282.0 7.3 %collective-permute-start.11 = (bf16[2,32,384]{2,1,0:T(8,128)(2,1)S(1)}, bf16[2,32,384]{2,1,0:T(8,128)(2,1)S(1)}, u32[]{:S(2)}, u32[]{:S(2)}) collective-permute-start(bf16[2,32,384]{2,1,0:T(8,128)(2,1)S(1)} %convert_element_type.131), channel_id=1, source_target_pairs={{0,65},{65,0},{2,33},{33,2},{4,1},{1,4},{6,97},{97,6},{8,81},{81,8... | collective-permute-start | bytes 147464 | tf_op jit(solution)/shard_map/ppermute | solution.py:161
  289.3 5.1 %collective-permute-start.12 = (f32[32,384]{1,0:T(8,128)S(1)}, f32[32,384]{1,0:T(8,128)S(1)}, u32[]{:S(2)}, u32[]{:S(2)}) collective-permute-start(f32[32,384]{1,0:T(8,128)S(1)} %fusion.1), channel_id=1, source_target_pairs={{0,1},{1,0},{2,3},{3,2},{4,5},{5,4},{6,7},{7,6},{8,9},{9,8},{10,11... | collective-permute-start | bytes 147464 | tf_op jit(solution)/shard_map/ppermute | solution.py:161

commit v6 on v5

--- a/solution.py
+++ b/solution.py
@@ -7,7 +7,7 @@
 
 DEG = 8
 GROUP = 32
-REST = 8
+REST = 16
 
 
 def keep_kernel(own_ref, other_ref, kept_ref, sems):

time: 296 us -> 297 us (level)
  starting transfers between devices: 53.6 us -> 58.8 us
  blocking collectives: 178 us -> 173 us
    ppermute x13, starting transfers between devices: 53.6 us -> 58.8 us  [send(): return lax.ppermute(value, axes, pairs)]
    all_to_all x16, blocking collectives: 178 us -> 173 us  [exchange(): lax.all_to_all(value, axes, 0, 0, axis_index_groups=groups, tiled=False)]
where the time goes in v6:
time: 297 us; the launch traced here: 296 us
  blocking collectives  173 us (58%)
  starting transfers between devices  58.8 us (20%)
  Pallas kernels  27.1 us (9%)
  waiting for transfers between devices  22.4 us (8%)
  other arithmetic  6.74 us (2%)
  between operations  4.92 us (2%)
    all_to_all x16, blocking collectives, exchange(): lax.all_to_all(value, axes, 0, 0, axis_index_groups=groups, tiled=False)  173 us
    ppermute x13, starting transfers between devices, send(): return lax.ppermute(value, axes, pairs)  58.8 us
    pallas_call x8, Pallas kernels, products(): pl.pallas_call(products_kernel, out_shape=jax.ShapeDtypeStruct(x.shape, j...  24.4 us
    ppermute x13, waiting for transfers between devices, send(): return lax.ppermute(value, axes, pairs)  22.4 us
  transfers between devices with their start and end apart: 13, of which 10 were waited for; matrix products, arithmetic and copies ran while one was open for 2% of the time, Pallas kernels for 0%

profile of v6, /device:TPU:7, one launch (start us, length us, event | category | flops | bytes accessed | tf_op | source)
XLA Modules:
  0.0 296.0 jit_solution(4814217594414874148)
XLA Ops:
  0.6 0.8 collective-permute-start
  1.4 0.7 broadcast_add_fusion
  2.0 0.7 pad_add_fusion.2
  2.7 0.1 collective-permute-start.2
  2.8 0.9 maximum_select_fusion
  3.7 0.2 collective-permute-done.2
  3.9 0.3 collective-permute-start.3
  4.9 5.9 %collective-permute-start.1 = (f32[2,32,384]{2,1,0:T(8,128)S(1)}, f32[2,32,384]{2,1,0:T(8,128)S(1)}, u32[]{:S(2)}, u32[]{:S(2)}) collective-permute-start(f32[2,32,384]{2,1,0:T(8,128)S(1)} %maximum_select_fusion), channel_id=1, source_target_pairs={{1,65},{3,33},{5,1},{7,97},{9,81},{11,49},{13,17},{15,113},{17,115... | collective-permute-start | bytes 294920 | tf_op jit(solution)/shard_map/ppermute | solution.py:161
  10.9 0.7 pad_add_fusion.3
  11.6 0.6 fusion.10
  14.9 0.1 add_add_fusion.1
  15.0 0.1 add_add_fusion
  15.0 0.1 select_reduce_fusion.3
  15.2 0.1 select_reduce_fusion.1
  15.3 0.7 bitcast_select_fusion.2
  16.0 0.7 broadcast_select_fusion.1
  16.7 12.5 %all_to_all.80 = bf16[8,2,32,384]{3,2,1,0:T(8,128)(2,1)S(1)} all-to-all(bf16[8,2,32,384]{3,2,1,0:T(8,128)(2,1)S(1)} %broadcast_in_dim.113), channel_id=1, replica_groups={{0,2,4,6,8,10,12,14},{16,18,20,22,24,26,28,30},{32,34,36,38,40,42,44,46..., dimensions={0} | all-to-all | bytes 786432 | tf_op jit(solution)/shard_map/all_to_all | solution.py:158
  29.3 2.3 copy-done
  31.6 2.7 shard_map.86.tiles_ref
  34.3 3.5 %shard_map.87 = bf16[16,32,384]{2,1,0:T(8,128)(2,1)S(1)} custom-call(s32[4,112]{1,0:T(4,128)S(1)} %get-tuple-element.14.table_ref, f32[8,128]{1,0:T(8,128)S(1)} %broadcast_in_dim.112.fold_ref, bf16[16,32,384]{2,1,0:T(8,128)(2,1)S(1)} %bitcast.63, bf16[96,192,192]{2,1,0:T(8,128)(2,1)S(1)} %shard_map.86.tiles_ref), custom_call_target="tpu_custom_call" | custom-call | flops 226492416 | bytes 7077888 | tf_op jit(solution)/shard_map/pallas_call | solution.py:106
  37.8 10.1 %all_to_all.81 = bf16[8,2,32,384]{3,2,1,0:T(8,128)(2,1)S(1)} all-to-all(bf16[8,2,32,384]{3,2,1,0:T(8,128)(2,1)S(1)} %bitcast.68), channel_id=1, replica_groups={{1,3,5,7,9,11,13,15},{17,19,21,23,25,27,29,31},{33,35,37,39,41,43,45,47..., dimensions={0} | all-to-all | bytes 786432 | tf_op jit(solution)/shard_map/all_to_all | solution.py:158
  48.0 0.1 convert_reduce_fusion.7
  48.0 0.1 collective-permute-start.4
  48.8 7.2 %collective-permute-done.4 = bf16[2,32,384]{2,1,0:T(8,128)(2,1)S(1)} collective-permute-done((bf16[2,32,384]{2,1,0:T(8,128)(2,1)S(1)}, bf16[2,32,384]{2,1,0:T(8,128)(2,1)S(1)}, u32[]{:S(2)}, u32[]{:S(2)}) %collective-permute-start.4) | collective-permute-done | bytes 49184 | tf_op jit(solution)/shard_map/ppermute | solution.py:161
  56.0 8.4 %all_to_all.82 = bf16[8,2,32,384]{3,2,1,0:T(8,128)(2,1)S(1)} all-to-all(bf16[8,2,32,384]{3,2,1,0:T(8,128)(2,1)S(1)} %broadcast_in_dim.114), channel_id=1, replica_groups={{1,3,5,7,9,11,13,15},{17,19,21,23,25,27,29,31},{33,35,37,39,41,43,45,47..., dimensions={0} | all-to-all | bytes 786432 | tf_op jit(solution)/shard_map/all_to_all | solution.py:158
  64.4 2.5 shard_map.88
  66.9 12.6 %all_to_all.83 = bf16[8,2,32,384]{3,2,1,0:T(8,128)(2,1)S(1)} all-to-all(bf16[8,2,32,384]{3,2,1,0:T(8,128)(2,1)S(1)} %bitcast.70), channel_id=1, replica_groups={{0,2,4,6,8,10,12,14},{16,18,20,22,24,26,28,30},{32,34,36,38,40,42,44,46..., dimensions={0} | all-to-all | bytes 786432 | tf_op jit(solution)/shard_map/all_to_all | solution.py:158
  79.5 0.1 convert_reduce_fusion.6
  79.6 6.4 %collective-permute-start.5 = (bf16[2,32,384]{2,1,0:T(8,128)(2,1)S(1)}, bf16[2,32,384]{2,1,0:T(8,128)(2,1)S(1)}, u32[]{:S(2)}, u32[]{:S(2)}) collective-permute-start(bf16[2,32,384]{2,1,0:T(8,128)(2,1)S(1)} %convert_element_type.107), channel_id=1, source_target_pairs={{0,65},{65,0},{2,33},{33,2},{4,1},{1,4},{6,97},{97,6},{8,81},{81,8... | collective-permute-start | bytes 147464 | tf_op jit(solution)/shard_map/ppermute | solution.py:161
  86.0 1.8 collective-permute-done.5
  87.8 10.9 %all_to_all.84 = bf16[8,2,32,384]{3,2,1,0:T(8,128)(2,1)S(1)} all-to-all(bf16[8,2,32,384]{3,2,1,0:T(8,128)(2,1)S(1)} %broadcast_in_dim.115), channel_id=1, replica_groups={{0,2,4,6,8,10,12,14},{16,18,20,22,24,26,28,30},{32,34,36,38,40,42,44,46..., dimensions={0} | all-to-all | bytes 786432 | tf_op jit(solution)/shard_map/all_to_all | solution.py:158
  98.7 3.5 %shard_map.89 = bf16[16,32,384]{2,1,0:T(8,128)(2,1)S(1)} custom-call(s32[4,112]{1,0:T(4,128)S(1)} %get-tuple-element.14.table_ref, f32[8,128]{1,0:T(8,128)S(1)} %broadcast_in_dim.112.fold_ref, bf16[16,32,384]{2,1,0:T(8,128)(2,1)S(1)} %bitcast.71, bf16[96,192,192]{2,1,0:T(8,128)(2,1)S(1)} %shard_map.86.tiles_ref), custom_call_target="tpu_custom_call" | custom-call | flops 226492416 | bytes 7077888 | tf_op jit(solution)/shard_map/pallas_call | solution.py:106
  102.2 9.2 %all_to_all.85 = bf16[8,2,32,384]{3,2,1,0:T(8,128)(2,1)S(1)} all-to-all(bf16[8,2,32,384]{3,2,1,0:T(8,128)(2,1)S(1)} %bitcast.72), channel_id=1, replica_groups={{1,3,5,7,9,11,13,15},{17,19,21,23,25,27,29,31},{33,35,37,39,41,43,45,47..., dimensions={0} | all-to-all | bytes 786432 | tf_op jit(solution)/shard_map/all_to_all | solution.py:158
  111.5 7.6 %collective-permute-start.6 = (bf16[2,32,384]{2,1,0:T(8,128)(2,1)S(1)}, bf16[2,32,384]{2,1,0:T(8,128)(2,1)S(1)}, u32[]{:S(2)}, u32[]{:S(2)}) collective-permute-start(bf16[2,32,384]{2,1,0:T(8,128)(2,1)S(1)} %convert_element_type.111), channel_id=1, source_target_pairs={{1,64},{64,1},{3,32},{32,3},{5,0},{0,5},{7,96},{96,7},{9,80},{80,9... | collective-permute-start | bytes 147464 | tf_op jit(solution)/shard_map/ppermute | solution.py:161
  119.1 2.2 collective-permute-done.6
  121.4 8.7 %all_to_all.86 = bf16[8,2,32,384]{3,2,1,0:T(8,128)(2,1)S(1)} all-to-all(bf16[8,2,32,384]{3,2,1,0:T(8,128)(2,1)S(1)} %broadcast_in_dim.116), channel_id=1, replica_groups={{1,3,5,7,9,11,13,15},{17,19,21,23,25,27,29,31},{33,35,37,39,41,43,45,47..., dimensions={0} | all-to-all | bytes 786432 | tf_op jit(solution)/shard_map/all_to_all | solution.py:158
  130.0 2.7 shard_map.90
  132.7 15.4 %all_to_all.87 = bf16[8,2,32,384]{3,2,1,0:T(8,128)(2,1)S(1)} all-to-all(bf16[8,2,32,384]{3,2,1,0:T(8,128)(2,1)S(1)} %bitcast.74), channel_id=1, replica_groups={{0,2,4,6,8,10,12,14},{16,18,20,22,24,26,28,30},{32,34,36,38,40,42,44,46..., dimensions={0} | all-to-all | bytes 786432 | tf_op jit(solution)/shard_map/all_to_all | solution.py:158
  148.2 5.2 %collective-permute-start.7 = (bf16[2,32,384]{2,1,0:T(8,128)(2,1)S(1)}, bf16[2,32,384]{2,1,0:T(8,128)(2,1)S(1)}, u32[]{:S(2)}, u32[]{:S(2)}) collective-permute-start(bf16[2,32,384]{2,1,0:T(8,128)(2,1)S(1)} %convert_element_type.115), channel_id=1, source_target_pairs={{0,65},{65,0},{2,33},{33,2},{4,1},{1,4},{6,97},{97,6},{8,81},{81,8... | collective-permute-start | bytes 147464 | tf_op jit(solution)/shard_map/ppermute | solution.py:161
  153.4 2.0 collective-permute-done.7
  155.5 10.7 %all_to_all.88 = bf16[8,2,32,384]{3,2,1,0:T(8,128)(2,1)S(1)} all-to-all(bf16[8,2,32,384]{3,2,1,0:T(8,128)(2,1)S(1)} %broadcast_in_dim.117), channel_id=1, replica_groups={{0,2,4,6,8,10,12,14},{16,18,20,22,24,26,28,30},{32,34,36,38,40,42,44,46..., dimensions={0} | all-to-all | bytes 786432 | tf_op jit(solution)/shard_map/all_to_all | solution.py:158
  166.2 3.5 %shard_map.91 = bf16[16,32,384]{2,1,0:T(8,128)(2,1)S(1)} custom-call(s32[4,112]{1,0:T(4,128)S(1)} %get-tuple-element.14.table_ref, f32[8,128]{1,0:T(8,128)S(1)} %broadcast_in_dim.112.fold_ref, bf16[16,32,384]{2,1,0:T(8,128)(2,1)S(1)} %bitcast.75, bf16[96,192,192]{2,1,0:T(8,128)(2,1)S(1)} %shard_map.86.tiles_ref), custom_call_target="tpu_custom_call" | custom-call | flops 226492416 | bytes 7077888 | tf_op jit(solution)/shard_map/pallas_call | solution.py:106
  169.7 9.6 %all_to_all.89 = bf16[8,2,32,384]{3,2,1,0:T(8,128)(2,1)S(1)} all-to-all(bf16[8,2,32,384]{3,2,1,0:T(8,128)(2,1)S(1)} %bitcast.76), channel_id=1, replica_groups={{1,3,5,7,9,11,13,15},{17,19,21,23,25,27,29,31},{33,35,37,39,41,43,45,47..., dimensions={0} | all-to-all | bytes 786432 | tf_op jit(solution)/shard_map/all_to_all | solution.py:158
  179.4 7.2 %collective-permute-start.8 = (bf16[2,32,384]{2,1,0:T(8,128)(2,1)S(1)}, bf16[2,32,384]{2,1,0:T(8,128)(2,1)S(1)}, u32[]{:S(2)}, u32[]{:S(2)}) collective-permute-start(bf16[2,32,384]{2,1,0:T(8,128)(2,1)S(1)} %convert_element_type.119), channel_id=1, source_target_pairs={{1,64},{64,1},{3,32},{32,3},{5,0},{0,5},{7,96},{96,7},{9,80},{80,9... | collective-permute-start | bytes 147464 | tf_op jit(solution)/shard_map/ppermute | solution.py:161
  186.6 2.2 collective-permute-done.8
  188.9 8.6 %all_to_all.90 = bf16[8,2,32,384]{3,2,1,0:T(8,128)(2,1)S(1)} all-to-all(bf16[8,2,32,384]{3,2,1,0:T(8,128)(2,1)S(1)} %broadcast_in_dim.118), channel_id=1, replica_groups={{1,3,5,7,9,11,13,15},{17,19,21,23,25,27,29,31},{33,35,37,39,41,43,45,47..., dimensions={0} | all-to-all | bytes 786432 | tf_op jit(solution)/shard_map/all_to_all | solution.py:158
  197.5 2.5 shard_map.92
  200.1 13.3 %all_to_all.91 = bf16[8,2,32,384]{3,2,1,0:T(8,128)(2,1)S(1)} all-to-all(bf16[8,2,32,384]{3,2,1,0:T(8,128)(2,1)S(1)} %bitcast.78), channel_id=1, replica_groups={{0,2,4,6,8,10,12,14},{16,18,20,22,24,26,28,30},{32,34,36,38,40,42,44,46..., dimensions={0} | all-to-all | bytes 786432 | tf_op jit(solution)/shard_map/all_to_all | solution.py:158
  213.4 7.6 %collective-permute-start.9 = (bf16[2,32,384]{2,1,0:T(8,128)(2,1)S(1)}, bf16[2,32,384]{2,1,0:T(8,128)(2,1)S(1)}, u32[]{:S(2)}, u32[]{:S(2)}) collective-permute-start(bf16[2,32,384]{2,1,0:T(8,128)(2,1)S(1)} %convert_element_type.123), channel_id=1, source_target_pairs={{0,65},{65,0},{2,33},{33,2},{4,1},{1,4},{6,97},{97,6},{8,81},{81,8... | collective-permute-start | bytes 147464 | tf_op jit(solution)/shard_map/ppermute | solution.py:161
  221.0 1.8 collective-permute-done.9
  222.9 10.7 %all_to_all.92 = bf16[8,2,32,384]{3,2,1,0:T(8,128)(2,1)S(1)} all-to-all(bf16[8,2,32,384]{3,2,1,0:T(8,128)(2,1)S(1)} %broadcast_in_dim.119), channel_id=1, replica_groups={{0,2,4,6,8,10,12,14},{16,18,20,22,24,26,28,30},{32,34,36,38,40,42,44,46..., dimensions={0} | all-to-all | bytes 786432 | tf_op jit(solution)/shard_map/all_to_all | solution.py:158
  233.5 3.5 %shard_map.93 = bf16[16,32,384]{2,1,0:T(8,128)(2,1)S(1)} custom-call(s32[4,112]{1,0:T(4,128)S(1)} %get-tuple-element.14.table_ref, f32[8,128]{1,0:T(8,128)S(1)} %broadcast_in_dim.112.fold_ref, bf16[16,32,384]{2,1,0:T(8,128)(2,1)S(1)} %bitcast.66, bf16[96,192,192]{2,1,0:T(8,128)(2,1)S(1)} %shard_map.86.tiles_ref), custom_call_target="tpu_custom_call" | custom-call | flops 226492416 | bytes 7077888 | tf_op jit(solution)/shard_map/pallas_call | solution.py:106
  237.1 9.8 %all_to_all.93 = bf16[8,2,32,384]{3,2,1,0:T(8,128)(2,1)S(1)} all-to-all(bf16[8,2,32,384]{3,2,1,0:T(8,128)(2,1)S(1)} %bitcast.67), channel_id=1, replica_groups={{1,3,5,7,9,11,13,15},{17,19,21,23,25,27,29,31},{33,35,37,39,41,43,45,47..., dimensions={0} | all-to-all | bytes 786432 | tf_op jit(solution)/shard_map/all_to_all | solution.py:158
  247.0 7.6 %collective-permute-start.10 = (bf16[2,32,384]{2,1,0:T(8,128)(2,1)S(1)}, bf16[2,32,384]{2,1,0:T(8,128)(2,1)S(1)}, u32[]{:S(2)}, u32[]{:S(2)}) collective-permute-start(bf16[2,32,384]{2,1,0:T(8,128)(2,1)S(1)} %convert_element_type.127), channel_id=1, source_target_pairs={{1,64},{64,1},{3,32},{32,3},{5,0},{0,5},{7,96},{96,7},{9,80},{80,9... | collective-permute-start | bytes 147464 | tf_op jit(solution)/shard_map/ppermute | solution.py:161
  254.6 2.4 collective-permute-done.10
  257.0 8.5 %all_to_all.94 = bf16[8,2,32,384]{3,2,1,0:T(8,128)(2,1)S(1)} all-to-all(bf16[8,2,32,384]{3,2,1,0:T(8,128)(2,1)S(1)} %broadcast_in_dim.120), channel_id=1, replica_groups={{1,3,5,7,9,11,13,15},{17,19,21,23,25,27,29,31},{33,35,37,39,41,43,45,47..., dimensions={0} | all-to-all | bytes 786432 | tf_op jit(solution)/shard_map/all_to_all | solution.py:158
  265.6 2.5 shard_map.94
  268.1 14.4 %all_to_all.95 = bf16[8,2,32,384]{3,2,1,0:T(8,128)(2,1)S(1)} all-to-all(bf16[8,2,32,384]{3,2,1,0:T(8,128)(2,1)S(1)} %bitcast.65), channel_id=1, replica_groups={{0,2,4,6,8,10,12,14},{16,18,20,22,24,26,28,30},{32,34,36,38,40,42,44,46..., dimensions={0} | all-to-all | bytes 786432 | tf_op jit(solution)/shard_map/all_to_all | solution.py:158
  282.5 0.1 convert_reduce_fusion
  282.6 5.8 %collective-permute-start.11 = (bf16[2,32,384]{2,1,0:T(8,128)(2,1)S(1)}, bf16[2,32,384]{2,1,0:T(8,128)(2,1)S(1)}, u32[]{:S(2)}, u32[]{:S(2)}) collective-permute-start(bf16[2,32,384]{2,1,0:T(8,128)(2,1)S(1)} %convert_element_type.131), channel_id=1, source_target_pairs={{0,65},{65,0},{2,33},{33,2},{4,1},{1,4},{6,97},{97,6},{8,81},{81,8... | collective-permute-start | bytes 147464 | tf_op jit(solution)/shard_map/ppermute | solution.py:161
  288.4 1.8 collective-permute-done.11
  290.2 4.2 %collective-permute-start.12 = (f32[32,384]{1,0:T(8,128)S(1)}, f32[32,384]{1,0:T(8,128)S(1)}, u32[]{:S(2)}, u32[]{:S(2)}) collective-permute-start(f32[32,384]{1,0:T(8,128)S(1)} %fusion.1), channel_id=1, source_target_pairs={{0,1},{1,0},{2,3},{3,2},{4,5},{5,4},{6,7},{7,6},{8,9},{9,8},{10,11... | collective-permute-start | bytes 147464 | tf_op jit(solution)/shard_map/ppermute | solution.py:161
  294.4 0.9 collective-permute-done.12
  295.3 0.6 fusion
  (40 shorter events, 1.0 us)
Async XLA Ops:
  0.6 2.2 collective-permute-start
  2.7 1.2 collective-permute-start.2
  3.9 25.3 %collective-permute-start.3 = (bf16[48,192,192]{2,1,0:T(8,128)(2,1)}, bf16[48,192,192]{2,1,0:T(8,128)(2,1)}, u32[]{:S(2)}, u32[]{:S(2)}) collective-permute-start(bf16[48,192,192]{2,1,0:T(8,128)(2,1)} %bitcast.61), channel_id=1, source_target_pairs={{0,1},{1,0},{2,3},{3,2},{4,5},{5,4},{6,7},{7,6},{8,9},{9,8},{10,11... | collective-permute-start | bytes 10616840 | tf_op jit(solution)/shard_map/ppermute | solution.py:161
  4.9 11.7 %collective-permute-start.1 = (f32[2,32,384]{2,1,0:T(8,128)S(1)}, f32[2,32,384]{2,1,0:T(8,128)S(1)}, u32[]{:S(2)}, u32[]{:S(2)}) collective-permute-start(f32[2,32,384]{2,1,0:T(8,128)S(1)} %maximum_select_fusion), channel_id=1, source_target_pairs={{1,65},{3,33},{5,1},{7,97},{9,81},{11,49},{13,17},{15,113},{17,115... | collective-permute-start | bytes 294920 | tf_op jit(solution)/shard_map/ppermute | solution.py:161
  29.3 2.3 copy-start
  48.0 7.9 %collective-permute-start.4 = (bf16[2,32,384]{2,1,0:T(8,128)(2,1)S(1)}, bf16[2,32,384]{2,1,0:T(8,128)(2,1)S(1)}, u32[]{:S(2)}, u32[]{:S(2)}) collective-permute-start(bf16[2,32,384]{2,1,0:T(8,128)(2,1)S(1)} %convert_element_type.103), channel_id=1, source_target_pairs={{1,64},{64,1},{3,32},{32,3},{5,0},{0,5},{7,96},{96,7},{9,80},{80,9... | collective-permute-start | bytes 147464 | tf_op jit(solution)/shard_map/ppermute | solution.py:161
  79.6 8.2 %collective-permute-start.5 = (bf16[2,32,384]{2,1,0:T(8,128)(2,1)S(1)}, bf16[2,32,384]{2,1,0:T(8,128)(2,1)S(1)}, u32[]{:S(2)}, u32[]{:S(2)}) collective-permute-start(bf16[2,32,384]{2,1,0:T(8,128)(2,1)S(1)} %convert_element_type.107), channel_id=1, source_target_pairs={{0,65},{65,0},{2,33},{33,2},{4,1},{1,4},{6,97},{97,6},{8,81},{81,8... | collective-permute-start | bytes 147464 | tf_op jit(solution)/shard_map/ppermute | solution.py:161
  111.5 9.8 %collective-permute-start.6 = (bf16[2,32,384]{2,1,0:T(8,128)(2,1)S(1)}, bf16[2,32,384]{2,1,0:T(8,128)(2,1)S(1)}, u32[]{:S(2)}, u32[]{:S(2)}) collective-permute-start(bf16[2,32,384]{2,1,0:T(8,128)(2,1)S(1)} %convert_element_type.111), channel_id=1, source_target_pairs={{1,64},{64,1},{3,32},{32,3},{5,0},{0,5},{7,96},{96,7},{9,80},{80,9... | collective-permute-start | bytes 147464 | tf_op jit(solution)/shard_map/ppermute | solution.py:161
  148.2 7.2 %collective-permute-start.7 = (bf16[2,32,384]{2,1,0:T(8,128)(2,1)S(1)}, bf16[2,32,384]{2,1,0:T(8,128)(2,1)S(1)}, u32[]{:S(2)}, u32[]{:S(2)}) collective-permute-start(bf16[2,32,384]{2,1,0:T(8,128)(2,1)S(1)} %convert_element_type.115), channel_id=1, source_target_pairs={{0,65},{65,0},{2,33},{33,2},{4,1},{1,4},{6,97},{97,6},{8,81},{81,8... | collective-permute-start | bytes 147464 | tf_op jit(solution)/shard_map/ppermute | solution.py:161
  179.4 9.4 %collective-permute-start.8 = (bf16[2,32,384]{2,1,0:T(8,128)(2,1)S(1)}, bf16[2,32,384]{2,1,0:T(8,128)(2,1)S(1)}, u32[]{:S(2)}, u32[]{:S(2)}) collective-permute-start(bf16[2,32,384]{2,1,0:T(8,128)(2,1)S(1)} %convert_element_type.119), channel_id=1, source_target_pairs={{1,64},{64,1},{3,32},{32,3},{5,0},{0,5},{7,96},{96,7},{9,80},{80,9... | collective-permute-start | bytes 147464 | tf_op jit(solution)/shard_map/ppermute | solution.py:161
  213.4 9.4 %collective-permute-start.9 = (bf16[2,32,384]{2,1,0:T(8,128)(2,1)S(1)}, bf16[2,32,384]{2,1,0:T(8,128)(2,1)S(1)}, u32[]{:S(2)}, u32[]{:S(2)}) collective-permute-start(bf16[2,32,384]{2,1,0:T(8,128)(2,1)S(1)} %convert_element_type.123), channel_id=1, source_target_pairs={{0,65},{65,0},{2,33},{33,2},{4,1},{1,4},{6,97},{97,6},{8,81},{81,8... | collective-permute-start | bytes 147464 | tf_op jit(solution)/shard_map/ppermute | solution.py:161
  247.0 10.0 %collective-permute-start.10 = (bf16[2,32,384]{2,1,0:T(8,128)(2,1)S(1)}, bf16[2,32,384]{2,1,0:T(8,128)(2,1)S(1)}, u32[]{:S(2)}, u32[]{:S(2)}) collective-permute-start(bf16[2,32,384]{2,1,0:T(8,128)(2,1)S(1)} %convert_element_type.127), channel_id=1, source_target_pairs={{1,64},{64,1},{3,32},{32,3},{5,0},{0,5},{7,96},{96,7},{9,80},{80,9... | collective-permute-start | bytes 147464 | tf_op jit(solution)/shard_map/ppermute | solution.py:161
  282.6 7.6 %collective-permute-start.11 = (bf16[2,32,384]{2,1,0:T(8,128)(2,1)S(1)}, bf16[2,32,384]{2,1,0:T(8,128)(2,1)S(1)}, u32[]{:S(2)}, u32[]{:S(2)}) collective-permute-start(bf16[2,32,384]{2,1,0:T(8,128)(2,1)S(1)} %convert_element_type.131), channel_id=1, source_target_pairs={{0,65},{65,0},{2,33},{33,2},{4,1},{1,4},{6,97},{97,6},{8,81},{81,8... | collective-permute-start | bytes 147464 | tf_op jit(solution)/shard_map/ppermute | solution.py:161
  290.2 5.1 %collective-permute-start.12 = (f32[32,384]{1,0:T(8,128)S(1)}, f32[32,384]{1,0:T(8,128)S(1)}, u32[]{:S(2)}, u32[]{:S(2)}) collective-permute-start(f32[32,384]{1,0:T(8,128)S(1)} %fusion.1), channel_id=1, source_target_pairs={{0,1},{1,0},{2,3},{3,2},{4,5},{5,4},{6,7},{7,6},{8,9},{9,8},{10,11... | collective-permute-start | bytes 147464 | tf_op jit(solution)/shard_map/ppermute | solution.py:161
